TPU v7x, 32 devices: a whole 2x2x4 slice. The times are simulated.
32 devices in a mesh: seq: 8 (over z, x), head: 4 (over y, core).
Axes of the slice: x: 2, y: 2, z: 4, core: 2. Of those that a mesh axis runs over, the one named last changes fastest.
Arguments:
- layer_input: bfloat16 [4096, 2048], P('seq', 'head'), may hold values from -6 to 6
- clip_lengths: int32 [3], replicated, may hold values from 1 to 4094, as said below
- key_padding: int32 [4096], replicated, may hold values 0 or 1
- norm1_gain: float32 [2048], replicated, may hold values from 0.1 to 1.9
- w_query: bfloat16 [2048, 2048], P(None, 'head'), may hold values from -0.125 to 0.125
- w_key: bfloat16 [2048, 2048], P(None, 'head'), may hold values from -0.125 to 0.125
- w_value: bfloat16 [2048, 2048], P(None, 'head'), may hold values from -0.125 to 0.125
- w_out: bfloat16 [2048, 2048], P(None, 'head'), may hold values from -1 to 1
- norm2_gain: float32 [2048], replicated, may hold values from 0.1 to 1.9
- w_up: bfloat16 [2048, 8192], P('seq', 'head'), may hold values from -0.125 to 0.125
- w_down: bfloat16 [2048, 8192], P('seq', 'head'), may hold values from -0.0625 to 0.0625
- out_grad: bfloat16 [4096, 2048], P('seq', 'head'), may hold values from -6 to 6
Outputs:
- layer_output: bfloat16 [4096, 2048], P('seq', 'head')
- input_grad: float32 [4096, 2048], P('seq', 'head')
- norm1_gain_grad: float32 [2048], replicated
- query_grad: float32 [2048, 2048], P(None, 'head')
- key_grad: float32 [2048, 2048], P(None, 'head')
- value_grad: float32 [2048, 2048], P(None, 'head')
- out_weight_grad: float32 [2048, 2048], P(None, 'head')
- norm2_gain_grad: float32 [2048], replicated
- up_grad: float32 [2048, 8192], P('seq', 'head')
- down_grad: float32 [2048, 8192], P('seq', 'head')
Inputs may be any that keep to these rules, and one draw needn't show every extreme that they name: `clip_lengths`: the 3 lengths sum to 4096; the longest clip begins within the first 512 positions and ends within the last 512.
All inputs are finite; a program needn't handle non-finite values.
Results may differ from a plain program's by a relative error of at most 0.025.
Values may be sent and summed in bfloat16 or wider, within the bound.
A program may use at most 384 MiB of HBM per device.

v0:
```python
import jax
import jax.numpy as jnp
from jax import lax
from jax.sharding import PartitionSpec as P

HD = 128


norm_eps = 1e-05


def passed_along(block, axis, distance):
    devices = range(lax.axis_size(axis))
    route = [((i - distance) % len(devices), i) for i in devices]
    return lax.ppermute(block, axis, route)


def layer_norm(tok_rows, gain_vector):
    row_mean = jnp.mean(tok_rows, axis=1, keepdims=True)
    centred = tok_rows - row_mean
    inverse = lax.rsqrt(jnp.mean(centred * centred, axis=1, keepdims=True) + norm_eps)
    normed = centred * inverse
    return (normed, inverse, (normed * gain_vector).astype(jnp.bfloat16))


def norm_back(grad_normed, normed, inverse, gain_vector):
    scaled = grad_normed * gain_vector
    centre_term = jnp.mean(scaled, axis=1, keepdims=True)
    slope_term = jnp.mean(scaled * normed, axis=1, keepdims=True)
    return (
        inverse * (scaled - centre_term - normed * slope_term),
        jnp.sum(grad_normed * normed, axis=0),
    )


def full_rows(part_rows):
    return lax.all_gather(part_rows, "head", axis=1, tiled=True)


def head_total(partial_sum):
    return lax.psum(partial_sum.astype(jnp.bfloat16), "head").astype(jnp.float32)


def pass_keys(key_state):
    return passed_along(key_state, "seq", -1)


def pass_grads(grad_state):
    return passed_along(grad_state.astype(jnp.bfloat16), "seq", -1).astype(grad_state.dtype)


def body(
    layer_input,
    clip_lengths,
    key_padding,
    norm1_gain,
    w_query,
    w_key,
    w_value,
    w_out,
    norm2_gain,
    w_up,
    w_down,
    out_grad,
):
    tok_count = layer_input.shape[0]
    share_width = layer_input.shape[1]
    local_width = w_query.shape[1]
    head_local = local_width // HD
    up_width = w_up.shape[1]
    score_scale = HD ** (-0.5)
    seq_count = lax.axis_size("seq")
    seq_index = lax.axis_index("seq")
    clip_ends = jnp.cumsum(clip_lengths)

    def clip_of(positions):
        return jnp.sum((positions[:, None] >= clip_ends[None, :]).astype(jnp.int32), axis=1)

    query_pos = seq_index * tok_count + jnp.arange(tok_count, dtype=jnp.int32)
    query_clip = clip_of(query_pos)

    def visible(first_key, key_rows):
        key_pos = first_key + jnp.arange(key_rows, dtype=jnp.int32)
        key_keep = lax.dynamic_slice_in_dim(key_padding, first_key, key_rows) > 0
        same_clip = query_clip[:, None] == clip_of(key_pos)[None, :]
        causal = key_pos[None, :] <= query_pos[:, None]
        return same_clip & causal & (key_keep[None, :] | (key_pos[None, :] == query_pos[:, None]))

    whole_input = full_rows(layer_input).astype(jnp.float32)
    normed1, inverse1, attn_in = layer_norm(whole_input, norm1_gain)
    query_b = jnp.dot(attn_in, w_query, preferred_element_type=jnp.float32).astype(jnp.bfloat16)
    key_f = jnp.dot(attn_in, w_key, preferred_element_type=jnp.float32)
    value_f = jnp.dot(attn_in, w_value, preferred_element_type=jnp.float32)
    key_value = jnp.concatenate([key_f, value_f], axis=1).astype(jnp.bfloat16)
    query_heads = query_b.reshape(tok_count, head_local, HD)
    start_state = (
        jnp.full((head_local, tok_count), -1e30, jnp.float32),
        jnp.zeros((head_local, tok_count), jnp.float32),
        jnp.zeros((head_local, tok_count, HD), jnp.float32),
    )
    fold_init = (start_state,)
    kv_piece = lax.all_gather(key_value, "seq", axis=0, tiled=True)
    key_rows = kv_piece.shape[0]
    allowed = visible(jnp.int32(0), key_rows)
    row_high, weight_sum, weighted = fold_init[0]
    key_heads = kv_piece[:, :local_width].reshape(key_rows, head_local, HD)
    value_heads = kv_piece[:, local_width:].reshape(key_rows, head_local, HD)
    scores = (
        jnp.einsum("qhd,khd->hqk", query_heads, key_heads, preferred_element_type=jnp.float32)
        * score_scale
    )
    scores = jnp.where(allowed[None], scores, -1e30)
    new_high = jnp.maximum(row_high, jnp.max(scores, axis=2))
    probabilities = jnp.where(allowed[None], jnp.exp(scores - new_high[:, :, None]), 0.0)
    weight_sum = jnp.sum(probabilities, axis=2)
    weighted = jnp.einsum(
        "hqk,khd->hqd",
        probabilities.astype(jnp.bfloat16),
        value_heads,
        preferred_element_type=jnp.float32,
    )
    row_high, weight_sum, weighted = (new_high, weight_sum, weighted)
    attn_heads = weighted / weight_sum[:, :, None]
    log_sum = row_high + jnp.log(weight_sum)
    attended = (
        jnp.transpose(attn_heads, (1, 0, 2)).reshape(tok_count, local_width).astype(jnp.bfloat16)
    )
    attn_part = jnp.einsum("tf,df->td", attended, w_out, preferred_element_type=jnp.float32)
    resid = whole_input + head_total(attn_part)
    normed2, inverse2, mlp_in = layer_norm(resid, norm2_gain)
    inputs = mlp_in
    up_f = jnp.dot(
        inputs, lax.all_gather(w_up, "seq", axis=0, tiled=True), preferred_element_type=jnp.float32
    )
    gelu_value, gelu_back = jax.vjp(jax.nn.gelu, up_f)
    activated = gelu_value.astype(jnp.bfloat16)
    down_part = jnp.einsum(
        "tf,df->td",
        activated,
        lax.all_gather(w_down, "seq", axis=0, tiled=True),
        preferred_element_type=jnp.float32,
    )
    mlp_share = lax.psum_scatter(
        down_part.astype(jnp.bfloat16), "head", scatter_dimension=1, tiled=True
    ).astype(jnp.float32)
    column_start = lax.axis_index("head") * share_width
    resid_share = lax.dynamic_slice_in_dim(resid, column_start, share_width, 1)
    layer_output = (resid_share + mlp_share).astype(jnp.bfloat16)
    grad_out = full_rows(out_grad)
    grad_slice = grad_out
    grad_act = jnp.dot(
        grad_slice,
        lax.all_gather(w_down, "seq", axis=0, tiled=True),
        preferred_element_type=jnp.float32,
    )
    grad_up_b = gelu_back(grad_act)[0].astype(jnp.bfloat16)
    grad_mlp_in = jnp.einsum(
        "tf,df->td",
        grad_up_b,
        lax.all_gather(w_up, "seq", axis=0, tiled=True),
        preferred_element_type=jnp.float32,
    )
    inputs = mlp_in
    grad_slice = grad_out
    up_term = jnp.einsum("tc,tf->cf", inputs, grad_up_b, preferred_element_type=jnp.float32)
    down_term = jnp.einsum("tc,tf->cf", grad_slice, activated, preferred_element_type=jnp.float32)
    mlp_grads = lax.psum_scatter(
        jnp.concatenate([up_term, down_term], axis=1).astype(jnp.bfloat16),
        "seq",
        scatter_dimension=0,
        tiled=True,
    ).astype(jnp.float32)
    up_grad = mlp_grads[:, :up_width]
    down_grad = mlp_grads[:, up_width:]
    grad_norm2_in, gain2_grad = norm_back(head_total(grad_mlp_in), normed2, inverse2, norm2_gain)
    grad_resid = grad_out.astype(jnp.float32) + grad_norm2_in
    grad_branch = grad_resid.astype(jnp.bfloat16)
    out_weight_grad = jnp.einsum(
        "td,tf->df", grad_branch, attended, preferred_element_type=jnp.float32
    )
    grad_attended = jnp.dot(grad_branch, w_out, preferred_element_type=jnp.float32).astype(
        jnp.bfloat16
    )
    grad_heads = grad_attended.reshape(tok_count, head_local, HD)
    delta_rows = jnp.einsum("thd,htd->ht", grad_heads.astype(jnp.float32), attn_heads)

    def key_grads(turn_index, kv_now, grad_state):
        key_owner = jnp.mod(seq_index + turn_index, seq_count)
        allowed = visible(key_owner * tok_count, tok_count)
        grad_query, grad_kv = grad_state
        key_heads = kv_now[:, :local_width].reshape(tok_count, head_local, HD)
        value_heads = kv_now[:, local_width:].reshape(tok_count, head_local, HD)
        scores = (
            jnp.einsum("qhd,khd->hqk", query_heads, key_heads, preferred_element_type=jnp.float32)
            * score_scale
        )
        probabilities = jnp.where(allowed[None], jnp.exp(scores - log_sum[:, :, None]), 0.0)
        grad_probs = jnp.einsum(
            "qhd,khd->hqk", grad_heads, value_heads, preferred_element_type=jnp.float32
        )
        grad_scores = (probabilities * (grad_probs - delta_rows[:, :, None]) * score_scale).astype(
            jnp.bfloat16
        )
        grad_query = grad_query + jnp.einsum(
            "hqk,khd->qhd", grad_scores, key_heads, preferred_element_type=jnp.float32
        )
        grad_key = jnp.einsum(
            "hqk,qhd->khd", grad_scores, query_heads, preferred_element_type=jnp.float32
        ).reshape(tok_count, local_width)
        grad_value = jnp.einsum(
            "hqk,qhd->khd",
            probabilities.astype(jnp.bfloat16),
            grad_heads,
            preferred_element_type=jnp.float32,
        ).reshape(tok_count, local_width)
        return (grad_query, grad_kv + jnp.concatenate([grad_key, grad_value], axis=1))

    first_query, first_kv = key_grads(
        0,
        key_value,
        (
            jnp.zeros((tok_count, head_local, HD), jnp.float32),
            jnp.zeros((tok_count, 2 * local_width), jnp.float32),
        ),
    )

    def one_turn(turn_index, loop_state):
        kv_now, grad_query, grad_kv = loop_state
        kv_now = pass_keys(kv_now)
        grad_query, grad_kv = key_grads(turn_index, kv_now, (grad_query, grad_kv))
        return (kv_now, grad_query, pass_grads(grad_kv))

    unused_kv, grad_query, grad_kv = lax.fori_loop(
        1, seq_count, one_turn, (key_value, first_query, pass_grads(first_kv))
    )
    query_grad_b = grad_query.reshape(tok_count, local_width).astype(jnp.bfloat16)
    kv_grad_b = grad_kv.astype(jnp.bfloat16)
    key_grad_b = kv_grad_b[:, :local_width]
    value_grad_b = kv_grad_b[:, local_width:]
    grad_attn_in = jnp.einsum(
        "tf,df->td", query_grad_b, w_query, preferred_element_type=jnp.float32
    )
    grad_attn_in = grad_attn_in + jnp.einsum(
        "tf,df->td", key_grad_b, w_key, preferred_element_type=jnp.float32
    )
    grad_attn_in = grad_attn_in + jnp.einsum(
        "tf,df->td", value_grad_b, w_value, preferred_element_type=jnp.float32
    )
    query_weight_grad = jnp.einsum(
        "td,tf->df", attn_in, query_grad_b, preferred_element_type=jnp.float32
    )
    key_weight_grad = jnp.einsum(
        "td,tf->df", attn_in, key_grad_b, preferred_element_type=jnp.float32
    )
    value_weight_grad = jnp.einsum(
        "td,tf->df", attn_in, value_grad_b, preferred_element_type=jnp.float32
    )
    grad_norm1_in, gain1_grad = norm_back(head_total(grad_attn_in), normed1, inverse1, norm1_gain)
    grad_input = grad_resid + grad_norm1_in
    input_grad = lax.dynamic_slice_in_dim(grad_input, column_start, share_width, 1)
    summed = (
        lax.psum(gain1_grad.astype(jnp.bfloat16), "seq").astype(jnp.float32),
        lax.psum(query_weight_grad.astype(jnp.bfloat16), "seq").astype(jnp.float32),
        lax.psum(key_weight_grad.astype(jnp.bfloat16), "seq").astype(jnp.float32),
        lax.psum(value_weight_grad.astype(jnp.bfloat16), "seq").astype(jnp.float32),
        lax.psum(out_weight_grad.astype(jnp.bfloat16), "seq").astype(jnp.float32),
        lax.psum(gain2_grad.astype(jnp.bfloat16), "seq").astype(jnp.float32),
    )
    return (
        layer_output,
        input_grad,
        summed[0],
        summed[1],
        summed[2],
        summed[3],
        summed[4],
        summed[5],
        up_grad,
        down_grad,
    )


def solution(mesh):
    placed = (
        P("seq", "head"),
        P(),
        P(),
        P(),
        P(None, "head"),
        P(None, "head"),
        P(None, "head"),
        P(None, "head"),
        P(),
        P("seq", "head"),
        P("seq", "head"),
        P("seq", "head"),
    )
    return jax.shard_map(
        body,
        mesh=mesh,
        in_specs=placed,
        out_specs=(
            P("seq", "head"),
            P("seq", "head"),
            P(),
            P(None, "head"),
            P(None, "head"),
            P(None, "head"),
            P(None, "head"),
            P(),
            P("seq", "head"),
            P("seq", "head"),
        ),
        check_vma=False,
    )
```

profile of v0, /device:TPU:0, one launch (start us, length us, event | category | flops | bytes accessed | tf_op | source)
XLA Modules:
  0.0 1658.2 jit_solution(13067588237359774659)
XLA Ops:
  8.0 26.9 %all-gather.6.cloned.1.call-done = bf16[512,2048]{1,0:T(8,128)(2,1)} async-done(((bf16[512,512]{1,0:T(8,128)(2,1)}), bf16[512,2048]{1,0:T(8,128)(2,1)}) %all-gather.6.cloned.1.call-update) | async-done | bytes 2097168 | tf_op jit(solution)/shard_map/all_gather | solution.py:37
  55.2 114.7 %all-gather.8.cloned.1.call-done = bf16[4096,1024]{0,1:T(8,128)(2,1)} async-done(((bf16[512,1024]{0,1:T(8,128)(2,1)}), bf16[4096,1024]{0,1:T(8,128)(2,1)}) %all-gather.8.cloned.1.call-update) | async-done | bytes 8388624 | tf_op jit(solution)/shard_map/all_gather | solution.py:102
  176.2 17.3 %fusion.13 = (f32[4,512]{1,0:T(4,128)S(1)}, f32[4,512,4096]{2,1,0:T(8,128)}) fusion(pred[512,4096]{1,0:T(8,128)(4,1)S(1)} %copy-done.10, bf16[512,4,128]{0,2,1:T(8,128)(2,1)S(1)} %bitcast.112, bf16[4096,4,128]{0,2,1:T(8,128)(2,1)} %bitcast.117), kind=kOutput, calls=%fused_computation.22 | convolution fusion | flops 2172647424 | bytes 40378368 | tf_op jit(solution)/shard_map/qhd,khd->hqk/dot_general | solution.py:109
  193.5 16.5 fusion.14
  210.0 15.8 fusion.55
  229.9 89.4 %all-gather.12.cloned.1.call-done = bf16[2048,2048]{1,0:T(8,128)(2,1)} async-done(((bf16[256,2048]{1,0:T(8,128)(2,1)}), bf16[2048,2048]{1,0:T(8,128)(2,1)}) %all-gather.12.cloned.1.call-update) | async-done | bytes 8388624 | tf_op jit(solution)/shard_map/all_gather | solution.py:140
  319.3 10.5 fusion.75
  329.8 41.9 %all-reduce.7.cloned.1.call-done = bf16[512,2048]{1,0:T(8,128)(2,1)} async-done(((bf16[512,2048]{1,0:T(8,128)(2,1)}), bf16[512,2048]{1,0:T(8,128)(2,1)}) %all-reduce.7.cloned.1.call-update) | async-done | bytes 2097168 | tf_op jit(solution)/shard_map/psum | solution.py:41
  376.1 122.8 %all-gather.10.cloned.1.call-done = bf16[2048,2048]{1,0:T(8,128)(2,1)} async-done(((bf16[256,2048]{1,0:T(8,128)(2,1)}), bf16[2048,2048]{1,0:T(8,128)(2,1)}) %all-gather.10.cloned.1.call-update) | async-done | bytes 8388624 | tf_op jit(solution)/shard_map/all_gather | solution.py:133
  498.9 14.1 fusion.40
  523.8 46.0 %all-reduce.9.cloned.1.call-done = bf16[512,2048]{1,0:T(8,128)(2,1)} async-done(((bf16[512,2048]{1,0:T(8,128)(2,1)}), bf16[512,2048]{1,0:T(8,128)(2,1)}) %all-reduce.9.cloned.1.call-update) | async-done | bytes 2097168 | tf_op jit(solution)/shard_map/psum | solution.py:41
  597.2 18.3 %collective-permute-done.2 = bf16[512,1024]{0,1:T(8,128)(2,1)} collective-permute-done((bf16[512,1024]{0,1:T(8,128)(2,1)}, bf16[512,1024]{0,1:T(8,128)(2,1)}, u32[]{:S(2)}, u32[]{:S(2)}) %collective-permute-start.2) | collective-permute-done | bytes 1048608 | tf_op jit(solution)/shard_map/ppermute | solution.py:15
  618.3 361.4 %while.20 = (s32[]{:T(128)}, bf16[512,1024]{0,1:T(8,128)(2,1)}, f32[512,4,128]{2,0,1:T(8,128)}, f32[512,1024]{0,1:T(8,128)}, s32[512]{0:T(512)S(1)}, /*index=5*/...) while((s32[]{:T(128)}, bf16[512,1024]{0,1:T(8,128)(2,1)}, ...), condition=%wide.region_17.18_spmd.clone, body=%wide.region_15.17_spmd.clone.sunk | while | flops 1357649408 | bytes 65318408 | solution.py:233
  624.1 21.2 %collective-permute-done = bf16[512,1024]{0,1:T(8,128)(2,1)S(1)} collective-permute-done((bf16[512,1024]{0,1:T(8,128)(2,1)}, bf16[512,1024]{0,1:T(8,128)(2,1)S(1)}, u32[]{:S(2)}, u32[]{:S(2)}) %collective-permute-start) | collective-permute-done | bytes 1048608 | tf_op jit(solution)/shard_map/while/body/eval_jaxpr/ppermute | solution.py:15
  658.1 18.8 %collective-permute-done.1 = bf16[512,1024]{0,1:T(8,128)(2,1)S(1)} collective-permute-done((bf16[512,1024]{0,1:T(8,128)(2,1)S(1)}, bf16[512,1024]{0,1:T(8,128)(2,1)S(1)}, u32[]{:S(2)}, u32[]{:S(2)}) %collective-permute-start.1) | collective-permute-done | bytes 1048608 | tf_op jit(solution)/shard_map/while/body/eval_jaxpr/ppermute | solution.py:15
  684.3 19.4 %collective-permute-done = bf16[512,1024]{0,1:T(8,128)(2,1)S(1)} collective-permute-done((bf16[512,1024]{0,1:T(8,128)(2,1)}, bf16[512,1024]{0,1:T(8,128)(2,1)S(1)}, u32[]{:S(2)}, u32[]{:S(2)}) %collective-permute-start) | collective-permute-done | bytes 1048608 | tf_op jit(solution)/shard_map/while/body/eval_jaxpr/ppermute | solution.py:15
  716.5 17.0 %collective-permute-done.1 = bf16[512,1024]{0,1:T(8,128)(2,1)S(1)} collective-permute-done((bf16[512,1024]{0,1:T(8,128)(2,1)S(1)}, bf16[512,1024]{0,1:T(8,128)(2,1)S(1)}, u32[]{:S(2)}, u32[]{:S(2)}) %collective-permute-start.1) | collective-permute-done | bytes 1048608 | tf_op jit(solution)/shard_map/while/body/eval_jaxpr/ppermute | solution.py:15
  740.8 17.5 %collective-permute-done = bf16[512,1024]{0,1:T(8,128)(2,1)S(1)} collective-permute-done((bf16[512,1024]{0,1:T(8,128)(2,1)}, bf16[512,1024]{0,1:T(8,128)(2,1)S(1)}, u32[]{:S(2)}, u32[]{:S(2)}) %collective-permute-start) | collective-permute-done | bytes 1048608 | tf_op jit(solution)/shard_map/while/body/eval_jaxpr/ppermute | solution.py:15
  771.2 15.1 collective-permute-done.1
  793.7 15.7 collective-permute-done
  822.2 14.6 collective-permute-done.1
  844.1 13.9 collective-permute-done
  870.8 14.6 collective-permute-done.1
  892.8 12.1 collective-permute-done
  917.7 15.6 collective-permute-done.1
  940.8 14.0 collective-permute-done
  967.6 10.6 collective-permute-done.1
  990.7 10.8 convolution_convert_fusion.6
  1030.3 10.7 pad_maximum_fusion
  1049.5 21.6 %all-reduce = (bf16[2048]{0:T(1024)(128)(2,1)S(1)}, bf16[2048]{0:T(1024)(128)(2,1)S(1)}) all-reduce(bf16[2048]{0:T(1024)(128)(2,1)S(1)} %get-tuple-element.422, bf16[2048]{0:T(1024)(128)(2,1)S(1)} %copy-done.38), channel_id=1, replica_groups=mesh['seq'=8,'head'=4] {'seq'}, use_global_device_ids=true, to_apply=%region_22.23 | all-reduce | flops 4096 | bytes 16384 | tf_op jit(solution)/shard_map/psum | solution.py:262
  1081.4 274.7 %all-reduce.13.cloned.1.call-done = (bf16[2048,512]{1,0:T(8,128)(2,1)}, bf16[2048,512]{1,0:T(8,128)(2,1)}, bf16[2048,512]{1,0:T(8,128)(2,1)}, bf16[2048,512]{1,0:T(8,128)(2,1)}) async-done(((bf16[2048,512]{1,0:T(8,128)(2,1)}, bf16[2048,512]{1,0:T(8,128)(2,1)}, bf16[2048,512]{1,0:T(8,128)(2,1)}, bf16[2048,512]{1,0:T(8,128)(2,1)}), (bf16[2048,512]{1,0:T(8,128)(2,1)}, bf16[2048,512]{1,0:T(8,128)(2,1)}, ...) | async-done | bytes 8388624 | tf_op jit(solution)/shard_map/psum | solution.py:263
  1368.3 273.3 %reduce-scatter.5.cloned.1.call-done = bf16[256,4096]{0,1:T(8,128)(2,1)} async-done(((bf16[2048,4096]{0,1:T(8,128)(2,1)}), bf16[256,4096]{0,1:T(8,128)(2,1)}) %reduce-scatter.5.cloned.1.call-update) | async-done | bytes 2097168 | tf_op jit(solution)/shard_map/reduce_scatter | solution.py:167
  (320 shorter events, 297.8 us)
Async XLA Ops:
  7.2 219.4 %copy-start = (bf16[2048,512]{1,0:T(8,128)(2,1)S(1)}, bf16[2048,512]{1,0:T(8,128)(2,1)}, u32[]{:S(2)}) copy-start(bf16[2048,512]{1,0:T(8,128)(2,1)} %param.21) | copy-start | bytes 6291460
  7.2 32.1 %copy-start.39 = (f32[2048]{0:T(1024)S(1)}, f32[2048]{0:T(1024)}, u32[]{:S(2)}) copy-start(f32[2048]{0:T(1024)} %param.17) | copy-start | bytes 24580
  7.2 27.7 %all-gather.6.cloned.1.call-start = ((), (), s32[]{:S(2)}) async-start(), calls=%async_computation.2 | async-start | bytes 2621440 | tf_op jit(solution)/shard_map/all_gather | solution.py:37
  7.9 162.0 %all-gather.8.cloned.1.call-start = ((), (), s32[]{:S(2)}) async-start(), calls=%async_computation.3 | async-start | bytes 9437184 | tf_op jit(solution)/shard_map/all_gather | solution.py:102
  44.4 185.5 %all-gather.14.cloned.1.call-start = ((), (), s32[]{:S(2)}) async-start(), calls=%async_computation.8 | async-start | bytes 2621440 | tf_op jit(solution)/shard_map/all_gather | solution.py:37
  45.1 274.1 %all-gather.12.cloned.1.call-start = ((), (), s32[]{:S(2)}) async-start(), calls=%async_computation.6 | async-start | bytes 9437184 | tf_op jit(solution)/shard_map/all_gather | solution.py:140
  45.7 325.9 %all-reduce.7.cloned.1.call-start = ((), (), s32[]{:S(2)}) async-start(), calls=%async_computation.4 | async-start | bytes 4194304 | tf_op jit(solution)/shard_map/psum | solution.py:41
  229.3 269.6 %all-gather.10.cloned.1.call-start = ((), (), s32[]{:S(2)}) async-start(), calls=%async_computation.5 | async-start | bytes 9437184 | tf_op jit(solution)/shard_map/all_gather | solution.py:133
  229.8 340.0 %all-reduce.9.cloned.1.call-start = ((), (), s32[]{:S(2)}) async-start(), calls=%async_computation.9 | async-start | bytes 4194304 | tf_op jit(solution)/shard_map/psum | solution.py:41
  371.7 127.2 %copy-start.33 = (f32[2048]{0:T(1024)S(1)}, f32[2048]{0:T(1024)}, u32[]{:S(2)}) copy-start(f32[2048]{0:T(1024)} %param.22) | copy-start | bytes 24580
  520.1 524.2 %all-reduce.11.cloned.1.call-start = ((), (), s32[]{:S(2)}) async-start(), calls=%async_computation.10 | async-start | bytes 4194304 | tf_op jit(solution)/shard_map/psum | solution.py:41
  588.5 27.0 %collective-permute-start.2 = (bf16[512,1024]{0,1:T(8,128)(2,1)}, bf16[512,1024]{0,1:T(8,128)(2,1)}, u32[]{:S(2)}, u32[]{:S(2)}) collective-permute-start(bf16[512,1024]{0,1:T(8,128)(2,1)} %pad_maximum_fusion.2), channel_id=1, source_target_pairs={{4,0},{8,4},{12,8},{16,12},{20,16},{24,20},{28,24},{0,28},{5,1},{9... | collective-permute-start | bytes 3145736 | tf_op jit(solution)/shard_map/ppermute | solution.py:15
  594.6 23.7 %copy-start.31 = (bf16[512,512]{0,1:T(8,128)(2,1)S(1)}, bf16[512,512]{0,1:T(8,128)(2,1)}, u32[]{:S(2)}) copy-start(bf16[512,512]{0,1:T(8,128)(2,1)} %copy-done.30) | copy-start | bytes 1572868
  618.3 27.0 %collective-permute-start = (bf16[512,1024]{0,1:T(8,128)(2,1)}, bf16[512,1024]{0,1:T(8,128)(2,1)S(1)}, u32[]{:S(2)}, u32[]{:S(2)}) collective-permute-start(bf16[512,1024]{0,1:T(8,128)(2,1)} %get-tuple-element.589), channel_id=1, source_target_pairs={{4,0},{8,4},{12,8},{16,12},{20,16},{24,20},{28,24},{0,28},{5,1},{9... | collective-permute-start | bytes 3145736 | tf_op jit(solution)/shard_map/while/body/eval_jaxpr/ppermute | solution.py:15
  651.3 25.7 %collective-permute-start.1 = (bf16[512,1024]{0,1:T(8,128)(2,1)S(1)}, bf16[512,1024]{0,1:T(8,128)(2,1)S(1)}, u32[]{:S(2)}, u32[]{:S(2)}) collective-permute-start(bf16[512,1024]{0,1:T(8,128)(2,1)S(1)} %fusion.150), channel_id=1, source_target_pairs={{4,0},{8,4},{12,8},{16,12},{20,16},{24,20},{28,24},{0,28},{5,1},{9... | collective-permute-start | bytes 3145736 | tf_op jit(solution)/shard_map/while/body/eval_jaxpr/ppermute | solution.py:15
  658.1 20.4 %copy-start.9 = (f32[512,4,128]{2,0,1:T(8,128)}, f32[512,4,128]{2,0,1:T(8,128)S(1)}, u32[]{:S(2)}) copy-start(f32[512,4,128]{2,0,1:T(8,128)S(1)} %fusion.147) | copy-start | bytes 3145732 | tf_op jit(solution)/shard_map/while
  678.5 25.1 %collective-permute-start = (bf16[512,1024]{0,1:T(8,128)(2,1)}, bf16[512,1024]{0,1:T(8,128)(2,1)S(1)}, u32[]{:S(2)}, u32[]{:S(2)}) collective-permute-start(bf16[512,1024]{0,1:T(8,128)(2,1)} %get-tuple-element.589), channel_id=1, source_target_pairs={{4,0},{8,4},{12,8},{16,12},{20,16},{24,20},{28,24},{0,28},{5,1},{9... | collective-permute-start | bytes 3145736 | tf_op jit(solution)/shard_map/while/body/eval_jaxpr/ppermute | solution.py:15
  709.6 23.8 %collective-permute-start.1 = (bf16[512,1024]{0,1:T(8,128)(2,1)S(1)}, bf16[512,1024]{0,1:T(8,128)(2,1)S(1)}, u32[]{:S(2)}, u32[]{:S(2)}) collective-permute-start(bf16[512,1024]{0,1:T(8,128)(2,1)S(1)} %fusion.150), channel_id=1, source_target_pairs={{4,0},{8,4},{12,8},{16,12},{20,16},{24,20},{28,24},{0,28},{5,1},{9... | collective-permute-start | bytes 3145736 | tf_op jit(solution)/shard_map/while/body/eval_jaxpr/ppermute | solution.py:15
  716.5 18.6 %copy-start.9 = (f32[512,4,128]{2,0,1:T(8,128)}, f32[512,4,128]{2,0,1:T(8,128)S(1)}, u32[]{:S(2)}) copy-start(f32[512,4,128]{2,0,1:T(8,128)S(1)} %fusion.147) | copy-start | bytes 3145732 | tf_op jit(solution)/shard_map/while
  735.1 23.3 %collective-permute-start = (bf16[512,1024]{0,1:T(8,128)(2,1)}, bf16[512,1024]{0,1:T(8,128)(2,1)S(1)}, u32[]{:S(2)}, u32[]{:S(2)}) collective-permute-start(bf16[512,1024]{0,1:T(8,128)(2,1)} %get-tuple-element.589), channel_id=1, source_target_pairs={{4,0},{8,4},{12,8},{16,12},{20,16},{24,20},{28,24},{0,28},{5,1},{9... | collective-permute-start | bytes 3145736 | tf_op jit(solution)/shard_map/while/body/eval_jaxpr/ppermute | solution.py:15
  764.3 22.0 %collective-permute-start.1 = (bf16[512,1024]{0,1:T(8,128)(2,1)S(1)}, bf16[512,1024]{0,1:T(8,128)(2,1)S(1)}, u32[]{:S(2)}, u32[]{:S(2)}) collective-permute-start(bf16[512,1024]{0,1:T(8,128)(2,1)S(1)} %fusion.150), channel_id=1, source_target_pairs={{4,0},{8,4},{12,8},{16,12},{20,16},{24,20},{28,24},{0,28},{5,1},{9... | collective-permute-start | bytes 3145736 | tf_op jit(solution)/shard_map/while/body/eval_jaxpr/ppermute | solution.py:15
  787.9 21.4 %collective-permute-start = (bf16[512,1024]{0,1:T(8,128)(2,1)}, bf16[512,1024]{0,1:T(8,128)(2,1)S(1)}, u32[]{:S(2)}, u32[]{:S(2)}) collective-permute-start(bf16[512,1024]{0,1:T(8,128)(2,1)} %get-tuple-element.589), channel_id=1, source_target_pairs={{4,0},{8,4},{12,8},{16,12},{20,16},{24,20},{28,24},{0,28},{5,1},{9... | collective-permute-start | bytes 3145736 | tf_op jit(solution)/shard_map/while/body/eval_jaxpr/ppermute | solution.py:15
  815.3 21.4 %collective-permute-start.1 = (bf16[512,1024]{0,1:T(8,128)(2,1)S(1)}, bf16[512,1024]{0,1:T(8,128)(2,1)S(1)}, u32[]{:S(2)}, u32[]{:S(2)}) collective-permute-start(bf16[512,1024]{0,1:T(8,128)(2,1)S(1)} %fusion.150), channel_id=1, source_target_pairs={{4,0},{8,4},{12,8},{16,12},{20,16},{24,20},{28,24},{0,28},{5,1},{9... | collective-permute-start | bytes 3145736 | tf_op jit(solution)/shard_map/while/body/eval_jaxpr/ppermute | solution.py:15
  838.3 19.7 %collective-permute-start = (bf16[512,1024]{0,1:T(8,128)(2,1)}, bf16[512,1024]{0,1:T(8,128)(2,1)S(1)}, u32[]{:S(2)}, u32[]{:S(2)}) collective-permute-start(bf16[512,1024]{0,1:T(8,128)(2,1)} %get-tuple-element.589), channel_id=1, source_target_pairs={{4,0},{8,4},{12,8},{16,12},{20,16},{24,20},{28,24},{0,28},{5,1},{9... | collective-permute-start | bytes 3145736 | tf_op jit(solution)/shard_map/while/body/eval_jaxpr/ppermute | solution.py:15
  863.9 21.5 %collective-permute-start.1 = (bf16[512,1024]{0,1:T(8,128)(2,1)S(1)}, bf16[512,1024]{0,1:T(8,128)(2,1)S(1)}, u32[]{:S(2)}, u32[]{:S(2)}) collective-permute-start(bf16[512,1024]{0,1:T(8,128)(2,1)S(1)} %fusion.150), channel_id=1, source_target_pairs={{4,0},{8,4},{12,8},{16,12},{20,16},{24,20},{28,24},{0,28},{5,1},{9... | collective-permute-start | bytes 3145736 | tf_op jit(solution)/shard_map/while/body/eval_jaxpr/ppermute | solution.py:15
  887.0 17.9 %collective-permute-start = (bf16[512,1024]{0,1:T(8,128)(2,1)}, bf16[512,1024]{0,1:T(8,128)(2,1)S(1)}, u32[]{:S(2)}, u32[]{:S(2)}) collective-permute-start(bf16[512,1024]{0,1:T(8,128)(2,1)} %get-tuple-element.589), channel_id=1, source_target_pairs={{4,0},{8,4},{12,8},{16,12},{20,16},{24,20},{28,24},{0,28},{5,1},{9... | collective-permute-start | bytes 3145736 | tf_op jit(solution)/shard_map/while/body/eval_jaxpr/ppermute | solution.py:15
  910.9 22.5 %collective-permute-start.1 = (bf16[512,1024]{0,1:T(8,128)(2,1)S(1)}, bf16[512,1024]{0,1:T(8,128)(2,1)S(1)}, u32[]{:S(2)}, u32[]{:S(2)}) collective-permute-start(bf16[512,1024]{0,1:T(8,128)(2,1)S(1)} %fusion.150), channel_id=1, source_target_pairs={{4,0},{8,4},{12,8},{16,12},{20,16},{24,20},{28,24},{0,28},{5,1},{9... | collective-permute-start | bytes 3145736 | tf_op jit(solution)/shard_map/while/body/eval_jaxpr/ppermute | solution.py:15
  935.0 19.8 %collective-permute-start = (bf16[512,1024]{0,1:T(8,128)(2,1)}, bf16[512,1024]{0,1:T(8,128)(2,1)S(1)}, u32[]{:S(2)}, u32[]{:S(2)}) collective-permute-start(bf16[512,1024]{0,1:T(8,128)(2,1)} %get-tuple-element.589), channel_id=1, source_target_pairs={{4,0},{8,4},{12,8},{16,12},{20,16},{24,20},{28,24},{0,28},{5,1},{9... | collective-permute-start | bytes 3145736 | tf_op jit(solution)/shard_map/while/body/eval_jaxpr/ppermute | solution.py:15
  960.7 17.4 %collective-permute-start.1 = (bf16[512,1024]{0,1:T(8,128)(2,1)S(1)}, bf16[512,1024]{0,1:T(8,128)(2,1)S(1)}, u32[]{:S(2)}, u32[]{:S(2)}) collective-permute-start(bf16[512,1024]{0,1:T(8,128)(2,1)S(1)} %fusion.150), channel_id=1, source_target_pairs={{4,0},{8,4},{12,8},{16,12},{20,16},{24,20},{28,24},{0,28},{5,1},{9... | collective-permute-start | bytes 3145736 | tf_op jit(solution)/shard_map/while/body/eval_jaxpr/ppermute | solution.py:15
  990.5 88.6 %reduce-scatter.3.cloned.1.call-start = ((), (), s32[]{:S(2)}) async-start(), calls=%async_computation.7 | async-start | bytes 2621440 | tf_op jit(solution)/shard_map/reduce_scatter | solution.py:143
  1001.6 354.5 %all-reduce.13.cloned.1.call-start = ((), (), s32[]{:S(2)}) async-start(), calls=%async_computation.12 | async-start | bytes 16777216 | tf_op jit(solution)/shard_map/psum | solution.py:263
  1015.5 626.1 %reduce-scatter.5.cloned.1.call-start = ((), (), s32[]{:S(2)}) async-start(), calls=%async_computation.11 | async-start | bytes 18874368 | tf_op jit(solution)/shard_map/reduce_scatter | solution.py:167
  (57 other events, 345.2 us)
Sparse Core Ops, SparseCore 0:
  9.6 25.2 all-gather.5
  44.5 125.3 all-gather.7
  171.5 20.7 all-gather.13
  194.3 124.9 all-gather.11
  322.1 49.5 all-reduce.6
  373.9 124.9 all-gather.9
  520.2 49.5 all-reduce.8
  990.6 53.6 all-reduce.10
  1047.6 31.4 reduce-scatter.2
  1083.5 272.5 all-reduce.12
  1359.9 281.6 reduce-scatter.4
where the time goes:
time: 1660 us
  waiting for transfers between devices  1240 us (75%)
  matrix products  163 us (10%)
  other arithmetic  101 us (6%)
  starting transfers between devices  78 us (5%)
  local copies, waits for them, and re-layouts  41.7 us (3%)
  blocking collectives  21.6 us (1%)
    psum x1, waiting for transfers between devices, body(): lax.psum(query_weight_grad.astype(jnp.bfloat16), 'seq').astype(jnp.float32)  275 us
    reduce_scatter x1, waiting for transfers between devices, body(): lax.psum_scatter(jnp.concatenate([up_term, down_term], axis=1).astype(jnp...  273 us
    ppermute x15, waiting for transfers between devices, passed_along(): return lax.ppermute(block, axis, route)  238 us
    all_gather x1, waiting for transfers between devices, body(): lax.all_gather(w_up, 'seq', axis=0, tiled=True)  123 us
    all_gather x1, waiting for transfers between devices, body(): kv_piece = lax.all_gather(key_value, 'seq', axis=0, tiled=True)  115 us
    psum x3, waiting for transfers between devices, head_total(): lax.psum(partial_sum.astype(jnp.bfloat16), 'head').astype(jnp.float32)  91.1 us
    all_gather x1, waiting for transfers between devices, body(): lax.all_gather(w_down, 'seq', axis=0, tiled=True)  89.4 us
    ppermute x15, starting transfers between devices, passed_along(): return lax.ppermute(block, axis, route)  76.5 us
  transfers between devices with their start and end apart: 26, of which 25 were waited for; matrix products, arithmetic and copies ran while one was open for 11% of the time, Pallas kernels for 0%

commit v1 on v0

v1 whole, which is shorter than its diff:
```python
import jax
import jax.numpy as jnp
from jax import lax
from jax.sharding import Mesh, PartitionSpec as P

HD = 128
NORM_EPS = 1e-05
BF16 = jnp.bfloat16
F32 = jnp.float32
LAYER = ("x", "y", "core")


def shifted(block, axis, step, first, last):
    return lax.ppermute(block, axis, [(i, i + step) for i in range(first, last + 1)])


def swapped(block, axis):
    return lax.ppermute(block, axis, [(0, 1), (1, 0)])


def line_gather_up(block, count):
    found, moving = [], block
    for hop in range(1, count):
        moving = shifted(moving, "z", 1, hop - 1, count - 2)
        found.append(moving)
    return found


def line_gather_down(block, count):
    found, moving = [], block
    for hop in range(1, count):
        moving = shifted(moving, "z", -1, 1, count - hop)
        found.append(moving)
    return found


def line_whole(block, count, z):
    up = line_gather_up(block, count)
    down = line_gather_down(block, count)
    rows = block.shape[0]
    both = jnp.concatenate(up[::-1] + [block] + down, axis=0)
    return lax.dynamic_slice_in_dim(both, (count - 1 - z) * rows, count * rows, 0)


def line_reduce(partial, count, z):
    rows = partial.shape[0] // count

    def chunk(index):
        index = jnp.clip(index, 0, count - 1)
        return lax.dynamic_slice_in_dim(partial, index * rows, rows, 0)

    up = down = None
    for hop in range(1, count):
        own = chunk(count - hop + z)
        send = own if up is None else (own.astype(F32) + up.astype(F32)).astype(BF16)
        up = shifted(send, "z", 1, 0, min(hop - 1, count - 2))
        own = chunk(z - count + hop)
        send = own if down is None else (own.astype(F32) + down.astype(F32)).astype(BF16)
        down = shifted(send, "z", -1, max(count - hop, 1), count - 1)
    total = chunk(z).astype(F32)
    if up is not None:
        total = total + up.astype(F32) + down.astype(F32)
    return total


def layer_gather(share):
    wide = lax.all_gather(share, ("y", "core"), axis=1, tiled=True)
    return lax.all_gather(wide, "x", axis=0, tiled=True)


def layer_reduce(partial):
    tall = lax.psum_scatter(partial, "x", scatter_dimension=0, tiled=True)
    return lax.psum_scatter(tall, ("y", "core"), scatter_dimension=1, tiled=True)


def body(
    layer_input,
    clip_lengths,
    key_padding,
    norm1_gain,
    w_query,
    w_key,
    w_value,
    w_out,
    norm2_gain,
    w_up,
    w_down,
    out_grad,
):
    count = lax.axis_size("z")
    z, x = lax.axis_index("z"), lax.axis_index("x")
    column = lax.axis_index("y") * lax.axis_size("core") + lax.axis_index("core")
    share_rows, share_width = layer_input.shape
    rows = 2 * share_rows
    width = w_query.shape[0]
    local = w_query.shape[1] // 2
    heads = local // HD
    hidden = w_up.shape[1] // 2
    scale = HD ** (-0.5)
    gain1_share = lax.dynamic_slice_in_dim(norm1_gain, column * share_width, share_width)
    gain2_share = lax.dynamic_slice_in_dim(norm2_gain, column * share_width, share_width)

    def half(weight, which):
        size = weight.shape[1] // 2
        return lax.dynamic_slice_in_dim(weight, which * size, size, 1)

    def layer_rows(weight):
        other = swapped(half(weight, 1 - x), "x")
        own = half(weight, x)
        return jnp.where(
            x == 0, jnp.concatenate([own, other], 0), jnp.concatenate([other, own], 0)
        )

    down_full = line_whole(layer_rows(w_down), count, z)
    up_full = line_whole(layer_rows(w_up), count, z)

    whole_input = layer_gather(layer_input)
    grad_out = layer_gather(out_grad)

    wide = whole_input.astype(F32)
    mean1 = jnp.mean(wide, axis=1, keepdims=True)
    centred = wide - mean1
    inverse1 = lax.rsqrt(jnp.mean(centred * centred, axis=1, keepdims=True) + NORM_EPS)
    attn_in = (centred * inverse1 * norm1_gain).astype(BF16)

    query_w, key_w, value_w, out_w = (half(w, x) for w in (w_query, w_key, w_value, w_out))
    query = jnp.dot(attn_in, query_w, preferred_element_type=F32).astype(BF16)
    key = jnp.dot(attn_in, key_w, preferred_element_type=F32).astype(BF16)
    value = jnp.dot(attn_in, value_w, preferred_element_type=F32).astype(BF16)
    own_kv = jnp.concatenate([key, value], axis=1)
    below = line_gather_up(own_kv, count)

    clip_ends = jnp.cumsum(clip_lengths)

    def clip_of(positions):
        return jnp.sum((positions[:, None] >= clip_ends[None, :]).astype(jnp.int32), axis=1)

    query_pos = z * rows + jnp.arange(rows, dtype=jnp.int32)
    query_clip = clip_of(query_pos)

    def visible(first_key, key_rows):
        key_pos = first_key + jnp.arange(key_rows, dtype=jnp.int32)
        keep = key_padding[jnp.clip(key_pos, 0, key_padding.shape[0] - 1)] > 0
        same = (query_clip[:, None] == clip_of(key_pos)[None, :]) & (key_pos >= 0)[None, :]
        causal = key_pos[None, :] <= query_pos[:, None]
        return same & causal & (keep[None, :] | (key_pos[None, :] == query_pos[:, None]))

    def split(block):
        return block.reshape(block.shape[0], heads, HD)

    query_heads = split(query)
    all_kv = jnp.concatenate(below[::-1] + [own_kv], axis=0)
    allowed = visible((z - count + 1) * rows, count * rows)
    scores = (
        jnp.einsum("qhd,khd->hqk", query_heads, split(all_kv[:, :local]), preferred_element_type=F32)
        * scale
    )
    scores = jnp.where(allowed[None], scores, -1e30)
    high = jnp.max(scores, axis=2, keepdims=True)
    weights = jnp.where(allowed[None], jnp.exp(scores - high), 0.0)
    total = jnp.sum(weights, axis=2, keepdims=True)
    attn_heads = (
        jnp.einsum(
            "hqk,khd->hqd", weights.astype(BF16), split(all_kv[:, local:]), preferred_element_type=F32
        )
        / total
    )
    log_sum = high + jnp.log(total)
    attended = jnp.transpose(attn_heads, (1, 0, 2)).reshape(rows, local).astype(BF16)
    attn_part = jnp.einsum("tf,df->td", attended, out_w, preferred_element_type=F32).astype(BF16)
    resid = layer_input.astype(F32) + layer_reduce(attn_part).astype(F32)

    mean_own = jnp.mean(resid, axis=1, keepdims=True)
    spread_own = jnp.sum((resid - mean_own) ** 2, axis=1, keepdims=True)
    parts = lax.all_gather(
        jnp.concatenate([mean_own, spread_own], axis=1), ("y", "core"), axis=0, tiled=False
    )
    mean2 = jnp.mean(parts[:, :, 0], axis=0)[:, None]
    var2 = (
        jnp.sum(parts[:, :, 1], axis=0)[:, None]
        + share_width * jnp.sum((parts[:, :, 0] - mean2[:, 0]) ** 2, axis=0)[:, None]
    ) / width
    inverse2 = lax.rsqrt(var2 + NORM_EPS)
    normed2 = (resid - mean2) * inverse2
    mlp_in = layer_gather((normed2 * gain2_share).astype(BF16))

    grad_act = jnp.dot(grad_out, down_full, preferred_element_type=F32)
    up_f = jnp.dot(mlp_in, up_full, preferred_element_type=F32)
    gelu_value, gelu_back = jax.vjp(jax.nn.gelu, up_f)
    activated = gelu_value.astype(BF16)
    grad_up = gelu_back(grad_act)[0].astype(BF16)
    grad_mlp_part = jnp.einsum("tf,df->td", grad_up, up_full, preferred_element_type=F32)
    grad_mlp = layer_reduce(grad_mlp_part.astype(BF16)).astype(F32)
    down_part = jnp.einsum("tf,df->td", activated, down_full, preferred_element_type=F32)
    layer_output = (resid + layer_reduce(down_part.astype(BF16)).astype(F32)).astype(BF16)

    down_term = jnp.einsum("tc,tf->cf", grad_out, activated, preferred_element_type=F32)
    up_term = jnp.einsum("tc,tf->cf", mlp_in, grad_up, preferred_element_type=F32)

    def weight_home(term):
        mine = line_reduce(term.astype(BF16), count, z).astype(BF16)
        size = mine.shape[0] // 2
        other = swapped(lax.dynamic_slice_in_dim(mine, (1 - x) * size, size, 0), "x")
        own = lax.dynamic_slice_in_dim(mine, x * size, size, 0)
        return jnp.where(
            x == 0, jnp.concatenate([own, other], 1), jnp.concatenate([other, own], 1)
        ).astype(F32)

    down_grad = weight_home(down_term)
    up_grad = weight_home(up_term)

    def norm_back(grad, normed, inverse, gain_share):
        scaled = grad * gain_share
        sums = lax.psum(
            jnp.stack([jnp.sum(scaled, axis=1), jnp.sum(scaled * normed, axis=1)], axis=1),
            ("y", "core"),
        )
        centre, slope = sums[:, :1] / width, sums[:, 1:] / width
        return inverse * (scaled - centre - normed * slope), jnp.sum(grad * normed, axis=0)

    back2, gain2_part = norm_back(grad_mlp, normed2, inverse2, gain2_share)
    grad_resid = out_grad.astype(F32) + back2
    grad_branch = layer_gather(grad_resid.astype(BF16))
    out_weight_part = jnp.einsum("td,tf->df", grad_branch, attended, preferred_element_type=F32)
    grad_attended = jnp.dot(grad_branch, out_w, preferred_element_type=F32).astype(BF16)
    grad_heads = split(grad_attended)
    delta = jnp.einsum("thd,htd->ht", grad_heads.astype(F32), attn_heads)

    def stage(kv, distance):
        keys, values = split(kv[:, :local]), split(kv[:, local:])
        allowed = visible((z - distance) * rows, rows)
        scores = jnp.einsum("qhd,khd->hqk", query_heads, keys, preferred_element_type=F32) * scale
        probs = jnp.where(allowed[None], jnp.exp(scores - log_sum), 0.0)
        grad_probs = jnp.einsum("qhd,khd->hqk", grad_heads, values, preferred_element_type=F32)
        grad_scores = (probs * (grad_probs - delta[:, :, None]) * scale).astype(BF16)
        grad_query = jnp.einsum("hqk,khd->qhd", grad_scores, keys, preferred_element_type=F32)
        grad_key = jnp.einsum("hqk,qhd->khd", grad_scores, query_heads, preferred_element_type=F32)
        grad_value = jnp.einsum(
            "hqk,qhd->khd", probs.astype(BF16), grad_heads, preferred_element_type=F32
        )
        return grad_query.reshape(rows, local), jnp.concatenate(
            [grad_key.reshape(rows, local), grad_value.reshape(rows, local)], axis=1
        )

    grad_query, moving = jnp.zeros((rows, local), F32), None
    for hop in range(1, count):
        more, grad_kv = stage(below[count - hop - 1], count - hop)
        grad_query = grad_query + more
        if moving is not None:
            grad_kv = grad_kv + moving.astype(F32)
        moving = shifted(grad_kv.astype(BF16), "z", -1, max(count - hop, 1), count - 1)
    more, grad_kv = stage(own_kv, 0)
    grad_query = (grad_query + more).astype(BF16)
    if moving is not None:
        grad_kv = grad_kv + moving.astype(F32)
    grad_kv = grad_kv.astype(BF16)
    grads = jnp.concatenate([grad_query, grad_kv], axis=1)

    qkv_w = jnp.concatenate([query_w, key_w, value_w], axis=1)
    grad_attn_part = jnp.einsum("tf,df->td", grads, qkv_w, preferred_element_type=F32)
    grad_attn = layer_reduce(grad_attn_part.astype(BF16)).astype(F32)
    qkv_part = jnp.einsum("td,tf->df", attn_in, grads, preferred_element_type=F32)

    def weight_everywhere(partial):
        mine = line_reduce(partial.astype(BF16), count, z).astype(BF16)
        return line_whole(mine, count, z)

    def both_halves(block):
        other = swapped(block, "x")
        return jnp.where(
            x == 0, jnp.concatenate([block, other], 1), jnp.concatenate([other, block], 1)
        ).astype(F32)

    out_weight_grad = both_halves(weight_everywhere(out_weight_part))
    qkv_grad = weight_everywhere(qkv_part)
    query_grad = both_halves(qkv_grad[:, :local])
    key_grad = both_halves(qkv_grad[:, local : 2 * local])
    value_grad = both_halves(qkv_grad[:, 2 * local :])

    def share_of(stat):
        return lax.dynamic_slice_in_dim(stat, x * share_rows, share_rows, 0)

    mean1_share, inverse1_share = share_of(mean1), share_of(inverse1)
    normed1 = (layer_input.astype(F32) - mean1_share) * inverse1_share
    back1, gain1_part = norm_back(grad_attn, normed1, inverse1_share, gain1_share)
    input_grad = grad_resid + back1

    gains = lax.psum(jnp.stack([gain1_part, gain2_part]), ("z", "x"))
    gains = lax.all_gather(gains, ("y", "core"), axis=1, tiled=True)
    return (
        layer_output,
        input_grad,
        gains[0],
        query_grad,
        key_grad,
        value_grad,
        out_weight_grad,
        gains[1],
        up_grad,
        down_grad,
    )


def solution(mesh):
    seq, head = mesh.shape["seq"], mesh.shape["head"]
    fine = Mesh(mesh.devices.reshape(seq // 2, 2, head // 2, 2), ("z", "x", "y", "core"))
    seq_axes, head_axes = ("z", "x"), ("y", "core")
    both, columns = P(seq_axes, head_axes), P(None, head_axes)
    return jax.shard_map(
        body,
        mesh=fine,
        in_specs=(both, P(), P(), P(), columns, columns, columns, columns, P(), both, both, both),
        out_specs=(both, both, P(), columns, columns, columns, columns, P(), both, both),
        check_vma=False,
    )
```

time: 1660 us -> 1370 us (0.83)
  waiting for transfers between devices: 1240 us -> 697 us
  starting transfers between devices: 78 us -> 191 us
  local copies, waits for them, and re-layouts: 41.7 us -> 118 us
  other arithmetic: 101 us -> 137 us
  blocking collectives: 21.6 us -> 40.5 us
    psum x4 -> x0, waiting for transfers between devices: 366 us -> none  [the longest x1 275 us: body(): lax.psum(query_weight_grad.astype(jnp.bfloat16), 'seq').astype(jnp.float32)]
    all_gather x5 -> x8, waiting for transfers between devices: 354 us -> 129 us  [the longest x4 80 us: layer_gather(): return lax.all_gather(wide, 'x', axis=0, tiled=True)]
    ppermute x15 -> x62, waiting for transfers between devices: 238 us -> 371 us  [the longest x54 322 us: shifted(): lax.ppermute(block, axis, [(i, i + step) for i in range(first, last + 1)])]
    ppermute x15 -> x62, starting transfers between devices: 76.5 us -> 189 us  [the longest x54 181 us: shifted(): lax.ppermute(block, axis, [(i, i + step) for i in range(first, last + 1)])]
    reduce_scatter x2 -> x8, waiting for transfers between devices: 277 us -> 195 us  [the longest x4 129 us: layer_reduce(): tall = lax.psum_scatter(partial, 'x', scatter_dimension=0, tiled=True)]
    gather x0 -> x5, local copies, waits for them, and re-layouts: none -> 47.6 us  [visible(): keep = key_padding[jnp.clip(key_pos, 0, key_padding.shape[0] - 1)] > 0]
    convert_element_type x23 -> x28, other arithmetic: 35.4 us -> 66.2 us  [the longest x8 21.3 us: line_reduce(): (own.astype(F32) + up.astype(F32)).astype(BF16)]
    unnamed x87 -> x192, local copies, waits for them, and re-layouts: 14.9 us -> 42.9 us
  transfers between devices with their start and end apart: 26 -> 78, of which waited for: 25 -> 33; matrix products, arithmetic and copies ran while one was open for 11% -> 20% of each run, Pallas kernels for 0% -> 0%
where the time goes in v1:
time: 1370 us
  waiting for transfers between devices  697 us (51%)
  starting transfers between devices  191 us (14%)
  matrix products  167 us (12%)
  other arithmetic  137 us (10%)
  local copies, waits for them, and re-layouts  118 us (9%)
  blocking collectives  40.5 us (3%)
  between operations  16.1 us (1%)
    ppermute x54, waiting for transfers between devices, shifted(): lax.ppermute(block, axis, [(i, i + step) for i in range(first, last + 1)])  322 us
    ppermute x54, starting transfers between devices, shifted(): lax.ppermute(block, axis, [(i, i + step) for i in range(first, last + 1)])  181 us
    reduce_scatter x4, waiting for transfers between devices, layer_reduce(): tall = lax.psum_scatter(partial, 'x', scatter_dimension=0, tiled=True)  129 us
    all_gather x4, waiting for transfers between devices, layer_gather(): return lax.all_gather(wide, 'x', axis=0, tiled=True)  80 us
    reduce_scatter x4, waiting for transfers between devices, layer_reduce(): lax.psum_scatter(tall, ('y', 'core'), scatter_dimension=1, tiled=True)  66.6 us
    ppermute x8, waiting for transfers between devices, swapped(): return lax.ppermute(block, axis, [(0, 1), (1, 0)])  49.4 us
    all_gather x4, waiting for transfers between devices, layer_gather(): wide = lax.all_gather(share, ('y', 'core'), axis=1, tiled=True)  49.1 us
    gather x5, local copies, waits for them, and re-layouts, visible(): keep = key_padding[jnp.clip(key_pos, 0, key_padding.shape[0] - 1)] > 0  47.6 us
  transfers between devices with their start and end apart: 78, of which 33 were waited for; matrix products, arithmetic and copies ran while one was open for 20% of the time, Pallas kernels for 0%

profile of v1, /device:TPU:0, one launch (start us, length us, event | category | flops | bytes accessed | tf_op | source)
XLA Modules:
  0.0 1365.1 jit_solution(3534585046489497606)
XLA Ops:
  8.0 26.9 %all-gather.10.cloned.1.call-done = bf16[512,2048]{1,0:T(8,128)(2,1)} async-done(((bf16[512,512]{1,0:T(8,128)(2,1)}), bf16[512,2048]{1,0:T(8,128)(2,1)}) %all-gather.10.cloned.1.call-update) | async-done | bytes 2097168 | tf_op jit(solution)/shard_map/all_gather | solution.py:67
  37.6 55.6 %all-gather.12.cloned.1.call-done = bf16[1024,2048]{1,0:T(8,128)(2,1)} async-done(((bf16[512,2048]{1,0:T(8,128)(2,1)}), bf16[1024,2048]{1,0:T(8,128)(2,1)}) %all-gather.12.cloned.1.call-update) | async-done | bytes 4194320 | tf_op jit(solution)/shard_map/all_gather | solution.py:68
  108.7 21.5 %collective-permute-done = bf16[1024,512]{0,1:T(8,128)(2,1)} collective-permute-done((bf16[1024,512]{0,1:T(8,128)(2,1)}, bf16[1024,512]{0,1:T(8,128)(2,1)}, u32[]{:S(2)}, u32[]{:S(2)}) %collective-permute-start) | collective-permute-done | bytes 1048608 | tf_op jit(solution)/shard_map/ppermute | solution.py:14
  131.9 23.0 %gather_fusion = s32[4096]{0:T(1024)S(1)} fusion(s32[4096]{0:T(1024)S(1)} %copy-done.2, s32[4096]{0:T(1024)S(1)} %broadcast_clamp_fusion), kind=kCustom, calls=%fused_computation | custom fusion | bytes 49152 | tf_op jit(solution)/shard_map/gather | solution.py:143
  167.2 14.8 %maximum_maximum_fusion = bf16[4096,512]{0,1:T(8,128)(2,1)S(1)} fusion(bf16[1024,256]{0,1:T(8,128)(2,1)S(1)} %copy-done.28, bf16[1024,256]{0,1:T(8,128)(2,1)S(1)} %convolution_convert_fusion.11, bf16[1024,512]{0,1:T(8,128)(2,1)} %collective-permute-done, bf16[1024,512]{0,1:T(8,128)(2,1)} %collective-permute-done.1, ...), kind=kLoop, calls=%fused_computation.41 | loop fusion | flops 20971520 | bytes 8388608 | tf_op jit(solution)/shard_map/concatenate | solution.py:152
  184.3 17.6 %fusion = (f32[2,1024]{1,0:T(2,128)S(1)}, f32[2,1024,4096]{2,1,0:T(8,128)}) fusion(pred[1024,4096]{1,0:T(8,128)(4,1)} %or_and_fusion, bf16[1024,2,128]{0,2,1:T(8,128)(2,1)S(1)} %bitcast.172, bf16[4096,2,128]{0,2,1:T(8,128)(2,1)} %bitcast.201), kind=kOutput, calls=%fused_computation.7 | convolution fusion | flops 2172647424 | bytes 40378368 | tf_op jit(solution)/shard_map/qhd,khd->hqk/dot_general | solution.py:155
  201.9 17.6 %fusion.1 = f32[2,1024]{1,0:T(2,128)S(1)} fusion(f32[2,1024,4096]{2,1,0:T(8,128)} %get-tuple-element.100, f32[2,1024]{1,0:T(2,128)S(1)} %get-tuple-element.99, pred[1024,4096]{1,0:T(8,128)(4,1)} %or_and_fusion), kind=kLoop, calls=%fused_computation.8 | loop fusion | flops 41940992 | bytes 37765120 | tf_op jit(solution)/shard_map/reduce_sum | solution.py:161
  219.5 16.4 %fusion.90 = (bf16[1024,2,128]{0,2,1:T(8,128)(2,1)S(1)}, f32[2,1024,128]{1,2,0:T(8,128)}) fusion(f32[1024,2]{0,1:T(2,128)S(1)} %bitcast.221, bf16[4096,2,128]{0,2,1:T(8,128)(2,1)S(1)} %bitcast.200, f32[2,1024,4096]{2,1,0:T(8,128)} %get-tuple-element.100, f32[2,1024]{1,0:T(2,128)S(1)} %get-tuple-element.99, pred[1024,4096]{1,0:T(8,128)(4,1)S(1)} %copy-done.7), kind=kOutput, calls=%fused_computation.160 | convolution fusion | flops 2189950976 | bytes 41435136 | tf_op jit(solution)/shard_map/hqk,khd->hqd/dot_general | solution.py:163
  240.1 70.0 %reduce-scatter.9.cloned.1.call-done = bf16[512,2048]{1,0:T(8,128)(2,1)} async-done(((bf16[1024,2048]{1,0:T(8,128)(2,1)}), bf16[512,2048]{1,0:T(8,128)(2,1)}) %reduce-scatter.9.cloned.1.call-update) | async-done | bytes 2097168 | tf_op jit(solution)/shard_map/reduce_scatter | solution.py:72
  310.9 33.1 %reduce-scatter.11.cloned.1.call-done = bf16[512,512]{1,0:T(8,128)(2,1)} async-done(((bf16[512,2048]{1,0:T(8,128)(2,1)}), bf16[512,512]{1,0:T(8,128)(2,1)}) %reduce-scatter.11.cloned.1.call-update) | async-done | bytes 524304 | tf_op jit(solution)/shard_map/reduce_scatter | solution.py:73
  354.7 22.1 %all-gather.14.cloned.1.call-done = bf16[512,2048]{1,0:T(8,128)(2,1)} async-done(((bf16[512,512]{1,0:T(8,128)(2,1)}), bf16[512,2048]{1,0:T(8,128)(2,1)}) %all-gather.14.cloned.1.call-update) | async-done | bytes 2097168 | tf_op jit(solution)/shard_map/all_gather | solution.py:67
  426.1 18.5 %collective-permute-done.11 = bf16[512,1024]{1,0:T(8,128)(2,1)} collective-permute-done((bf16[512,1024]{1,0:T(8,128)(2,1)}, bf16[512,1024]{1,0:T(8,128)(2,1)}, u32[]{:S(2)}, u32[]{:S(2)}) %collective-permute-start.11) | collective-permute-done | bytes 1048608 | tf_op jit(solution)/shard_map/ppermute | solution.py:14
  447.7 15.2 %collective-permute-done.14 = bf16[512,1024]{1,0:T(8,128)(2,1)} collective-permute-done((bf16[512,1024]{1,0:T(8,128)(2,1)}, bf16[512,1024]{1,0:T(8,128)(2,1)}, u32[]{:S(2)}, u32[]{:S(2)}) %collective-permute-start.14) | collective-permute-done | bytes 1048608 | tf_op jit(solution)/shard_map/ppermute | solution.py:14
  467.4 17.9 %collective-permute-done.8 = bf16[512,1024]{1,0:T(8,128)(2,1)} collective-permute-done((bf16[512,1024]{1,0:T(8,128)(2,1)}, bf16[512,1024]{1,0:T(8,128)(2,1)}, u32[]{:S(2)}, u32[]{:S(2)}) %collective-permute-start.8) | collective-permute-done | bytes 1048608 | tf_op jit(solution)/shard_map/ppermute | solution.py:14
  486.6 21.2 %collective-permute-done.15 = bf16[512,1024]{1,0:T(8,128)(2,1)} collective-permute-done((bf16[512,1024]{1,0:T(8,128)(2,1)}, bf16[512,1024]{1,0:T(8,128)(2,1)}, u32[]{:S(2)}, u32[]{:S(2)}) %collective-permute-start.15) | collective-permute-done | bytes 1048608 | tf_op jit(solution)/shard_map/ppermute | solution.py:14
  530.6 20.1 %collective-permute-done.16 = bf16[512,1024]{1,0:T(8,128)(2,1)S(1)} collective-permute-done((bf16[512,1024]{1,0:T(8,128)(2,1)}, bf16[512,1024]{1,0:T(8,128)(2,1)S(1)}, u32[]{:S(2)}, u32[]{:S(2)}) %collective-permute-start.16) | collective-permute-done | bytes 1048608 | tf_op jit(solution)/shard_map/ppermute | solution.py:14
  561.7 11.4 fusion.21
  580.6 58.6 %reduce-scatter.17.cloned.1.call-done = bf16[512,2048]{1,0:T(8,128)(2,1)} async-done(((bf16[1024,2048]{1,0:T(8,128)(2,1)}), bf16[512,2048]{1,0:T(8,128)(2,1)}) %reduce-scatter.17.cloned.1.call-update) | async-done | bytes 2097168 | tf_op jit(solution)/shard_map/reduce_scatter | solution.py:72
  639.6 33.5 %reduce-scatter.19.cloned.1.call-done = bf16[512,512]{1,0:T(8,128)(2,1)} async-done(((bf16[512,2048]{1,0:T(8,128)(2,1)}), bf16[512,512]{1,0:T(8,128)(2,1)}) %reduce-scatter.19.cloned.1.call-update) | async-done | bytes 524304 | tf_op jit(solution)/shard_map/reduce_scatter | solution.py:73
  742.6 24.4 %all-gather.24.cloned.1.call-done = bf16[1024,2048]{1,0:T(8,128)(2,1)} async-done(((bf16[512,2048]{1,0:T(8,128)(2,1)}), bf16[1024,2048]{1,0:T(8,128)(2,1)}) %all-gather.24.cloned.1.call-update) | async-done | bytes 4194320 | tf_op jit(solution)/shard_map/all_gather | solution.py:68
  820.7 43.8 %collective-permute-done.19 = bf16[1024,512]{0,1:T(8,128)(2,1)S(1)} collective-permute-done((bf16[1024,512]{0,1:T(8,128)(2,1)S(1)}, bf16[1024,512]{0,1:T(8,128)(2,1)S(1)}, u32[]{:S(2)}, u32[]{:S(2)}) %collective-permute-start.19) | collective-permute-done | bytes 1048608 | tf_op jit(solution)/shard_map/ppermute | solution.py:14
  929.0 14.3 %collective-permute-done.55 = bf16[512,1024]{0,1:T(8,128)(2,1)} collective-permute-done((bf16[512,1024]{0,1:T(8,128)(2,1)}, bf16[512,1024]{0,1:T(8,128)(2,1)}, u32[]{:S(2)}, u32[]{:S(2)}) %collective-permute-start.55) | collective-permute-done | bytes 1048608 | tf_op jit(solution)/shard_map/ppermute | solution.py:14
  970.9 11.7 collective-permute-done.49
  991.1 33.6 %collective-permute-done.35 = bf16[512,256]{1,0:T(8,128)(2,1)S(1)} collective-permute-done((bf16[512,256]{1,0:T(8,128)(2,1)S(1)}, bf16[512,256]{1,0:T(8,128)(2,1)S(1)}, u32[]{:S(2)}, u32[]{:S(2)}) %collective-permute-start.35) | collective-permute-done | bytes 262176 | tf_op jit(solution)/shard_map/ppermute | solution.py:14
  1048.9 25.4 %collective-permute-start.22 = (bf16[512,768]{1,0:T(8,128)(2,1)}, bf16[512,768]{1,0:T(8,128)(2,1)S(1)}, u32[]{:S(2)}, u32[]{:S(2)}) collective-permute-start(bf16[512,768]{1,0:T(8,128)(2,1)} %get-tuple-element.65), channel_id=1, source_target_pairs={{0,8},{8,16},{16,24},{1,9},{9,17},{17,25},{2,10},{10,18},{18,26},{... | collective-permute-start | bytes 2359304 | tf_op jit(solution)/shard_map/ppermute | solution.py:14
  1081.0 21.3 %collective-permute-start.37 = (bf16[512,256]{1,0:T(8,128)(2,1)S(1)}, bf16[512,256]{1,0:T(8,128)(2,1)S(1)}, u32[]{:S(2)}, u32[]{:S(2)}) collective-permute-start(bf16[512,256]{1,0:T(8,128)(2,1)S(1)} %get-tuple-element.73), channel_id=1, source_target_pairs={{0,8},{8,16},{16,24},{1,9},{9,17},{17,25},{2,10},{10,18},{18,26},{... | collective-permute-start | bytes 786440 | tf_op jit(solution)/shard_map/ppermute | solution.py:14
  1118.3 22.9 %collective-permute-done.40 = bf16[512,256]{1,0:T(8,128)(2,1)S(1)} collective-permute-done((bf16[512,256]{1,0:T(8,128)(2,1)S(1)}, bf16[512,256]{1,0:T(8,128)(2,1)S(1)}, u32[]{:S(2)}, u32[]{:S(2)}) %collective-permute-start.40) | collective-permute-done | bytes 262176 | tf_op jit(solution)/shard_map/ppermute | solution.py:14
  1141.2 25.7 %collective-permute-start.26 = (bf16[512,768]{1,0:T(8,128)(2,1)S(1)}, bf16[512,768]{1,0:T(8,128)(2,1)}, u32[]{:S(2)}, u32[]{:S(2)}) collective-permute-start(bf16[512,768]{1,0:T(8,128)(2,1)S(1)} %add_convert_fusion.5), channel_id=1, source_target_pairs={{0,8},{8,16},{16,24},{1,9},{9,17},{17,25},{2,10},{10,18},{18,26},{... | collective-permute-start | bytes 2359304 | tf_op jit(solution)/shard_map/ppermute | solution.py:14
  1169.7 15.5 %collective-permute-done.41 = bf16[512,256]{1,0:T(8,128)(2,1)S(1)} collective-permute-done((bf16[512,256]{1,0:T(8,128)(2,1)S(1)}, bf16[512,256]{1,0:T(8,128)(2,1)S(1)}, u32[]{:S(2)}, u32[]{:S(2)}) %collective-permute-start.41) | collective-permute-done | bytes 262176 | tf_op jit(solution)/shard_map/ppermute | solution.py:14
  1198.3 15.3 %collective-permute-done.45 = bf16[512,256]{1,0:T(8,128)(2,1)S(1)} collective-permute-done((bf16[512,256]{1,0:T(8,128)(2,1)}, bf16[512,256]{1,0:T(8,128)(2,1)S(1)}, u32[]{:S(2)}, u32[]{:S(2)}) %collective-permute-start.45) | collective-permute-done | bytes 262176 | tf_op jit(solution)/shard_map/ppermute | solution.py:14
  1286.2 17.6 %collective-permute-done.33 = bf16[2048,256]{1,0:T(8,128)(2,1)} collective-permute-done((bf16[2048,256]{1,0:T(8,128)(2,1)}, bf16[2048,256]{1,0:T(8,128)(2,1)}, u32[]{:S(2)}, u32[]{:S(2)}) %collective-permute-start.33) | collective-permute-done | bytes 1048608 | tf_op jit(solution)/shard_map/ppermute | solution.py:18
  1325.0 18.7 %psum.23 = f32[2,512]{1,0:T(2,128)S(1)} all-reduce(f32[2,512]{1,0:T(2,128)S(1)} %pad_maximum_fusion.8), channel_id=1, replica_groups=mesh['z'=4,'x'=2,'y'=2,'core'=2] {'z','x'}, use_global_device_ids=true, to_apply=%region_31.32 | all-reduce | flops 1024 | bytes 8192 | tf_op jit(solution)/shard_map/psum | solution.py:288
  (486 shorter events, 543.9 us)
Async XLA Ops:
  7.9 85.3 %all-gather.12.cloned.1.call-start = ((), (), s32[]{:S(2)}) async-start(), calls=%async_computation.9 | async-start | bytes 6291456 | tf_op jit(solution)/shard_map/all_gather | solution.py:68
  34.9 275.2 %reduce-scatter.9.cloned.1.call-start = ((), (), s32[]{:S(2)}) async-start(), calls=%async_computation.10 | async-start | bytes 6291456 | tf_op jit(solution)/shard_map/reduce_scatter | solution.py:72
  240.0 104.0 %reduce-scatter.11.cloned.1.call-start = ((), (), s32[]{:S(2)}) async-start(), calls=%async_computation.11 | async-start | bytes 2621440 | tf_op jit(solution)/shard_map/reduce_scatter | solution.py:73
  310.1 66.7 %all-gather.14.cloned.1.call-start = ((), (), s32[]{:S(2)}) async-start(), calls=%async_computation.12 | async-start | bytes 2621440 | tf_op jit(solution)/shard_map/all_gather | solution.py:67
  354.1 92.2 %all-gather.18.cloned.1.call-start = ((), (), s32[]{:S(2)}) async-start(), calls=%async_computation.16 | async-start | bytes 2621440 | tf_op jit(solution)/shard_map/all_gather | solution.py:67
  354.7 197.1 %all-gather.16.cloned.1.call-start = ((), (), s32[]{:S(2)}) async-start(), calls=%async_computation.13 | async-start | bytes 6291456 | tf_op jit(solution)/shard_map/all_gather | solution.py:68
  376.9 184.9 %all-gather.20.cloned.1.call-start = ((), (), s32[]{:S(2)}) async-start(), calls=%async_computation.17 | async-start | bytes 6291456 | tf_op jit(solution)/shard_map/all_gather | solution.py:68
  413.3 49.5 %collective-permute-start.14 = (bf16[512,1024]{1,0:T(8,128)(2,1)}, bf16[512,1024]{1,0:T(8,128)(2,1)}, u32[]{:S(2)}, u32[]{:S(2)}) collective-permute-start(bf16[512,1024]{1,0:T(8,128)(2,1)} %maximum_select_fusion.5), channel_id=1, source_target_pairs={{8,0},{16,8},{24,16},{9,1},{17,9},{25,17},{10,2},{18,10},{26,18},{... | collective-permute-start | bytes 3145736 | tf_op jit(solution)/shard_map/ppermute | solution.py:14
  446.3 192.9 %reduce-scatter.17.cloned.1.call-start = ((), (), s32[]{:S(2)}) async-start(), calls=%async_computation.18 | async-start | bytes 6291456 | tf_op jit(solution)/shard_map/reduce_scatter | solution.py:72
  465.8 48.5 %collective-permute-start.13 = (bf16[512,1024]{1,0:T(8,128)(2,1)}, bf16[512,1024]{1,0:T(8,128)(2,1)}, u32[]{:S(2)}, u32[]{:S(2)}) collective-permute-start(bf16[512,1024]{1,0:T(8,128)(2,1)} %collective-permute-done.12), channel_id=1, source_target_pairs={{16,24},{17,25},{18,26},{19,27},{20,28},{21,29},{22,30},{23,31}} | collective-permute-start | bytes 3145736 | tf_op jit(solution)/shard_map/ppermute | solution.py:14
  580.5 92.6 %reduce-scatter.19.cloned.1.call-start = ((), (), s32[]{:S(2)}) async-start(), calls=%async_computation.19 | async-start | bytes 2621440 | tf_op jit(solution)/shard_map/reduce_scatter | solution.py:73
  639.2 69.8 %all-gather.22.cloned.1.call-start = ((), (), s32[]{:S(2)}) async-start(), calls=%async_computation.20 | async-start | bytes 2621440 | tf_op jit(solution)/shard_map/all_gather | solution.py:67
  684.1 82.9 %all-gather.24.cloned.1.call-start = ((), (), s32[]{:S(2)}) async-start(), calls=%async_computation.21 | async-start | bytes 6291456 | tf_op jit(solution)/shard_map/all_gather | solution.py:68
  709.0 261.8 %reduce-scatter.21.cloned.1.call-start = ((), (), s32[]{:S(2)}) async-start(), calls=%async_computation.22 | async-start | bytes 6291456 | tf_op jit(solution)/shard_map/reduce_scatter | solution.py:72
  816.2 48.3 %collective-permute-start.19 = (bf16[1024,512]{0,1:T(8,128)(2,1)S(1)}, bf16[1024,512]{0,1:T(8,128)(2,1)S(1)}, u32[]{:S(2)}, u32[]{:S(2)}) collective-permute-start(bf16[1024,512]{0,1:T(8,128)(2,1)S(1)} %fusion.51), channel_id=1, source_target_pairs={{8,0},{16,8},{24,16},{9,1},{17,9},{25,17},{10,2},{18,10},{26,18},{... | collective-permute-start | bytes 3145736 | tf_op jit(solution)/shard_map/ppermute | solution.py:14
  870.9 327.4 %reduce-scatter.13.cloned.1.call-start = ((), (), s32[]{:S(2)}) async-start(), calls=%async_computation.14 | async-start | bytes 6291456 | tf_op jit(solution)/shard_map/reduce_scatter | solution.py:72
  881.3 442.0 %reduce-scatter.23.cloned.1.call-start = ((), (), s32[]{:S(2)}) async-start(), calls=%async_computation.23 | async-start | bytes 2621440 | tf_op jit(solution)/shard_map/reduce_scatter | solution.py:73
  917.6 119.0 %collective-permute-start.58 = (bf16[512,1024]{0,1:T(8,128)(2,1)S(1)}, bf16[512,1024]{0,1:T(8,128)(2,1)}, u32[]{:S(2)}, u32[]{:S(2)}) collective-permute-start(bf16[512,1024]{0,1:T(8,128)(2,1)S(1)} %get-tuple-element.58), channel_id=1, source_target_pairs={{24,16},{25,17},{26,18},{27,19},{28,20},{29,21},{30,22},{31,23}} | collective-permute-start | bytes 3145736 | tf_op jit(solution)/shard_map/ppermute | solution.py:14
  923.6 59.0 %collective-permute-start.49 = (bf16[512,1024]{0,1:T(8,128)(2,1)}, bf16[512,1024]{0,1:T(8,128)(2,1)}, u32[]{:S(2)}, u32[]{:S(2)}) collective-permute-start(bf16[512,1024]{0,1:T(8,128)(2,1)} %add_convert_fusion.4), channel_id=1, source_target_pairs={{0,8},{8,16},{1,9},{9,17},{2,10},{10,18},{3,11},{11,19},{4,12},{12... | collective-permute-start | bytes 3145736 | tf_op jit(solution)/shard_map/ppermute | solution.py:14
  946.1 92.3 %collective-permute-start.56 = (bf16[512,1024]{0,1:T(8,128)(2,1)}, bf16[512,1024]{0,1:T(8,128)(2,1)}, u32[]{:S(2)}, u32[]{:S(2)}) collective-permute-start(bf16[512,1024]{0,1:T(8,128)(2,1)} %fusion.59), channel_id=1, source_target_pairs={{0,8},{8,16},{1,9},{9,17},{2,10},{10,18},{3,11},{11,19},{4,12},{12... | collective-permute-start | bytes 3145736 | tf_op jit(solution)/shard_map/ppermute | solution.py:14
  960.1 66.1 %collective-permute-start.23 = (bf16[512,768]{1,0:T(8,128)(2,1)}, bf16[512,768]{1,0:T(8,128)(2,1)}, u32[]{:S(2)}, u32[]{:S(2)}) collective-permute-start(bf16[512,768]{1,0:T(8,128)(2,1)} %get-tuple-element.68), channel_id=1, source_target_pairs={{24,16},{25,17},{26,18},{27,19},{28,20},{29,21},{30,22},{31,23}} | collective-permute-start | bytes 2359304 | tf_op jit(solution)/shard_map/ppermute | solution.py:14
  964.1 63.5 %collective-permute-start.21 = (bf16[512,768]{1,0:T(8,128)(2,1)}, bf16[512,768]{1,0:T(8,128)(2,1)}, u32[]{:S(2)}, u32[]{:S(2)}) collective-permute-start(bf16[512,768]{1,0:T(8,128)(2,1)} %add_convert_fusion.9), channel_id=1, source_target_pairs={{0,8},{8,16},{1,9},{9,17},{2,10},{10,18},{3,11},{11,19},{4,12},{12... | collective-permute-start | bytes 2359304 | tf_op jit(solution)/shard_map/ppermute | solution.py:14
  970.9 384.3 %reduce-scatter.15.cloned.1.call-start = ((), (), s32[]{:S(2)}) async-start(), calls=%async_computation.15 | async-start | bytes 2621440 | tf_op jit(solution)/shard_map/reduce_scatter | solution.py:73
  1024.7 51.1 %collective-permute-start.52 = (bf16[512,1024]{0,1:T(8,128)(2,1)}, bf16[512,1024]{0,1:T(8,128)(2,1)S(1)}, u32[]{:S(2)}, u32[]{:S(2)}) collective-permute-start(bf16[512,1024]{0,1:T(8,128)(2,1)} %get-tuple-element.60), channel_id=1, source_target_pairs={{16,8},{24,16},{17,9},{25,17},{18,10},{26,18},{19,11},{27,19},{20,... | collective-permute-start | bytes 3145736 | tf_op jit(solution)/shard_map/ppermute | solution.py:14
  1043.8 123.3 %collective-permute-start.50 = (bf16[512,1024]{0,1:T(8,128)(2,1)}, bf16[512,1024]{0,1:T(8,128)(2,1)S(1)}, u32[]{:S(2)}, u32[]{:S(2)}) collective-permute-start(bf16[512,1024]{0,1:T(8,128)(2,1)} %get-tuple-element.59), channel_id=1, source_target_pairs={{0,8},{8,16},{16,24},{1,9},{9,17},{17,25},{2,10},{10,18},{18,26},{... | collective-permute-start | bytes 3145736 | tf_op jit(solution)/shard_map/ppermute | solution.py:14
  1048.9 65.3 %collective-permute-start.22 = (bf16[512,768]{1,0:T(8,128)(2,1)}, bf16[512,768]{1,0:T(8,128)(2,1)S(1)}, u32[]{:S(2)}, u32[]{:S(2)}) collective-permute-start(bf16[512,768]{1,0:T(8,128)(2,1)} %get-tuple-element.65), channel_id=1, source_target_pairs={{0,8},{8,16},{16,24},{1,9},{9,17},{17,25},{2,10},{10,18},{18,26},{... | collective-permute-start | bytes 2359304 | tf_op jit(solution)/shard_map/ppermute | solution.py:14
  1079.7 88.7 %collective-permute-start.53 = (bf16[512,1024]{0,1:T(8,128)(2,1)}, bf16[512,1024]{0,1:T(8,128)(2,1)}, u32[]{:S(2)}, u32[]{:S(2)}) collective-permute-start(bf16[512,1024]{0,1:T(8,128)(2,1)} %add_convert_fusion.1), channel_id=1, source_target_pairs={{8,0},{16,8},{24,16},{9,1},{17,9},{25,17},{10,2},{18,10},{26,18},{... | collective-permute-start | bytes 3145736 | tf_op jit(solution)/shard_map/ppermute | solution.py:14
  1108.8 79.7 %collective-permute-start.57 = (bf16[512,1024]{0,1:T(8,128)(2,1)}, bf16[512,1024]{0,1:T(8,128)(2,1)}, u32[]{:S(2)}, u32[]{:S(2)}) collective-permute-start(bf16[512,1024]{0,1:T(8,128)(2,1)} %get-tuple-element.55), channel_id=1, source_target_pairs={{0,8},{8,16},{16,24},{1,9},{9,17},{17,25},{2,10},{10,18},{18,26},{... | collective-permute-start | bytes 3145736 | tf_op jit(solution)/shard_map/ppermute | solution.py:14
  1114.2 78.2 %collective-permute-start.60 = (bf16[512,1024]{0,1:T(8,128)(2,1)}, bf16[512,1024]{0,1:T(8,128)(2,1)}, u32[]{:S(2)}, u32[]{:S(2)}) collective-permute-start(bf16[512,1024]{0,1:T(8,128)(2,1)} %fusion.58), channel_id=1, source_target_pairs={{8,0},{16,8},{24,16},{9,1},{17,9},{25,17},{10,2},{18,10},{26,18},{... | collective-permute-start | bytes 3145736 | tf_op jit(solution)/shard_map/ppermute | solution.py:14
  1141.2 48.6 %collective-permute-start.26 = (bf16[512,768]{1,0:T(8,128)(2,1)S(1)}, bf16[512,768]{1,0:T(8,128)(2,1)}, u32[]{:S(2)}, u32[]{:S(2)}) collective-permute-start(bf16[512,768]{1,0:T(8,128)(2,1)S(1)} %add_convert_fusion.5), channel_id=1, source_target_pairs={{0,8},{8,16},{16,24},{1,9},{9,17},{17,25},{2,10},{10,18},{18,26},{... | collective-permute-start | bytes 2359304 | tf_op jit(solution)/shard_map/ppermute | solution.py:14
  1192.4 65.5 %collective-permute-start.54 = (bf16[256,1024]{0,1:T(8,128)(2,1)}, bf16[256,1024]{0,1:T(8,128)(2,1)}, u32[]{:S(2)}, u32[]{:S(2)}) collective-permute-start(bf16[256,1024]{0,1:T(8,128)(2,1)} %get-tuple-element.72), channel_id=1, source_target_pairs={{0,4},{4,0},{1,5},{5,1},{2,6},{6,2},{3,7},{7,3},{8,12},{12,8},{9,1... | collective-permute-start | bytes 1572872 | tf_op jit(solution)/shard_map/ppermute | solution.py:18
  1259.7 59.2 %collective-permute-start.34 = (bf16[2048,256]{1,0:T(8,128)(2,1)}, bf16[2048,256]{1,0:T(8,128)(2,1)}, u32[]{:S(2)}, u32[]{:S(2)}) collective-permute-start(bf16[2048,256]{1,0:T(8,128)(2,1)} %get-tuple-element.52), channel_id=1, source_target_pairs={{0,4},{4,0},{1,5},{5,1},{2,6},{6,2},{3,7},{7,3},{8,12},{12,8},{9,1... | collective-permute-start | bytes 3145736 | tf_op jit(solution)/shard_map/ppermute | solution.py:18
  (129 other events, 4007.0 us)
Sparse Core Ops, SparseCore 0:
  9.6 25.2 all-gather.9
  36.5 56.7 all-gather.11
  240.2 69.8 reduce-scatter.8
  312.6 31.3 reduce-scatter.10
  354.2 22.5 all-gather.13
  378.3 22.5 all-gather.17
  402.4 56.7 all-gather.15
  460.7 56.7 all-gather.19
  580.7 58.4 reduce-scatter.16
  641.7 31.3 reduce-scatter.18
  684.2 23.6 all-gather.21
  709.3 57.6 all-gather.23
  871.0 54.2 reduce-scatter.20
  928.2 54.3 reduce-scatter.12
  984.9 31.4 reduce-scatter.22
  1198.4 39.5 reduce-scatter.14

commit v2 on v1

--- a/solution.py
+++ b/solution.py
@@ -1,6 +1,10 @@
+import functools
+
 import jax
 import jax.numpy as jnp
 from jax import lax
+from jax.experimental import pallas as pl
+from jax.experimental.pallas import tpu as pltpu
 from jax.sharding import Mesh, PartitionSpec as P
 
 HD = 128
@@ -8,6 +12,675 @@
 BF16 = jnp.bfloat16
 F32 = jnp.float32
 LAYER = ("x", "y", "core")
+
+
+MESH = pl.DeviceIdType.MESH
+LOG2E = 1.4426950408889634
+
+
+def remote(src, dst, sends, recvs, slot, **device):
+    return pltpu.make_async_remote_copy(
+        src_ref=src,
+        dst_ref=dst,
+        send_sem=sends.at[slot],
+        recv_sem=recvs.at[slot],
+        device_id=device,
+        device_id_type=MESH,
+    )
+
+
+def contract(left, right, dims):
+    return lax.dot_general(left, right, (dims, ((), ())), preferred_element_type=F32)
+
+
+class Place:
+    def __init__(self, count):
+        self.count = count
+        self.z = lax.axis_index("z")
+        self.x, self.y, self.c = lax.axis_index("x"), lax.axis_index("y"), lax.axis_index("core")
+        self.ox, self.oy, self.oc = 1 - self.x, 1 - self.y, 1 - self.c
+
+    def meet(self):
+        barrier = pltpu.get_barrier_semaphore()
+        for device in ({"x": self.ox}, {"y": self.oy}, {"core": self.oc}):
+            pl.semaphore_signal(barrier, inc=1, device_id=device, device_id_type=MESH)
+        above, below = self.z < self.count - 1, self.z > 0
+        for there, step in ((above, 1), (below, -1)):
+
+            @pl.when(there)
+            def _():
+                pl.semaphore_signal(
+                    barrier, inc=1, device_id={"z": self.z + step}, device_id_type=MESH
+                )
+
+        pl.semaphore_wait(barrier, 3 + above.astype(jnp.int32) + below.astype(jnp.int32))
+
+
+class Gather:
+    def __init__(self, at, array, rows, width, sends, recvs, lead=()):
+        self.at, self.array, self.sends, self.recvs, self.lead = at, array, sends, recvs, lead
+        self.rows, self.width = rows, width
+
+    def block(self, xi, yi, ci, first=0, size=None):
+        size = self.rows if size is None else size
+        return self.array.at[
+            pl.ds(pl.multiple_of(xi * self.rows + first, size), size),
+            pl.ds(pl.multiple_of((2 * yi + ci) * self.width, self.width), self.width),
+        ]
+
+    def copy(self, k, landing=False):
+        at, half = self.at, self.rows // 2
+        x, y, c, ox, oy, oc = at.x, at.y, at.c, at.ox, at.oy, at.oc
+        place = {
+            0: ((x, y, c), (ox, y, c), {"x": ox}),
+            1: ((x, y, c), (x, oy, c), {"y": oy}),
+            2: ((x, y, c), (x, y, oc), {"core": oc}),
+            3: ((ox, y, c, 0, half), (ox, oy, c, 0, half), {"y": oy}),
+            4: ((x, oy, c, half, half), (ox, oy, c, half, half), {"x": ox}),
+            5: ((ox, y, c), (ox, y, oc), {"core": oc}),
+            6: ((x, oy, c), (x, oy, oc), {"core": oc}),
+            7: ((ox, oy, c, 0, half), (ox, oy, oc, 0, half), {"core": oc}),
+            8: ((ox, oy, c, half, half), (ox, oy, oc, half, half), {"core": oc}),
+        }
+        source, lands, device = place[k]
+        ref = self.block(*(lands if landing else source))
+        return remote(ref, ref, self.sends, self.recvs, self.lead + (k,), **device)
+
+    def start(self):
+        for k in (0, 1, 2):
+            self.copy(k).start()
+
+    def middle(self):
+        self.copy(0, True).wait_recv()
+        self.copy(3).start()
+        self.copy(5).start()
+        self.copy(1, True).wait_recv()
+        self.copy(4).start()
+        self.copy(6).start()
+
+    def corner(self):
+        self.copy(3, True).wait_recv()
+        self.copy(7).start()
+        self.copy(4, True).wait_recv()
+        self.copy(8).start()
+
+    def end(self):
+        for k in (2, 5, 6, 7, 8):
+            self.copy(k, True).wait_recv()
+
+    def drain(self):
+        for k in range(9):
+            self.copy(k).wait_send()
+
+
+class Reduce:
+    def __init__(self, at, array, rows, width, buffers, sends, recvs):
+        self.at, self.array, self.sends, self.recvs = at, array, sends, recvs
+        self.rows, self.width = rows, width
+        self.twin, self.corner_x, self.corner_y, self.from_x, self.from_y = buffers
+
+    def block(self, xi, yi, ci, first=0, size=None):
+        return Gather.block(self, xi, yi, ci, first, size)
+
+    def copy(self, k):
+        at, half = self.at, self.rows // 2
+        x, y, c, ox, oy, oc = at.x, at.y, at.c, at.ox, at.oy, at.oc
+        low, high = pl.ds(0, half), pl.ds(half, half)
+        place = {
+            0: ((ox, oy, oc), self.twin.at[0], {"core": oc}),
+            1: ((ox, y, oc), self.twin.at[1], {"core": oc}),
+            2: ((x, oy, oc), self.twin.at[2], {"core": oc}),
+            3: ((x, y, oc), self.twin.at[3], {"core": oc}),
+            4: ((ox, oy, c, 0, half), self.corner_y, {"y": oy}),
+            5: ((ox, oy, c, half, half), self.corner_x, {"x": ox}),
+            6: ((ox, y, c, half, half), self.from_x.at[high], {"x": ox}),
+            7: ((x, oy, c, 0, half), self.from_y.at[low], {"y": oy}),
+            8: ((ox, y, c, 0, half), self.from_x.at[low], {"x": ox}),
+            9: ((x, oy, c, half, half), self.from_y.at[high], {"y": oy}),
+        }
+        source, lands, device = place[k]
+        return remote(self.block(*source), lands, self.sends, self.recvs, (k,), **device)
+
+    def add(self, target, other):
+        rows = target.shape[0]
+        tile = min(rows, 128)
+
+        @pl.loop(0, rows // tile)
+        def _(i):
+            part = pl.ds(pl.multiple_of(i * tile, tile), tile)
+            target[part, :] = (target[part, :].astype(F32) + other[part, :].astype(F32)).astype(
+                target.dtype
+            )
+
+    def start(self):
+        for k in (0, 1, 2, 3):
+            self.copy(k).start()
+
+    def twins(self):
+        at, half = self.at, self.rows // 2
+        x, y, c, ox, oy = at.x, at.y, at.c, at.ox, at.oy
+        self.copy(0).wait_recv()
+        self.add(self.block(ox, oy, c), self.twin.at[0])
+        self.copy(4).start()
+        self.copy(5).start()
+        self.copy(1).wait_recv()
+        self.add(self.block(ox, y, c), self.twin.at[1])
+        self.copy(6).start()
+        self.copy(2).wait_recv()
+        self.add(self.block(x, oy, c), self.twin.at[2])
+        self.copy(7).start()
+        self.copy(3).wait_recv()
+
+    def corners(self):
+        at, half = self.at, self.rows // 2
+        self.copy(4).wait_recv()
+        self.add(self.block(at.ox, at.y, at.c, 0, half), self.corner_y)
+        self.copy(8).start()
+        self.copy(5).wait_recv()
+        self.add(self.block(at.x, at.oy, at.c, half, half), self.corner_x)
+        self.copy(9).start()
+
+    def end(self, store):
+        for k in (6, 7, 8, 9):
+            self.copy(k).wait_recv()
+        own = self.block(self.at.x, self.at.y, self.at.c)
+        tile = min(self.rows, 128)
+
+        @pl.loop(0, self.rows // tile)
+        def _(i):
+            part = pl.ds(pl.multiple_of(i * tile, tile), tile)
+            store(
+                part,
+                own[part, :].astype(F32)
+                + self.twin[3, part, :].astype(F32)
+                + self.from_x[part, :].astype(F32)
+                + self.from_y[part, :].astype(F32),
+            )
+
+    def drain(self):
+        for k in range(10):
+            self.copy(k).wait_send()
+
+
+def reduce_scratch(rows, width):
+    return [
+        pltpu.VMEM((4, rows, width), BF16),
+        pltpu.VMEM((rows // 2, width), BF16),
+        pltpu.VMEM((rows // 2, width), BF16),
+        pltpu.VMEM((rows, width), BF16),
+        pltpu.VMEM((rows, width), BF16),
+    ]
+
+
+def normed_rows(rows):
+    mean = jnp.mean(rows, axis=1, keepdims=True)
+    centred = rows - mean
+    inverse = lax.rsqrt(jnp.mean(centred * centred, axis=1, keepdims=True) + NORM_EPS)
+    return centred * inverse, inverse
+
+
+class Weights:
+    def __init__(self, at, which, weight, whole, sems):
+        self.at, self.which, self.weight, self.whole = at, which, weight, whole
+        self.local, self.xs, self.xr, self.us, self.ds, self.rs = sems
+        self.half = weight.shape[1] // 2
+
+    def columns(self, which):
+        return self.weight.at[:, pl.ds(pl.multiple_of(which * self.half, self.half), self.half)]
+
+    def own(self):
+        at = self.at
+        return pltpu.make_async_copy(
+            self.columns(at.x), self.whole.at[at.z, at.x], self.local.at[self.which]
+        )
+
+    def swap(self, landing=False):
+        at = self.at
+        dst = self.whole.at[at.z, at.ox] if landing else self.whole.at[at.z, at.x]
+        return remote(self.columns(at.ox), dst, self.xs, self.xr, (self.which,), x=at.ox)
+
+    def move(self, layer, part, step):
+        ref = self.whole.at[layer, part]
+        sends = self.us if step > 0 else self.ds
+        return pltpu.make_async_remote_copy(
+            src_ref=ref,
+            dst_ref=ref,
+            send_sem=sends.at[self.which, layer, part],
+            recv_sem=self.rs.at[self.which, layer, part],
+            device_id={"z": self.at.z + step},
+            device_id_type=MESH,
+        )
+
+    def first(self, mine):
+        at = self.at
+        part = at.x if mine else at.ox
+        if mine:
+            self.own().wait()
+        else:
+            self.swap(True).wait_recv()
+
+        @pl.when(at.z < at.count - 1)
+        def _():
+            self.move(at.z, part, 1).start()
+
+        @pl.when(at.z > 0)
+        def _():
+            self.move(at.z, part, -1).start()
+
+    def hop(self, distance, mine):
+        at = self.at
+        part = at.x if mine else at.ox
+
+        @pl.when(at.z >= distance)
+        def _():
+            self.move(at.z - distance, part, 1).wait_recv()
+
+            @pl.when(at.z < at.count - 1)
+            def _():
+                self.move(at.z - distance, part, 1).start()
+
+        @pl.when(at.z + distance < at.count)
+        def _():
+            self.move(at.z + distance, part, -1).wait_recv()
+
+            @pl.when(at.z > 0)
+            def _():
+                self.move(at.z + distance, part, -1).start()
+
+    def drain(self):
+        at = self.at
+        self.swap().wait_send()
+        for part in (0, 1):
+
+            @pl.loop(0, at.count)
+            def _(layer):
+                @pl.when((layer <= at.z) & (at.z < at.count - 1))
+                def _():
+                    self.move(layer, part, 1).wait_send()
+
+                @pl.when((layer >= at.z) & (at.z > 0))
+                def _():
+                    self.move(layer, part, -1).wait_send()
+
+
+def front_kernel(
+    count,
+    xs,
+    og,
+    w_query,
+    w_key,
+    w_value,
+    w_out,
+    w_up,
+    w_down,
+    gain1,
+    gain2,
+    start_of,
+    key_place,
+    x_all,
+    in_all,
+    kv_all,
+    query_out,
+    attended_out,
+    log_out,
+    branch_out,
+    mlp_out,
+    og_all,
+    down_all,
+    up_all,
+    qkv_w,
+    out_w,
+    query,
+    kv,
+    high,
+    total,
+    sums,
+    attended,
+    partial,
+    branch,
+    twin,
+    corner_x,
+    corner_y,
+    from_x,
+    from_y,
+    load_sem,
+    gather_send,
+    gather_recv,
+    line_send,
+    line_recv,
+    w_local,
+    w_xs,
+    w_xr,
+    w_us,
+    w_ds,
+    w_rs,
+    reduce_send,
+    reduce_recv,
+):
+    at = Place(count)
+    z, x, y, c = at.z, at.x, at.y, at.c
+    rows, width = xs.shape
+    group = 2 * rows
+    local = w_query.shape[1] // 2
+    heads = local // HD
+    features = gain1.shape[1]
+    tile = 256 if group % 256 == 0 else group
+    tiles = group // tile
+
+    def columns_of(weight):
+        return weight.at[:, pl.ds(pl.multiple_of(x * local, local), local)]
+
+    loads = [
+        pltpu.make_async_copy(
+            columns_of(w), qkv_w.at[:, pl.ds(i * local, local)], load_sem.at[i]
+        )
+        for i, w in enumerate((w_key, w_value, w_query))
+    ]
+    loads.append(pltpu.make_async_copy(columns_of(w_out), out_w, load_sem.at[3]))
+
+    def gather_of(d):
+        return Gather(at, x_all.at[d], rows, width, gather_send, gather_recv, (d,))
+
+    og_gather = Gather(at, og_all, rows, width, gather_send, gather_recv, (count,))
+    branch_gather = Gather(at, branch, rows, width, gather_send, gather_recv, (count + 1,))
+
+    def own_block(d):
+        return gather_of(d).block(x, y, c)
+
+    def line_copy(d):
+        return remote(own_block(d), own_block(d + 1), line_send, line_recv, (d,), z=z + 1)
+
+    weight_sems = (w_local, w_xs, w_xr, w_us, w_ds, w_rs)
+    down = Weights(at, 0, w_down, down_all, weight_sems)
+    up = Weights(at, 1, w_up, up_all, weight_sems)
+
+    own_x = pltpu.make_async_copy(xs, own_block(0), load_sem.at[4])
+    own_og = pltpu.make_async_copy(og, og_gather.block(x, y, c), load_sem.at[5])
+    own_x.start()
+    down.own().start()
+    up.own().start()
+    own_og.start()
+    for load in loads:
+        load.start()
+    at.meet()
+    own_x.wait()
+
+    @pl.when(z < count - 1)
+    def _():
+        line_copy(0).start()
+
+    gather_of(0).start()
+    down.first(True)
+    gather_of(0).middle()
+    down.swap().start()
+    for load in loads:
+        load.wait()
+
+    def project(d, with_query):
+        size = qkv_w.shape[1] if with_query else 2 * local
+
+        def step(x_ref, in_ref, kv_ref, *maybe_query):
+            normed, _ = normed_rows(x_ref[...].astype(F32))
+            rounded = (normed * gain1[...]).astype(BF16)
+            in_ref[...] = rounded
+            product = jnp.dot(rounded, qkv_w[:, :size], preferred_element_type=F32)
+            kv_ref[...] = product[:, : 2 * local].astype(BF16)
+            if with_query:
+                maybe_query[0][...] = product[:, 2 * local :].astype(BF16)
+
+        def rows_of(size):
+            return pl.BlockSpec((tile, size), lambda i: (i, 0))
+
+        outs = [rows_of(features), rows_of(2 * local)] + ([rows_of(local)] if with_query else [])
+        refs = [in_all.at[d], kv_all.at[d]] + ([query_out] if with_query else [])
+        pltpu.emit_pipeline(step, grid=(tiles,), in_specs=[rows_of(features)], out_specs=outs)(
+            x_all.at[d], *refs
+        )
+
+    def attend(d, diagonal):
+        keys = key_place[z - d]
+
+        @pl.loop(0, tiles)
+        def _(i):
+            part = pl.ds(pl.multiple_of(i * tile, tile), tile)
+            allowed = keys >= start_of[part, :]
+            if diagonal:
+                query_at = lax.broadcasted_iota(jnp.int32, (tile, group), 0) + i * tile
+                key_at = lax.broadcasted_iota(jnp.int32, (tile, group), 1)
+                allowed = (allowed & (key_at <= query_at)) | (key_at == query_at)
+            for h in range(heads):
+                span = slice(h * HD, (h + 1) * HD)
+                scores = contract(query[part, span], kv[:, span], ((1,), (1,)))
+                scores = jnp.where(allowed, scores * (HD**-0.5 * LOG2E), -1e30)
+                top = jnp.max(scores, axis=1, keepdims=True)
+                if not diagonal:
+                    old = high[h, part, :1]
+                    top = jnp.maximum(old, top)
+                    fade = jnp.exp2(old - top)
+                weights = jnp.exp2(scores - top)
+                mass = jnp.sum(weights, axis=1, keepdims=True)
+                value = jnp.dot(
+                    weights.astype(BF16),
+                    kv[:, local + h * HD : local + (h + 1) * HD],
+                    preferred_element_type=F32,
+                )
+                if not diagonal:
+                    mass = mass + total[h, part, :1] * fade
+                    value = value + sums[part, span] * fade
+                high[h, part, :] = jnp.broadcast_to(top, (tile, HD))
+                total[h, part, :] = jnp.broadcast_to(mass, (tile, HD))
+                sums[part, span] = value
+
+    def piece(d, diagonal):
+        project(d, diagonal)
+        pltpu.sync_copy(kv_all.at[d], kv)
+        if diagonal:
+            pltpu.sync_copy(query_out, query)
+        attend(d, diagonal)
+
+    halves = [(up, True), (down, False), (up, False)]
+
+    def send_half(step):
+        weight, mine = halves[step]
+        weight.first(mine)
+        if step == 0:
+            up.swap().start()
+
+    def bring(d):
+        @pl.when(z >= d)
+        def _():
+            remote(own_block(d - 1), own_block(d), line_send, line_recv, (d - 1,), z=z).wait_recv()
+
+            @pl.when((d < count - 1) & (z < count - 1))
+            def _():
+                line_copy(d).start()
+
+            gather_of(d).start()
+
+    def within(d, *names):
+        @pl.when(z >= d)
+        def _():
+            for name in names:
+                getattr(gather_of(d), name)()
+
+    hops = [
+        (weight, distance, mine)
+        for distance in range(1, count)
+        for weight, mine in ((down, True), (up, True), (down, False), (up, False))
+    ]
+
+    def hop(many=1):
+        for _ in range(min(many, len(hops))):
+            weight, distance, mine = hops.pop(0)
+            weight.hop(distance, mine)
+
+    gather_of(0).corner()
+    gather_of(0).end()
+    bring(1)
+    send_half(0)
+    piece(0, True)
+    within(1, "middle")
+
+    @pl.loop(2, count)
+    def _(d):
+        within(d - 1, "corner", "end")
+        bring(d)
+        for step in (1, 2):
+
+            @pl.when(d == step + 1)
+            def _():
+                send_half(step)
+
+        @pl.when(z >= d - 1)
+        def _():
+            piece(d - 1, False)
+
+        within(d, "middle")
+
+    for step in range(max(count - 1, 1), 3):
+        send_half(step)
+    hop(2)
+    within(count - 1, "corner", "end")
+    own_og.wait()
+    og_gather.start()
+
+    @pl.when(z >= count - 1)
+    def _():
+        piece(count - 1, False)
+
+    hop()
+    og_gather.middle()
+
+    @pl.loop(0, tiles)
+    def _(i):
+        part = pl.ds(pl.multiple_of(i * tile, tile), tile)
+        for h in range(heads):
+            span = slice(h * HD, (h + 1) * HD)
+            mass = total[h, part, :]
+            attended[part, span] = (sums[part, span] / mass).astype(BF16)
+            high[h, part, :] = high[h, part, :] + jnp.log2(mass)
+        partial[part, :] = contract(attended[part, :], out_w[...], ((1,), (1,))).astype(BF16)
+
+    outs = [
+        pltpu.make_async_copy(attended, attended_out, load_sem.at[6]),
+        pltpu.make_async_copy(high, log_out, load_sem.at[7]),
+    ]
+    for out in outs:
+        out.start()
+    hop()
+    og_gather.corner()
+    reduce = Reduce(
+        at, partial, rows, width, (twin, corner_x, corner_y, from_x, from_y), reduce_send, reduce_recv
+    )
+    reduce.start()
+    og_gather.end()
+    reduce.twins()
+    hop()
+    reduce.corners()
+    hop()
+    own_branch = branch_gather.block(x, y, c)
+
+    def store(part, value):
+        own_branch[part, :] = value.astype(BF16)
+
+    reduce.end(store)
+    branch_gather.start()
+    hop()
+    branch_gather.middle()
+    hop()
+    branch_gather.corner()
+    hop()
+    branch_gather.end()
+    pltpu.sync_copy(branch, branch_out)
+
+    def second_norm(x_ref, branch_ref, mlp_ref):
+        normed, _ = normed_rows(x_ref[...].astype(F32) + branch_ref[...].astype(F32))
+        mlp_ref[...] = (normed * gain2[...]).astype(BF16)
+
+    spec = pl.BlockSpec((tile, features), lambda i: (i, 0))
+    pltpu.emit_pipeline(second_norm, grid=(tiles,), in_specs=[spec, spec], out_specs=[spec])(
+        x_all.at[0], branch_out, mlp_out
+    )
+    hop(len(hops))
+
+    for out in outs:
+        out.wait()
+    down.drain()
+    up.drain()
+    reduce.drain()
+    branch_gather.drain()
+    og_gather.drain()
+
+    @pl.loop(0, count)
+    def _(d):
+        within(d, "drain")
+
+        @pl.when((z >= d) & (d < count - 1) & (z < count - 1))
+        def _():
+            line_copy(d).wait_send()
+
+
+def front(count, xs, og, w_query, w_key, w_value, w_out, w_up, w_down, gain1, gain2, start_of, key_place):
+    rows, width = xs.shape
+    group, features = 2 * rows, gain1.shape[1]
+    local = w_query.shape[1] // 2
+    heads = local // HD
+    hidden = w_up.shape[1] // 2
+    w_rows = w_up.shape[0]
+    hbm, vmem = pl.BlockSpec(memory_space=pl.ANY), pl.BlockSpec(memory_space=pltpu.VMEM)
+
+    def out(*shape, dtype=BF16):
+        return jax.ShapeDtypeStruct(shape, dtype)
+
+    dma = pltpu.SemaphoreType.DMA
+    return pl.pallas_call(
+        functools.partial(front_kernel, count),
+        name="front",
+        out_shape=(
+            out(count, group, features),
+            out(count, group, features),
+            out(count, group, 2 * local),
+            out(group, local),
+            out(group, local),
+            out(heads, group, HD, dtype=F32),
+            out(group, features),
+            out(group, features),
+            out(group, features),
+            out(count, 2, w_rows, hidden),
+            out(count, 2, w_rows, hidden),
+        ),
+        in_specs=[hbm] * 8 + [vmem] * 4,
+        out_specs=[hbm] * 11,
+        scratch_shapes=[
+            pltpu.VMEM((features, 3 * local), BF16),
+            pltpu.VMEM((features, local), BF16),
+            pltpu.VMEM((group, local), BF16),
+            pltpu.VMEM((group, 2 * local), BF16),
+            pltpu.VMEM((heads, group, HD), F32),
+            pltpu.VMEM((heads, group, HD), F32),
+            pltpu.VMEM((group, local), F32),
+            pltpu.VMEM((group, local), BF16),
+            pltpu.VMEM((group, features), BF16),
+            pltpu.VMEM((group, features), BF16),
+            *reduce_scratch(rows, width),
+            dma((8,)),
+            dma((count + 2, 9)),
+            dma((count + 2, 9)),
+            dma((count,)),
+            dma((count,)),
+            dma((2,)),
+            dma((2,)),
+            dma((2,)),
+            dma((2, count, 2)),
+            dma((2, count, 2)),
+            dma((2, count, 2)),
+            dma((10,)),
+            dma((10,)),
+        ],
+        compiler_params=pltpu.CompilerParams(
+            collective_id=0, has_side_effects=True, vmem_limit_bytes=56 * 1024 * 1024
+        ),
+    )(xs, og, w_query, w_key, w_value, w_out, w_up, w_down, gain1, gain2, start_of, key_place)
 
 
 def shifted(block, axis, step, first, last):
@@ -104,85 +777,40 @@
         size = weight.shape[1] // 2
         return lax.dynamic_slice_in_dim(weight, which * size, size, 1)
 
-    def layer_rows(weight):
-        other = swapped(half(weight, 1 - x), "x")
-        own = half(weight, x)
-        return jnp.where(
-            x == 0, jnp.concatenate([own, other], 0), jnp.concatenate([other, own], 0)
-        )
-
-    down_full = line_whole(layer_rows(w_down), count, z)
-    up_full = line_whole(layer_rows(w_up), count, z)
-
-    whole_input = layer_gather(layer_input)
-    grad_out = layer_gather(out_grad)
-
-    wide = whole_input.astype(F32)
+    clip_ends = jnp.cumsum(clip_lengths)
+    position = jnp.arange(key_padding.shape[0], dtype=jnp.int32)
+    starts = jnp.max(jnp.where(position[:, None] >= clip_ends, clip_ends, 0), axis=1)
+    key_place = jnp.where(key_padding > 0, position, -1).reshape(count, 1, rows)
+    start_of = lax.dynamic_slice_in_dim(starts, z * rows, rows)[:, None]
+    (x_all, in_all, kv_all, query, attended, log_sum, branch, mlp_in, grad_out, down_full, up_full) = front(
+        count, layer_input, out_grad, w_query, w_key, w_value, w_out, w_up, w_down,
+        norm1_gain[None], norm2_gain[None], start_of, key_place,
+    )
+    down_full = down_full.reshape(width, hidden)
+    up_full = up_full.reshape(width, hidden)
+    attn_in = in_all[0]
+    below = [kv_all[d] for d in range(1, count)]
+    own_kv = kv_all[0]
+    log_sum = log_sum[:, :, :1]
+    query_w, key_w, value_w, out_w = (half(w, x) for w in (w_query, w_key, w_value, w_out))
+    wide = x_all[0].astype(F32)
+    normed1_all, inverse1 = normed_rows(wide)
     mean1 = jnp.mean(wide, axis=1, keepdims=True)
-    centred = wide - mean1
-    inverse1 = lax.rsqrt(jnp.mean(centred * centred, axis=1, keepdims=True) + NORM_EPS)
-    attn_in = (centred * inverse1 * norm1_gain).astype(BF16)
-
-    query_w, key_w, value_w, out_w = (half(w, x) for w in (w_query, w_key, w_value, w_out))
-    query = jnp.dot(attn_in, query_w, preferred_element_type=F32).astype(BF16)
-    key = jnp.dot(attn_in, key_w, preferred_element_type=F32).astype(BF16)
-    value = jnp.dot(attn_in, value_w, preferred_element_type=F32).astype(BF16)
-    own_kv = jnp.concatenate([key, value], axis=1)
-    below = line_gather_up(own_kv, count)
-
-    clip_ends = jnp.cumsum(clip_lengths)
-
-    def clip_of(positions):
-        return jnp.sum((positions[:, None] >= clip_ends[None, :]).astype(jnp.int32), axis=1)
-
-    query_pos = z * rows + jnp.arange(rows, dtype=jnp.int32)
-    query_clip = clip_of(query_pos)
-
-    def visible(first_key, key_rows):
-        key_pos = first_key + jnp.arange(key_rows, dtype=jnp.int32)
-        keep = key_padding[jnp.clip(key_pos, 0, key_padding.shape[0] - 1)] > 0
-        same = (query_clip[:, None] == clip_of(key_pos)[None, :]) & (key_pos >= 0)[None, :]
-        causal = key_pos[None, :] <= query_pos[:, None]
-        return same & causal & (keep[None, :] | (key_pos[None, :] == query_pos[:, None]))
+    normed2_all, inverse2_all = normed_rows(wide + branch.astype(F32))
 
     def split(block):
         return block.reshape(block.shape[0], heads, HD)
 
     query_heads = split(query)
-    all_kv = jnp.concatenate(below[::-1] + [own_kv], axis=0)
-    allowed = visible((z - count + 1) * rows, count * rows)
-    scores = (
-        jnp.einsum("qhd,khd->hqk", query_heads, split(all_kv[:, :local]), preferred_element_type=F32)
-        * scale
-    )
-    scores = jnp.where(allowed[None], scores, -1e30)
-    high = jnp.max(scores, axis=2, keepdims=True)
-    weights = jnp.where(allowed[None], jnp.exp(scores - high), 0.0)
-    total = jnp.sum(weights, axis=2, keepdims=True)
-    attn_heads = (
-        jnp.einsum(
-            "hqk,khd->hqd", weights.astype(BF16), split(all_kv[:, local:]), preferred_element_type=F32
-        )
-        / total
-    )
-    log_sum = high + jnp.log(total)
-    attended = jnp.transpose(attn_heads, (1, 0, 2)).reshape(rows, local).astype(BF16)
-    attn_part = jnp.einsum("tf,df->td", attended, out_w, preferred_element_type=F32).astype(BF16)
-    resid = layer_input.astype(F32) + layer_reduce(attn_part).astype(F32)
-
-    mean_own = jnp.mean(resid, axis=1, keepdims=True)
-    spread_own = jnp.sum((resid - mean_own) ** 2, axis=1, keepdims=True)
-    parts = lax.all_gather(
-        jnp.concatenate([mean_own, spread_own], axis=1), ("y", "core"), axis=0, tiled=False
-    )
-    mean2 = jnp.mean(parts[:, :, 0], axis=0)[:, None]
-    var2 = (
-        jnp.sum(parts[:, :, 1], axis=0)[:, None]
-        + share_width * jnp.sum((parts[:, :, 0] - mean2[:, 0]) ** 2, axis=0)[:, None]
-    ) / width
-    inverse2 = lax.rsqrt(var2 + NORM_EPS)
-    normed2 = (resid - mean2) * inverse2
-    mlp_in = layer_gather((normed2 * gain2_share).astype(BF16))
+
+    def share_of(array):
+        return lax.dynamic_slice_in_dim(array, x * share_rows, share_rows, 0)
+
+    def block_of(array):
+        return lax.dynamic_slice_in_dim(share_of(array), column * share_width, share_width, 1)
+
+    resid = layer_input.astype(F32) + block_of(branch).astype(F32)
+    normed2, inverse2 = block_of(normed2_all), share_of(inverse2_all)
 
     grad_act = jnp.dot(grad_out, down_full, preferred_element_type=F32)
     up_f = jnp.dot(mlp_in, up_full, preferred_element_type=F32)
@@ -224,13 +852,17 @@
     out_weight_part = jnp.einsum("td,tf->df", grad_branch, attended, preferred_element_type=F32)
     grad_attended = jnp.dot(grad_branch, out_w, preferred_element_type=F32).astype(BF16)
     grad_heads = split(grad_attended)
-    delta = jnp.einsum("thd,htd->ht", grad_heads.astype(F32), attn_heads)
+    delta = jnp.einsum("thd,thd->ht", grad_heads.astype(F32), split(attended).astype(F32))
 
     def stage(kv, distance):
         keys, values = split(kv[:, :local]), split(kv[:, local:])
-        allowed = visible((z - distance) * rows, rows)
-        scores = jnp.einsum("qhd,khd->hqk", query_heads, keys, preferred_element_type=F32) * scale
-        probs = jnp.where(allowed[None], jnp.exp(scores - log_sum), 0.0)
+        places = key_place[jnp.maximum(z - distance, 0)]
+        allowed = (places >= start_of) & (z >= distance)
+        if distance == 0:
+            at = jnp.arange(rows)
+            allowed = (allowed & (at[None, :] <= at[:, None])) | (at[None, :] == at[:, None])
+        scores = jnp.einsum("qhd,khd->hqk", query_heads, keys, preferred_element_type=F32) * (scale * LOG2E)
+        probs = jnp.where(allowed[None], jnp.exp2(scores - log_sum), 0.0)
         grad_probs = jnp.einsum("qhd,khd->hqk", grad_heads, values, preferred_element_type=F32)
         grad_scores = (probs * (grad_probs - delta[:, :, None]) * scale).astype(BF16)
         grad_query = jnp.einsum("hqk,khd->qhd", grad_scores, keys, preferred_element_type=F32)
@@ -276,9 +908,6 @@
     query_grad = both_halves(qkv_grad[:, :local])
     key_grad = both_halves(qkv_grad[:, local : 2 * local])
     value_grad = both_halves(qkv_grad[:, 2 * local :])
-
-    def share_of(stat):
-        return lax.dynamic_slice_in_dim(stat, x * share_rows, share_rows, 0)
 
     mean1_share, inverse1_share = share_of(mean1), share_of(inverse1)
     normed1 = (layer_input.astype(F32) - mean1_share) * inverse1_share

time: 1370 us -> 1050 us (0.77)
  waiting for transfers between devices: 697 us -> 355 us
  Pallas kernels: 0 us -> 204 us
  local copies, waits for them, and re-layouts: 118 us -> 55.3 us
  other arithmetic: 137 us -> 96.9 us
  matrix products: 167 us -> 127 us
  starting transfers between devices: 191 us -> 156 us
    pallas_call x0 -> x1, Pallas kernels: none -> 204 us  [front(): pl.pallas_call(functools.partial(front_kernel, count), name='front', out_...]
    ppermute x54 -> x39, waiting for transfers between devices: 322 us -> 195 us  [shifted(): lax.ppermute(block, axis, [(i, i + step) for i in range(first, last + 1)])]
    all_gather x4 -> x1, waiting for transfers between devices: 80 us -> 17.3 us  [layer_gather(): return lax.all_gather(wide, 'x', axis=0, tiled=True)]
    reduce_scatter x4 -> x3, waiting for transfers between devices: 129 us -> 67.1 us  [layer_reduce(): tall = lax.psum_scatter(partial, 'x', scatter_dimension=0, tiled=True)]
    reduce_scatter x4 -> x3, waiting for transfers between devices: 66.6 us -> 18.1 us  [layer_reduce(): lax.psum_scatter(tall, ('y', 'core'), scatter_dimension=1, tiled=True)]
    gather x5 -> x0, local copies, waits for them, and re-layouts: 47.6 us -> none  [visible(): keep = key_padding[jnp.clip(key_pos, 0, key_padding.shape[0] - 1)] > 0]
    dot_general x6 -> x0, matrix products: 41.1 us -> none  [the longest x1 17.6 us: body(): jnp.einsum('qhd,khd->hqk', query_heads, split(all_kv[:, :local]), preferr...]
    ppermute x54 -> x39, starting transfers between devices: 181 us -> 149 us  [shifted(): lax.ppermute(block, axis, [(i, i + step) for i in range(first, last + 1)])]
  transfers between devices with their start and end apart: 78 -> 53, of which waited for: 33 -> 20; matrix products, arithmetic and copies ran while one was open for 20% -> 19% of each run, Pallas kernels for 0% -> 0%
where the time goes in v2:
time: 1050 us
  waiting for transfers between devices  355 us (34%)
  Pallas kernels  204 us (19%)
  starting transfers between devices  156 us (15%)
  matrix products  127 us (12%)
  other arithmetic  96.9 us (9%)
  local copies, waits for them, and re-layouts  55.3 us (5%)
  blocking collectives  35.2 us (3%)
  between operations  15.9 us (2%)
    pallas_call x1, Pallas kernels, front(): pl.pallas_call(functools.partial(front_kernel, count), name='front', out_...  204 us
    ppermute x39, waiting for transfers between devices, shifted(): lax.ppermute(block, axis, [(i, i + step) for i in range(first, last + 1)])  195 us
    ppermute x39, starting transfers between devices, shifted(): lax.ppermute(block, axis, [(i, i + step) for i in range(first, last + 1)])  149 us
    reduce_scatter x3, waiting for transfers between devices, layer_reduce(): tall = lax.psum_scatter(partial, 'x', scatter_dimension=0, tiled=True)  67.1 us
    ppermute x6, waiting for transfers between devices, swapped(): return lax.ppermute(block, axis, [(0, 1), (1, 0)])  39.2 us
    unnamed x133, local copies, waits for them, and re-layouts  24 us
    convert_element_type x8, other arithmetic, line_reduce(): (own.astype(F32) + up.astype(F32)).astype(BF16)  22.1 us
  transfers between devices with their start and end apart: 53, of which 20 were waited for; matrix products, arithmetic and copies ran while one was open for 19% of the time, Pallas kernels for 0%

profile of v2, /device:TPU:0, one launch (start us, length us, event | category | flops | bytes accessed | tf_op | source)
XLA Modules:
  0.0 1045.6 jit_solution(5100264947559831919)
XLA Ops:
  10.5 204.3 %front.1 = (bf16[4,1024,2048]{2,1,0:T(8,128)(2,1)}, bf16[4,1024,2048]{2,1,0:T(8,128)(2,1)}, bf16[4,1024,512]{2,1,0:T(8,128)(2,1)}, bf16[1024,256]{1,0:T(8,128)(2...) custom-call(bf16[512,512]{1,0:T(8,128)(2,1)} %xs.1, ...), custom_call_target="tpu_custom_call" | custom-call | tf_op jit(solution)/shard_map/front/pallas_call | solution.py:636
  214.8 7.7 fusion.105
  222.5 8.2 fusion.16
  232.1 6.1 convolution_convert_fusion.3
  238.2 67.1 %reduce-scatter.11.cloned.1.call-done = bf16[512,2048]{1,0:T(8,128)(2,1)} async-done(((bf16[1024,2048]{1,0:T(8,128)(2,1)}), bf16[512,2048]{1,0:T(8,128)(2,1)}) %reduce-scatter.11.cloned.1.call-update) | async-done | bytes 2097168 | tf_op jit(solution)/shard_map/reduce_scatter | solution.py:745
  315.0 6.3 multiply_reduce_fusion
  321.4 18.1 %reduce-scatter.13.cloned.1.call-done = bf16[512,512]{1,0:T(8,128)(2,1)} async-done(((bf16[512,2048]{1,0:T(8,128)(2,1)}), bf16[512,512]{1,0:T(8,128)(2,1)}) %reduce-scatter.13.cloned.1.call-update) | async-done | bytes 524304 | tf_op jit(solution)/shard_map/reduce_scatter | solution.py:746
  342.3 5.7 psum.21
  356.7 18.7 %all-gather.3.cloned.1.call-done = bf16[512,2048]{1,0:T(8,128)(2,1)} async-done(((bf16[512,512]{1,0:T(8,128)(2,1)}), bf16[512,2048]{1,0:T(8,128)(2,1)}) %all-gather.3.cloned.1.call-update) | async-done | bytes 2097168 | tf_op jit(solution)/shard_map/all_gather | solution.py:740
  416.2 17.3 %all-gather.5.cloned.1.call-done = bf16[1024,2048]{1,0:T(8,128)(2,1)} async-done(((bf16[512,2048]{1,0:T(8,128)(2,1)}), bf16[1024,2048]{1,0:T(8,128)(2,1)}) %all-gather.5.cloned.1.call-update) | async-done | bytes 4194320 | tf_op jit(solution)/shard_map/all_gather | solution.py:741
  443.7 6.5 fusion.55
  450.3 6.3 multiply_convert_fusion.3
  498.0 43.0 %collective-permute-done.2 = bf16[1024,512]{0,1:T(8,128)(2,1)S(1)} collective-permute-done((bf16[1024,512]{0,1:T(8,128)(2,1)S(1)}, bf16[1024,512]{0,1:T(8,128)(2,1)S(1)}, u32[]{:S(2)}, u32[]{:S(2)}) %collective-permute-start.2) | collective-permute-done | bytes 1048608 | tf_op jit(solution)/shard_map/ppermute | solution.py:687
  547.7 10.3 convolution_convert_fusion.4
  558.1 8.6 convolution_convert_fusion.1
  584.4 5.9 fusion.34
  606.3 14.2 %collective-permute-done.31 = bf16[512,1024]{0,1:T(8,128)(2,1)} collective-permute-done((bf16[512,1024]{0,1:T(8,128)(2,1)}, bf16[512,1024]{0,1:T(8,128)(2,1)}, u32[]{:S(2)}, u32[]{:S(2)}) %collective-permute-start.31) | collective-permute-done | bytes 1048608 | tf_op jit(solution)/shard_map/ppermute | solution.py:687
  628.7 8.7 collective-permute-done.3
  649.6 10.3 collective-permute-done.39
  668.4 33.6 %collective-permute-done.18 = bf16[512,256]{1,0:T(8,128)(2,1)S(1)} collective-permute-done((bf16[512,256]{1,0:T(8,128)(2,1)}, bf16[512,256]{1,0:T(8,128)(2,1)S(1)}, u32[]{:S(2)}, u32[]{:S(2)}) %collective-permute-start.18) | collective-permute-done | bytes 262176 | tf_op jit(solution)/shard_map/ppermute | solution.py:687
  727.5 24.1 %collective-permute-start.5 = (bf16[512,768]{1,0:T(8,128)(2,1)}, bf16[512,768]{1,0:T(8,128)(2,1)S(1)}, u32[]{:S(2)}, u32[]{:S(2)}) collective-permute-start(bf16[512,768]{1,0:T(8,128)(2,1)} %get-tuple-element.89), channel_id=1, source_target_pairs={{0,8},{8,16},{16,24},{1,9},{9,17},{17,25},{2,10},{10,18},{18,26},{... | collective-permute-start | bytes 2359304 | tf_op jit(solution)/shard_map/ppermute | solution.py:687
  758.5 20.9 %collective-permute-start.20 = (bf16[512,256]{1,0:T(8,128)(2,1)S(1)}, bf16[512,256]{1,0:T(8,128)(2,1)S(1)}, u32[]{:S(2)}, u32[]{:S(2)}) collective-permute-start(bf16[512,256]{1,0:T(8,128)(2,1)S(1)} %get-tuple-element.97), channel_id=1, source_target_pairs={{0,8},{8,16},{16,24},{1,9},{9,17},{17,25},{2,10},{10,18},{18,26},{... | collective-permute-start | bytes 786440 | tf_op jit(solution)/shard_map/ppermute | solution.py:687
  795.2 23.2 %collective-permute-done.23 = bf16[512,256]{1,0:T(8,128)(2,1)S(1)} collective-permute-done((bf16[512,256]{1,0:T(8,128)(2,1)S(1)}, bf16[512,256]{1,0:T(8,128)(2,1)S(1)}, u32[]{:S(2)}, u32[]{:S(2)}) %collective-permute-start.23) | collective-permute-done | bytes 262176 | tf_op jit(solution)/shard_map/ppermute | solution.py:687
  818.3 24.9 %collective-permute-start.9 = (bf16[512,768]{1,0:T(8,128)(2,1)}, bf16[512,768]{1,0:T(8,128)(2,1)S(1)}, u32[]{:S(2)}, u32[]{:S(2)}) collective-permute-start(bf16[512,768]{1,0:T(8,128)(2,1)} %add_convert_fusion.10), channel_id=1, source_target_pairs={{0,8},{8,16},{16,24},{1,9},{9,17},{17,25},{2,10},{10,18},{18,26},{... | collective-permute-start | bytes 2359304 | tf_op jit(solution)/shard_map/ppermute | solution.py:687
  847.6 14.9 %collective-permute-done.24 = bf16[512,256]{1,0:T(8,128)(2,1)S(1)} collective-permute-done((bf16[512,256]{1,0:T(8,128)(2,1)S(1)}, bf16[512,256]{1,0:T(8,128)(2,1)S(1)}, u32[]{:S(2)}, u32[]{:S(2)}) %collective-permute-start.24) | collective-permute-done | bytes 262176 | tf_op jit(solution)/shard_map/ppermute | solution.py:687
  875.3 15.4 %collective-permute-done.28 = bf16[512,256]{1,0:T(8,128)(2,1)} collective-permute-done((bf16[512,256]{1,0:T(8,128)(2,1)S(1)}, bf16[512,256]{1,0:T(8,128)(2,1)}, u32[]{:S(2)}, u32[]{:S(2)}) %collective-permute-start.28) | collective-permute-done | bytes 262176 | tf_op jit(solution)/shard_map/ppermute | solution.py:687
  904.9 10.5 %collective-permute-done.13 = bf16[512,768]{1,0:T(8,128)(2,1)S(1)} collective-permute-done((bf16[512,768]{1,0:T(8,128)(2,1)}, bf16[512,768]{1,0:T(8,128)(2,1)S(1)}, u32[]{:S(2)}, u32[]{:S(2)}) %collective-permute-start.13) | collective-permute-done | bytes 786464 | tf_op jit(solution)/shard_map/ppermute | solution.py:687
  920.5 11.4 %collective-permute-done.14 = bf16[512,768]{1,0:T(8,128)(2,1)S(1)} collective-permute-done((bf16[512,768]{1,0:T(8,128)(2,1)S(1)}, bf16[512,768]{1,0:T(8,128)(2,1)S(1)}, u32[]{:S(2)}, u32[]{:S(2)}) %collective-permute-start.14) | collective-permute-done | bytes 786464 | tf_op jit(solution)/shard_map/ppermute | solution.py:687
  949.3 10.8 %collective-permute-done.15 = bf16[2048,256]{1,0:T(8,128)(2,1)} collective-permute-done((bf16[2048,256]{1,0:T(8,128)(2,1)}, bf16[2048,256]{1,0:T(8,128)(2,1)}, u32[]{:S(2)}, u32[]{:S(2)}) %collective-permute-start.15) | collective-permute-done | bytes 1048608 | tf_op jit(solution)/shard_map/ppermute | solution.py:691
  965.0 17.6 %collective-permute-done.16 = bf16[2048,256]{1,0:T(8,128)(2,1)} collective-permute-done((bf16[2048,256]{1,0:T(8,128)(2,1)}, bf16[2048,256]{1,0:T(8,128)(2,1)}, u32[]{:S(2)}, u32[]{:S(2)}) %collective-permute-start.16) | collective-permute-done | bytes 1048608 | tf_op jit(solution)/shard_map/ppermute | solution.py:691
  987.5 10.8 %collective-permute-done.17 = bf16[2048,256]{1,0:T(8,128)(2,1)} collective-permute-done((bf16[2048,256]{1,0:T(8,128)(2,1)}, bf16[2048,256]{1,0:T(8,128)(2,1)}, u32[]{:S(2)}, u32[]{:S(2)}) %collective-permute-start.17) | collective-permute-done | bytes 1048608 | tf_op jit(solution)/shard_map/ppermute | solution.py:691
  1004.8 18.6 %psum.23 = f32[2,512]{1,0:T(2,128)S(1)} all-reduce(f32[2,512]{1,0:T(2,128)S(1)} %pad_maximum_fusion.6), channel_id=1, replica_groups=mesh['z'=4,'x'=2,'y'=2,'core'=2] {'z','x'}, use_global_device_ids=true, to_apply=%region_20.21 | all-reduce | flops 1024 | bytes 8192 | tf_op jit(solution)/shard_map/psum | solution.py:917
  (330 shorter events, 319.9 us)
Async XLA Ops:
  7.2 298.2 %reduce-scatter.11.cloned.1.call-start = ((), (), s32[]{:S(2)}) async-start(), calls=%async_computation.8 | async-start | bytes 6291456 | tf_op jit(solution)/shard_map/reduce_scatter | solution.py:745
  238.2 101.3 %reduce-scatter.13.cloned.1.call-start = ((), (), s32[]{:S(2)}) async-start(), calls=%async_computation.9 | async-start | bytes 2621440 | tf_op jit(solution)/shard_map/reduce_scatter | solution.py:746
  305.4 70.0 %all-gather.3.cloned.1.call-start = ((), (), s32[]{:S(2)}) async-start(), calls=%async_computation.10 | async-start | bytes 2621440 | tf_op jit(solution)/shard_map/all_gather | solution.py:740
  351.6 82.0 %all-gather.5.cloned.1.call-start = ((), (), s32[]{:S(2)}) async-start(), calls=%async_computation.11 | async-start | bytes 6291456 | tf_op jit(solution)/shard_map/all_gather | solution.py:741
  375.4 274.1 %reduce-scatter.15.cloned.1.call-start = ((), (), s32[]{:S(2)}) async-start(), calls=%async_computation.12 | async-start | bytes 6291456 | tf_op jit(solution)/shard_map/reduce_scatter | solution.py:745
  493.3 47.7 %collective-permute-start.2 = (bf16[1024,512]{0,1:T(8,128)(2,1)S(1)}, bf16[1024,512]{0,1:T(8,128)(2,1)S(1)}, u32[]{:S(2)}, u32[]{:S(2)}) collective-permute-start(bf16[1024,512]{0,1:T(8,128)(2,1)S(1)} %fusion.43), channel_id=1, source_target_pairs={{8,0},{16,8},{24,16},{9,1},{17,9},{25,17},{10,2},{18,10},{26,18},{... | collective-permute-start | bytes 3145736 | tf_op jit(solution)/shard_map/ppermute | solution.py:687
  547.5 327.8 %reduce-scatter.7.cloned.1.call-start = ((), (), s32[]{:S(2)}) async-start(), calls=%async_computation.6 | async-start | bytes 6291456 | tf_op jit(solution)/shard_map/reduce_scatter | solution.py:745
  558.0 445.1 %reduce-scatter.17.cloned.1.call-start = ((), (), s32[]{:S(2)}) async-start(), calls=%async_computation.13 | async-start | bytes 2621440 | tf_op jit(solution)/shard_map/reduce_scatter | solution.py:746
  581.8 38.7 %collective-permute-start.31 = (bf16[512,1024]{0,1:T(8,128)(2,1)}, bf16[512,1024]{0,1:T(8,128)(2,1)}, u32[]{:S(2)}, u32[]{:S(2)}) collective-permute-start(bf16[512,1024]{0,1:T(8,128)(2,1)} %get-tuple-element.83), channel_id=1, source_target_pairs={{0,8},{1,9},{2,10},{3,11},{4,12},{5,13},{6,14},{7,15}} | collective-permute-start | bytes 3145736 | tf_op jit(solution)/shard_map/ppermute | solution.py:687
  591.6 45.7 %collective-permute-start.3 = (bf16[512,768]{1,0:T(8,128)(2,1)}, bf16[512,768]{1,0:T(8,128)(2,1)}, u32[]{:S(2)}, u32[]{:S(2)}) collective-permute-start(bf16[512,768]{1,0:T(8,128)(2,1)} %get-tuple-element.91), channel_id=1, source_target_pairs={{0,8},{1,9},{2,10},{3,11},{4,12},{5,13},{6,14},{7,15}} | collective-permute-start | bytes 2359304 | tf_op jit(solution)/shard_map/ppermute | solution.py:687
  593.8 47.3 %collective-permute-start.41 = (bf16[512,1024]{0,1:T(8,128)(2,1)}, bf16[512,1024]{0,1:T(8,128)(2,1)}, u32[]{:S(2)}, u32[]{:S(2)}) collective-permute-start(bf16[512,1024]{0,1:T(8,128)(2,1)} %get-tuple-element.80), channel_id=1, source_target_pairs={{24,16},{25,17},{26,18},{27,19},{28,20},{29,21},{30,22},{31,23}} | collective-permute-start | bytes 3145736 | tf_op jit(solution)/shard_map/ppermute | solution.py:687
  595.4 118.9 %collective-permute-start.34 = (bf16[512,1024]{0,1:T(8,128)(2,1)}, bf16[512,1024]{0,1:T(8,128)(2,1)}, u32[]{:S(2)}, u32[]{:S(2)}) collective-permute-start(bf16[512,1024]{0,1:T(8,128)(2,1)} %get-tuple-element.84), channel_id=1, source_target_pairs={{24,16},{25,17},{26,18},{27,19},{28,20},{29,21},{30,22},{31,23}} | collective-permute-start | bytes 3145736 | tf_op jit(solution)/shard_map/ppermute | solution.py:687
  601.3 58.6 %collective-permute-start.39 = (bf16[512,1024]{0,1:T(8,128)(2,1)}, bf16[512,1024]{0,1:T(8,128)(2,1)}, u32[]{:S(2)}, u32[]{:S(2)}) collective-permute-start(bf16[512,1024]{0,1:T(8,128)(2,1)} %add_convert_fusion.4), channel_id=1, source_target_pairs={{0,8},{8,16},{1,9},{9,17},{2,10},{10,18},{3,11},{11,19},{4,12},{12... | collective-permute-start | bytes 3145736 | tf_op jit(solution)/shard_map/ppermute | solution.py:687
  623.3 92.6 %collective-permute-start.32 = (bf16[512,1024]{0,1:T(8,128)(2,1)}, bf16[512,1024]{0,1:T(8,128)(2,1)}, u32[]{:S(2)}, u32[]{:S(2)}) collective-permute-start(bf16[512,1024]{0,1:T(8,128)(2,1)} %add_convert_fusion.9), channel_id=1, source_target_pairs={{0,8},{8,16},{1,9},{9,17},{2,10},{10,18},{3,11},{11,19},{4,12},{12... | collective-permute-start | bytes 3145736 | tf_op jit(solution)/shard_map/ppermute | solution.py:687
  637.4 68.0 %collective-permute-start.6 = (bf16[512,768]{1,0:T(8,128)(2,1)}, bf16[512,768]{1,0:T(8,128)(2,1)}, u32[]{:S(2)}, u32[]{:S(2)}) collective-permute-start(bf16[512,768]{1,0:T(8,128)(2,1)} %get-tuple-element.92), channel_id=1, source_target_pairs={{24,16},{25,17},{26,18},{27,19},{28,20},{29,21},{30,22},{31,23}} | collective-permute-start | bytes 2359304 | tf_op jit(solution)/shard_map/ppermute | solution.py:687
  641.1 65.6 %collective-permute-start.4 = (bf16[512,768]{1,0:T(8,128)(2,1)}, bf16[512,768]{1,0:T(8,128)(2,1)}, u32[]{:S(2)}, u32[]{:S(2)}) collective-permute-start(bf16[512,768]{1,0:T(8,128)(2,1)} %add_convert_fusion.14), channel_id=1, source_target_pairs={{0,8},{8,16},{1,9},{9,17},{2,10},{10,18},{3,11},{11,19},{4,12},{12... | collective-permute-start | bytes 2359304 | tf_op jit(solution)/shard_map/ppermute | solution.py:687
  649.5 385.4 %reduce-scatter.9.cloned.1.call-start = ((), (), s32[]{:S(2)}) async-start(), calls=%async_computation.7 | async-start | bytes 2621440 | tf_op jit(solution)/shard_map/reduce_scatter | solution.py:746
  659.8 42.2 %collective-permute-start.18 = (bf16[512,256]{1,0:T(8,128)(2,1)}, bf16[512,256]{1,0:T(8,128)(2,1)S(1)}, u32[]{:S(2)}, u32[]{:S(2)}) collective-permute-start(bf16[512,256]{1,0:T(8,128)(2,1)} %get-tuple-element.99), channel_id=1, source_target_pairs={{0,8},{1,9},{2,10},{3,11},{4,12},{5,13},{6,14},{7,15}} | collective-permute-start | bytes 786440 | tf_op jit(solution)/shard_map/ppermute | solution.py:687
  702.0 50.9 %collective-permute-start.42 = (bf16[512,1024]{0,1:T(8,128)(2,1)}, bf16[512,1024]{0,1:T(8,128)(2,1)}, u32[]{:S(2)}, u32[]{:S(2)}) collective-permute-start(bf16[512,1024]{0,1:T(8,128)(2,1)} %get-tuple-element.78), channel_id=1, source_target_pairs={{16,8},{24,16},{17,9},{25,17},{18,10},{26,18},{19,11},{27,19},{20,... | collective-permute-start | bytes 3145736 | tf_op jit(solution)/shard_map/ppermute | solution.py:687
  719.6 37.5 %collective-permute-start.35 = (bf16[512,1024]{0,1:T(8,128)(2,1)}, bf16[512,1024]{0,1:T(8,128)(2,1)}, u32[]{:S(2)}, u32[]{:S(2)}) collective-permute-start(bf16[512,1024]{0,1:T(8,128)(2,1)} %get-tuple-element.82), channel_id=1, source_target_pairs={{16,8},{24,16},{17,9},{25,17},{18,10},{26,18},{19,11},{27,19},{20,... | collective-permute-start | bytes 3145736 | tf_op jit(solution)/shard_map/ppermute | solution.py:687
  721.2 122.1 %collective-permute-start.40 = (bf16[512,1024]{0,1:T(8,128)(2,1)}, bf16[512,1024]{0,1:T(8,128)(2,1)}, u32[]{:S(2)}, u32[]{:S(2)}) collective-permute-start(bf16[512,1024]{0,1:T(8,128)(2,1)} %get-tuple-element.77), channel_id=1, source_target_pairs={{0,8},{8,16},{16,24},{1,9},{9,17},{17,25},{2,10},{10,18},{18,26},{... | collective-permute-start | bytes 3145736 | tf_op jit(solution)/shard_map/ppermute | solution.py:687
  727.5 63.9 %collective-permute-start.5 = (bf16[512,768]{1,0:T(8,128)(2,1)}, bf16[512,768]{1,0:T(8,128)(2,1)S(1)}, u32[]{:S(2)}, u32[]{:S(2)}) collective-permute-start(bf16[512,768]{1,0:T(8,128)(2,1)} %get-tuple-element.89), channel_id=1, source_target_pairs={{0,8},{8,16},{16,24},{1,9},{9,17},{17,25},{2,10},{10,18},{18,26},{... | collective-permute-start | bytes 2359304 | tf_op jit(solution)/shard_map/ppermute | solution.py:687
  752.9 39.7 %collective-permute-start.8 = (bf16[512,768]{1,0:T(8,128)(2,1)S(1)}, bf16[512,768]{1,0:T(8,128)(2,1)S(1)}, u32[]{:S(2)}, u32[]{:S(2)}) collective-permute-start(bf16[512,768]{1,0:T(8,128)(2,1)S(1)} %add_convert_fusion.11), channel_id=1, source_target_pairs={{8,0},{16,8},{24,16},{9,1},{17,9},{25,17},{10,2},{18,10},{26,18},{... | collective-permute-start | bytes 2359304 | tf_op jit(solution)/shard_map/ppermute | solution.py:687
  757.1 89.0 %collective-permute-start.43 = (bf16[512,1024]{0,1:T(8,128)(2,1)}, bf16[512,1024]{0,1:T(8,128)(2,1)}, u32[]{:S(2)}, u32[]{:S(2)}) collective-permute-start(bf16[512,1024]{0,1:T(8,128)(2,1)} %add_convert_fusion.1), channel_id=1, source_target_pairs={{8,0},{16,8},{24,16},{9,1},{17,9},{25,17},{10,2},{18,10},{26,18},{... | collective-permute-start | bytes 3145736 | tf_op jit(solution)/shard_map/ppermute | solution.py:687
  786.0 79.5 %collective-permute-start.33 = (bf16[512,1024]{0,1:T(8,128)(2,1)}, bf16[512,1024]{0,1:T(8,128)(2,1)}, u32[]{:S(2)}, u32[]{:S(2)}) collective-permute-start(bf16[512,1024]{0,1:T(8,128)(2,1)} %get-tuple-element.81), channel_id=1, source_target_pairs={{0,8},{8,16},{16,24},{1,9},{9,17},{17,25},{2,10},{10,18},{18,26},{... | collective-permute-start | bytes 3145736 | tf_op jit(solution)/shard_map/ppermute | solution.py:687
  791.4 78.0 %collective-permute-start.36 = (bf16[512,1024]{0,1:T(8,128)(2,1)}, bf16[512,1024]{0,1:T(8,128)(2,1)}, u32[]{:S(2)}, u32[]{:S(2)}) collective-permute-start(bf16[512,1024]{0,1:T(8,128)(2,1)} %add_convert_fusion.6), channel_id=1, source_target_pairs={{8,0},{16,8},{24,16},{9,1},{17,9},{25,17},{10,2},{18,10},{26,18},{... | collective-permute-start | bytes 3145736 | tf_op jit(solution)/shard_map/ppermute | solution.py:687
  818.3 48.5 %collective-permute-start.9 = (bf16[512,768]{1,0:T(8,128)(2,1)}, bf16[512,768]{1,0:T(8,128)(2,1)S(1)}, u32[]{:S(2)}, u32[]{:S(2)}) collective-permute-start(bf16[512,768]{1,0:T(8,128)(2,1)} %add_convert_fusion.10), channel_id=1, source_target_pairs={{0,8},{8,16},{16,24},{1,9},{9,17},{17,25},{2,10},{10,18},{18,26},{... | collective-permute-start | bytes 2359304 | tf_op jit(solution)/shard_map/ppermute | solution.py:687
  869.4 66.4 %collective-permute-start.44 = (bf16[256,1024]{0,1:T(8,128)(2,1)}, bf16[256,1024]{0,1:T(8,128)(2,1)}, u32[]{:S(2)}, u32[]{:S(2)}) collective-permute-start(bf16[256,1024]{0,1:T(8,128)(2,1)} %get-tuple-element.94), channel_id=1, source_target_pairs={{0,4},{4,0},{1,5},{5,1},{2,6},{6,2},{3,7},{7,3},{8,12},{12,8},{9,1... | collective-permute-start | bytes 1572872 | tf_op jit(solution)/shard_map/ppermute | solution.py:691
  890.7 48.2 %collective-permute-start.37 = (bf16[256,1024]{0,1:T(8,128)(2,1)}, bf16[256,1024]{0,1:T(8,128)(2,1)S(1)}, u32[]{:S(2)}, u32[]{:S(2)}) collective-permute-start(bf16[256,1024]{0,1:T(8,128)(2,1)} %get-tuple-element.96), channel_id=1, source_target_pairs={{0,4},{4,0},{1,5},{5,1},{2,6},{6,2},{3,7},{7,3},{8,12},{12,8},{9,1... | collective-permute-start | bytes 1572872 | tf_op jit(solution)/shard_map/ppermute | solution.py:691
  903.4 41.7 %collective-permute-start.30 = (bf16[2048,256]{1,0:T(8,128)(2,1)S(1)}, bf16[2048,256]{1,0:T(8,128)(2,1)}, u32[]{:S(2)}, u32[]{:S(2)}) collective-permute-start(bf16[2048,256]{1,0:T(8,128)(2,1)S(1)} %constant_dynamic-slice_fusion.9), channel_id=1, source_target_pairs={{0,4},{4,0},{1,5},{5,1},{2,6},{6,2},{3,7},{7,3},{8,12},{12,8},{9,1... | collective-permute-start | bytes 3145736 | tf_op jit(solution)/shard_map/ppermute | solution.py:691
  935.3 47.3 %collective-permute-start.16 = (bf16[2048,256]{1,0:T(8,128)(2,1)}, bf16[2048,256]{1,0:T(8,128)(2,1)}, u32[]{:S(2)}, u32[]{:S(2)}) collective-permute-start(bf16[2048,256]{1,0:T(8,128)(2,1)} %get-tuple-element.75), channel_id=1, source_target_pairs={{0,4},{4,0},{1,5},{5,1},{2,6},{6,2},{3,7},{7,3},{8,12},{12,8},{9,1... | collective-permute-start | bytes 3145736 | tf_op jit(solution)/shard_map/ppermute | solution.py:691
  937.4 60.9 %collective-permute-start.17 = (bf16[2048,256]{1,0:T(8,128)(2,1)}, bf16[2048,256]{1,0:T(8,128)(2,1)}, u32[]{:S(2)}, u32[]{:S(2)}) collective-permute-start(bf16[2048,256]{1,0:T(8,128)(2,1)} %get-tuple-element.74), channel_id=1, source_target_pairs={{0,4},{4,0},{1,5},{5,1},{2,6},{6,2},{3,7},{7,3},{8,12},{12,8},{9,1... | collective-permute-start | bytes 3145736 | tf_op jit(solution)/shard_map/ppermute | solution.py:691
  (79 other events, 1380.0 us)
Sparse Core Ops, SparseCore 0:
  238.3 66.9 reduce-scatter.10
  308.0 31.4 reduce-scatter.12
  351.7 23.6 all-gather.2
  376.8 56.7 all-gather.4
  547.6 54.3 reduce-scatter.14
  604.8 54.3 reduce-scatter.6
  661.7 31.4 reduce-scatter.16
  875.4 40.2 reduce-scatter.8

commit v3 on v2

--- a/solution.py
+++ b/solution.py
@@ -40,10 +40,20 @@
         self.x, self.y, self.c = lax.axis_index("x"), lax.axis_index("y"), lax.axis_index("core")
         self.ox, self.oy, self.oc = 1 - self.x, 1 - self.y, 1 - self.c
 
-    def meet(self):
+    def meet(self, whole_line=False):
         barrier = pltpu.get_barrier_semaphore()
         for device in ({"x": self.ox}, {"y": self.oy}, {"core": self.oc}):
             pl.semaphore_signal(barrier, inc=1, device_id=device, device_id_type=MESH)
+        if whole_line:
+            for step in range(1, self.count):
+                pl.semaphore_signal(
+                    barrier,
+                    inc=1,
+                    device_id={"z": lax.rem(self.z + step, self.count)},
+                    device_id_type=MESH,
+                )
+            pl.semaphore_wait(barrier, 3 + self.count - 1)
+            return
         above, below = self.z < self.count - 1, self.z > 0
         for there, step in ((above, 1), (below, -1)):
 
@@ -683,67 +693,755 @@
     )(xs, og, w_query, w_key, w_value, w_out, w_up, w_down, gain1, gain2, start_of, key_place)
 
 
-def shifted(block, axis, step, first, last):
-    return lax.ppermute(block, axis, [(i, i + step) for i in range(first, last + 1)])
-
-
-def swapped(block, axis):
-    return lax.ppermute(block, axis, [(0, 1), (1, 0)])
-
-
-def line_gather_up(block, count):
-    found, moving = [], block
-    for hop in range(1, count):
-        moving = shifted(moving, "z", 1, hop - 1, count - 2)
-        found.append(moving)
-    return found
-
-
-def line_gather_down(block, count):
-    found, moving = [], block
-    for hop in range(1, count):
-        moving = shifted(moving, "z", -1, 1, count - hop)
-        found.append(moving)
-    return found
-
-
-def line_whole(block, count, z):
-    up = line_gather_up(block, count)
-    down = line_gather_down(block, count)
-    rows = block.shape[0]
-    both = jnp.concatenate(up[::-1] + [block] + down, axis=0)
-    return lax.dynamic_slice_in_dim(both, (count - 1 - z) * rows, count * rows, 0)
-
-
-def line_reduce(partial, count, z):
-    rows = partial.shape[0] // count
-
-    def chunk(index):
-        index = jnp.clip(index, 0, count - 1)
-        return lax.dynamic_slice_in_dim(partial, index * rows, rows, 0)
-
-    up = down = None
-    for hop in range(1, count):
-        own = chunk(count - hop + z)
-        send = own if up is None else (own.astype(F32) + up.astype(F32)).astype(BF16)
-        up = shifted(send, "z", 1, 0, min(hop - 1, count - 2))
-        own = chunk(z - count + hop)
-        send = own if down is None else (own.astype(F32) + down.astype(F32)).astype(BF16)
-        down = shifted(send, "z", -1, max(count - hop, 1), count - 1)
-    total = chunk(z).astype(F32)
-    if up is not None:
-        total = total + up.astype(F32) + down.astype(F32)
-    return total
-
-
-def layer_gather(share):
-    wide = lax.all_gather(share, ("y", "core"), axis=1, tiled=True)
-    return lax.all_gather(wide, "x", axis=0, tiled=True)
-
-
-def layer_reduce(partial):
-    tall = lax.psum_scatter(partial, "x", scatter_dimension=0, tiled=True)
-    return lax.psum_scatter(tall, ("y", "core"), scatter_dimension=1, tiled=True)
+class LineSum:
+    def __init__(self, at, which, terms, landing, sums, sends, recvs):
+        self.at, self.which = at, which
+        self.terms, self.landing, self.sums = terms, landing, sums
+        self.sends, self.recvs = sends, recvs
+        self.rows = sums.shape[2]
+
+    def chunk(self, c):
+        return self.terms.at[self.which, pl.ds(pl.multiple_of(c * self.rows, self.rows), self.rows)]
+
+    def move(self, source, c, slot, step):
+        return pltpu.make_async_remote_copy(
+            src_ref=source,
+            dst_ref=self.landing.at[self.which, slot],
+            send_sem=self.sends.at[self.which, c],
+            recv_sem=self.recvs.at[self.which, slot],
+            device_id={"z": self.at.z + step},
+            device_id_type=MESH,
+        )
+
+    def landed(self, slot):
+        ref = self.landing.at[self.which, slot]
+        self.move(ref, 0, slot, 0).wait_recv()
+
+    def total(self, refs, out):
+        tile = min(256, self.rows)
+
+        def step(*tiles):
+            value = tiles[0][...].astype(F32)
+            for other in tiles[1:-1]:
+                value = value + other[...].astype(F32)
+            tiles[-1][...] = value.astype(BF16)
+
+        spec = pl.BlockSpec((tile, self.sums.shape[3]), lambda i: (i, 0))
+        pltpu.emit_pipeline(
+            step, grid=(self.rows // tile,), in_specs=[spec] * len(refs), out_specs=[spec]
+        )(*refs, out)
+
+    def hop(self, h):
+        at, n, z = self.at, self.at.count, self.at.z
+        for step, c, there, slot in (
+            (1, n - h + z, (z <= h - 1) & (z < n - 1), n - h + z),
+            (-1, z - n + h, (z >= n - h) & (z > 0), None),
+        ):
+            if slot is None:
+                slot = jnp.where(c == z - 1, n, c)
+            first = z == (0 if step > 0 else n - 1)
+
+            @pl.when(there & first)
+            def _():
+                self.move(self.chunk(c), c, slot, step).start()
+
+            @pl.when(there & jnp.logical_not(first))
+            def _():
+                self.landed(c)
+                self.total([self.chunk(c), self.landing.at[self.which, c]], self.sums.at[self.which, c])
+                self.move(self.sums.at[self.which, c], c, slot, step).start()
+
+    def final(self, out):
+        n, z = self.at.count, self.at.z
+        below, above = self.landing.at[self.which, z], self.landing.at[self.which, n]
+
+        @pl.when(z > 0)
+        def _():
+            self.landed(z)
+
+        @pl.when(z < n - 1)
+        def _():
+            self.landed(n)
+
+        @pl.when(z == 0)
+        def _():
+            self.total([self.chunk(z), above], out)
+
+        @pl.when(z == n - 1)
+        def _():
+            self.total([self.chunk(z), below], out)
+
+        @pl.when((z > 0) & (z < n - 1))
+        def _():
+            self.total([self.chunk(z), below, above], out)
+
+    def drain(self):
+        z = self.at.z
+
+        @pl.loop(0, self.at.count)
+        def _(c):
+            @pl.when(c != z)
+            def _():
+                self.move(self.chunk(c), c, 0, 0).wait_send()
+
+
+class Spread:
+    def __init__(self, at, whole, ups, downs, lines, sides, sidesr):
+        self.at, self.whole = at, whole
+        self.ups, self.downs, self.lines, self.sides, self.sidesr = ups, downs, lines, sides, sidesr
+
+    def move(self, layer, step):
+        ref = self.whole.at[layer, self.at.x]
+        sends = self.ups if step > 0 else self.downs
+        return remote(ref, ref, sends, self.lines, (layer,), z=self.at.z + step)
+
+    def side(self, layer, part):
+        ref = self.whole.at[layer, part]
+        return remote(ref, ref, self.sides, self.sidesr, (layer,), x=self.at.ox)
+
+    def first(self):
+        at = self.at
+
+        @pl.when(at.z < at.count - 1)
+        def _():
+            self.move(at.z, 1).start()
+
+        @pl.when(at.z > 0)
+        def _():
+            self.move(at.z, -1).start()
+
+        self.side(at.z, at.x).start()
+
+    def hop(self, distance):
+        at = self.at
+
+        @pl.when(at.z >= distance)
+        def _():
+            self.move(at.z - distance, 1).wait_recv()
+
+            @pl.when(at.z < at.count - 1)
+            def _():
+                self.move(at.z - distance, 1).start()
+
+            self.side(at.z - distance, at.x).start()
+
+        @pl.when(at.z + distance < at.count)
+        def _():
+            self.move(at.z + distance, -1).wait_recv()
+
+            @pl.when(at.z > 0)
+            def _():
+                self.move(at.z + distance, -1).start()
+
+            self.side(at.z + distance, at.x).start()
+
+    def end(self):
+        at = self.at
+
+        @pl.loop(0, at.count)
+        def _(layer):
+            self.side(layer, at.ox).wait_recv()
+            self.side(layer, at.x).wait_send()
+
+            @pl.when((layer <= at.z) & (at.z < at.count - 1))
+            def _():
+                self.move(layer, 1).wait_send()
+
+            @pl.when((layer >= at.z) & (at.z > 0))
+            def _():
+                self.move(layer, -1).wait_send()
+
+
+def back_kernel(
+    count,
+    x_all,
+    in_all,
+    kv_all,
+    query_in,
+    attended_in,
+    log_in,
+    branch_in,
+    mlp_in,
+    og_all,
+    down_all,
+    up_all,
+    w_query,
+    w_key,
+    w_value,
+    w_out,
+    gain1,
+    gain2,
+    start_row,
+    key_place,
+    output,
+    input_grad,
+    gains_out,
+    mlp_grads,
+    attn_grads,
+    terms,
+    landing,
+    sums,
+    mine,
+    grad_branch,
+    grad_resid,
+    kv_own,
+    kv_landing,
+    kv_sums,
+    partial,
+    partial2,
+    full1,
+    full3,
+    twin_a,
+    corner_xa,
+    corner_ya,
+    from_xa,
+    from_ya,
+    twin_b,
+    corner_xb,
+    corner_yb,
+    from_xb,
+    from_yb,
+    twin_c,
+    corner_xc,
+    corner_yc,
+    from_xc,
+    from_yc,
+    gains,
+    gains_landing,
+    load_sem,
+    reduce_send,
+    reduce_recv,
+    gather_send,
+    gather_recv,
+    sum_send,
+    sum_recv,
+    home_send,
+    home_recv,
+    spread_up,
+    spread_down,
+    spread_line,
+    spread_side,
+    spread_side_recv,
+    kv_send,
+    kv_recv,
+    gain_send,
+    gain_recv,
+):
+    at = Place(count)
+    z, x, y, c = at.z, at.x, at.y, at.c
+    group, features = mlp_in.shape
+    rows = group // 2
+    width = output.shape[1]
+    local = w_query.shape[1] // 2
+    heads = local // HD
+    hidden = down_all.shape[1]
+    tile = min(256, group)
+    tiles = group // tile
+    thin = min(128, group)
+    block = min(512, features)
+    blocks = features // block
+    own_column = pl.ds(pl.multiple_of((2 * y + c) * width, width), width)
+
+    def columns_of(weight):
+        return weight.at[:, pl.ds(pl.multiple_of(x * local, local), local)]
+
+    def rows_spec(size, many=None):
+        return pl.BlockSpec((many or tile, size), lambda i: (i, 0))
+
+    def column_spec(tall):
+        return pl.BlockSpec((tall, block), lambda i: (0, i))
+
+    def whole_spec(*shape):
+        return pl.BlockSpec(shape, lambda i: (0,) * len(shape))
+
+    def reduce_of(array, buffers, k):
+        return Reduce(at, array, rows, width, buffers, reduce_send.at[k], reduce_recv.at[k])
+
+    def gather_of(array, k):
+        return Gather(at, array, rows, width, gather_send, gather_recv, (k,))
+
+    first_sum = reduce_of(partial, (twin_a, corner_xa, corner_ya, from_xa, from_ya), 0)
+    out_sum = reduce_of(partial2, (twin_b, corner_xb, corner_yb, from_xb, from_yb), 1)
+    last_sum = reduce_of(partial, (twin_c, corner_xc, corner_yc, from_xc, from_yc), 2)
+    first_gather, last_gather = gather_of(full1, 0), gather_of(full3, 1)
+    down_line, up_line, attn_line = (
+        LineSum(at, k, terms, landing, sums, sum_send, sum_recv) for k in range(3)
+    )
+    spread = Spread(
+        at, attn_grads, spread_up, spread_down, spread_line, spread_side, spread_side_recv
+    )
+
+    def weight_terms(which, left, right, size, column):
+        def step(left_ref, right_ref, out_ref):
+            out_ref[...] = contract(left_ref[...], right_ref[...], ((0,), (0,))).astype(BF16)
+
+        pltpu.emit_pipeline(
+            step,
+            grid=(blocks,),
+            in_specs=[column_spec(group), whole_spec(group, size)],
+            out_specs=[pl.BlockSpec((block, size), lambda i: (i, column))],
+        )(left, right, terms.at[which])
+
+    def home(which):
+        line = (down_line, up_line)[which]
+        line.final(mine.at[which])
+        half = mine.shape[1] // 2
+        own = pltpu.make_async_copy(
+            mine.at[which, pl.ds(pl.multiple_of(x * half, half), half)],
+            mlp_grads.at[which, x],
+            load_sem.at[which],
+        )
+        own.start()
+        home_copy(which).start()
+        own.wait()
+
+    def home_copy(which, landing_part=False):
+        half = mine.shape[1] // 2
+        return remote(
+            mine.at[which, pl.ds(pl.multiple_of(at.ox * half, half), half)],
+            mlp_grads.at[which, at.ox if landing_part else x],
+            home_send,
+            home_recv,
+            (which,),
+            x=at.ox,
+        )
+
+    def store_into(gather):
+        def store(part, value):
+            gather.block(x, y, c)[part, :] = value.astype(BF16)
+
+        return store
+
+    at.meet(whole_line=True)
+
+    def feed_forward(active, grad_up, w_down, w_up):
+        loads = [
+            pltpu.make_async_copy(up_all, w_up, load_sem.at[0]),
+            pltpu.make_async_copy(down_all, w_down, load_sem.at[1]),
+        ]
+        for load in loads:
+            load.start()
+        for load in loads:
+            load.wait()
+
+        def step(mlp_ref, og_ref, active_ref, grad_ref):
+            up = jnp.dot(mlp_ref[...], w_up[...], preferred_element_type=F32)
+            grad = jnp.dot(og_ref[...], w_down[...], preferred_element_type=F32)
+            square = up * up
+            root = 0.7978845608028654
+            bend = jnp.tanh(up * (root + (root * 0.044715) * square))
+            half = 0.5 * (1.0 + bend)
+            slope = half + 0.5 * up * (1.0 - bend * bend) * (root + (3.0 * root * 0.044715) * square)
+            active_ref[...] = (up * half).astype(BF16)
+            grad_ref[...] = (grad * slope).astype(BF16)
+
+        pltpu.emit_pipeline(
+            step,
+            grid=(tiles,),
+            in_specs=[rows_spec(features)] * 2,
+            out_specs=[rows_spec(hidden)] * 2,
+        )(mlp_in, og_all, active, grad_up)
+        weight_terms(0, og_all, active, hidden, 0)
+        down_line.hop(1)
+        weight_terms(1, mlp_in, grad_up, hidden, 0)
+        up_line.hop(1)
+
+        @pl.loop(0, tiles)
+        def _(i):
+            part = pl.ds(pl.multiple_of(i * tile, tile), tile)
+            partial[part, :] = contract(grad_up[part, :], w_up[...], ((1,), (1,))).astype(BF16)
+
+        first_sum.start()
+
+        @pl.loop(0, tiles)
+        def _(i):
+            part = pl.ds(pl.multiple_of(i * tile, tile), tile)
+            partial2[part, :] = contract(active[part, :], w_down[...], ((1,), (1,))).astype(BF16)
+
+    pl.run_scoped(
+        feed_forward,
+        pltpu.VMEM((group, hidden), BF16),
+        pltpu.VMEM((group, hidden), BF16),
+        pltpu.VMEM((features, hidden), BF16),
+        pltpu.VMEM((features, hidden), BF16),
+    )
+    first_sum.twins()
+    first_sum.corners()
+    first_sum.end(store_into(first_gather))
+    first_gather.start()
+    down_line.hop(2)
+    first_gather.middle()
+    first_gather.corner()
+    first_gather.end()
+    out_sum.start()
+
+    def attention(
+        qkv_w, out_w, query, attended, kv, grad_att, grad_query, grad_kv, grad_kv_low, kv_weight,
+        logs, log_row, delta_row, wide, resid_x, resid_branch,
+    ):
+        loads = [
+            pltpu.make_async_copy(
+                columns_of(w), qkv_w.at[:, pl.ds(i * local, local)], load_sem.at[i]
+            )
+            for i, w in enumerate((w_key, w_value, w_query))
+        ]
+        loads += [
+            pltpu.make_async_copy(columns_of(w_out), out_w, load_sem.at[3]),
+            pltpu.make_async_copy(query_in, query, load_sem.at[4]),
+            pltpu.make_async_copy(attended_in, attended, load_sem.at[5]),
+            pltpu.make_async_copy(log_in, logs, load_sem.at[6]),
+        ]
+        for load in loads:
+            load.start()
+        for load in loads:
+            load.wait()
+        gains[...] = jnp.zeros_like(gains)
+
+        def second_back(x_ref, branch_ref, og_ref, grad_ref, low_ref, resid_ref, att_ref):
+            normed, inverse = normed_rows(x_ref[...].astype(F32) + branch_ref[...].astype(F32))
+            grad = grad_ref[...].astype(F32)
+            scaled = grad * gain2[...]
+            centre = jnp.mean(scaled, axis=1, keepdims=True)
+            slope = jnp.mean(scaled * normed, axis=1, keepdims=True)
+            gains[1:2, :] += jnp.sum(grad * normed, axis=0, keepdims=True)
+            total = og_ref[...].astype(F32) + inverse * (scaled - centre - normed * slope)
+            wide[...] = total
+            low = total.astype(BF16)
+            low_ref[...] = low
+            resid_ref[...] = wide[:, own_column]
+            att_ref[...] = jnp.dot(low, out_w[...], preferred_element_type=F32).astype(BF16)
+
+        thin_spec = rows_spec(features, thin)
+        pltpu.emit_pipeline(
+            second_back,
+            grid=(group // thin,),
+            in_specs=[thin_spec] * 4,
+            out_specs=[thin_spec, rows_spec(width, thin), rows_spec(local, thin)],
+        )(x_all.at[0], branch_in, og_all, full1, grad_branch, grad_resid, grad_att)
+        up_line.hop(2)
+        out_sum.twins()
+        weight_terms(2, grad_branch, attended, local, 3)
+        for h in range(heads):
+            span = slice(h * HD, (h + 1) * HD)
+            log_row[h] = jnp.transpose(logs[h])[:1]
+            product = grad_att[:, span].astype(F32) * attended[:, span].astype(F32)
+            delta_row[h] = jnp.sum(jnp.transpose(product), axis=0, keepdims=True)
+        grad_query[...] = jnp.zeros_like(grad_query)
+        kv_weight[...] = jnp.zeros_like(kv_weight)
+
+        def stage(layer, diagonal):
+            pltpu.sync_copy(kv_all.at[z - layer], kv)
+            grad_kv[...] = jnp.zeros_like(grad_kv)
+            keys = jnp.transpose(jnp.broadcast_to(key_place[layer], (HD, group)))[:, :1]
+
+            @pl.loop(0, tiles)
+            def _(i):
+                part = pl.ds(pl.multiple_of(i * tile, tile), tile)
+                allowed = keys >= start_row[:, part]
+                if diagonal:
+                    query_at = lax.broadcasted_iota(jnp.int32, (group, tile), 1) + i * tile
+                    key_at = lax.broadcasted_iota(jnp.int32, (group, tile), 0)
+                    allowed = (allowed & (key_at <= query_at)) | (key_at == query_at)
+                for h in range(heads):
+                    span = slice(h * HD, (h + 1) * HD)
+                    value_span = slice(local + h * HD, local + (h + 1) * HD)
+                    key, value = kv[:, span], kv[:, value_span]
+                    asked, grad = query[part, span], grad_att[part, span]
+                    scores = contract(key, asked, ((1,), (1,))) * (HD**-0.5 * LOG2E)
+                    probs = jnp.exp2(jnp.where(allowed, scores, -1e30) - log_row[h, :, part])
+                    grad_probs = contract(value, grad, ((1,), (1,)))
+                    grad_scores = (
+                        probs * (grad_probs - delta_row[h, :, part]) * HD**-0.5
+                    ).astype(BF16)
+                    grad_kv[:, value_span] += jnp.dot(
+                        probs.astype(BF16), grad, preferred_element_type=F32
+                    )
+                    grad_kv[:, span] += jnp.dot(grad_scores, asked, preferred_element_type=F32)
+                    grad_query[part, span] += contract(grad_scores, key, ((0,), (0,)))
+
+            grad_kv_low[...] = grad_kv[...].astype(BF16)
+
+            def add(in_ref, grad_ref, out_ref):
+                out_ref[...] += contract(in_ref[...], grad_ref[...], ((0,), (0,)))
+
+            pltpu.emit_pipeline(
+                add,
+                grid=(blocks,),
+                in_specs=[column_spec(group), whole_spec(group, 2 * local)],
+                out_specs=[pl.BlockSpec((block, 2 * local), lambda i: (i, 0))],
+            )(in_all.at[z - layer], grad_kv_low, kv_weight)
+
+        def kv_move(layer, source):
+            return remote(
+                source.at[layer], kv_landing.at[layer], kv_send, kv_recv, (layer,), z=z - 1
+            )
+
+        def finish_output():
+            own = pl.ds(pl.multiple_of(x * rows, rows), rows)
+            pltpu.sync_copy(x_all.at[0, own, own_column], resid_x)
+            pltpu.sync_copy(branch_in.at[own, own_column], resid_branch)
+
+            def store(part, value):
+                resid = resid_x[part, :].astype(F32) + resid_branch[part, :].astype(F32)
+                resid_x[part, :] = (resid + value).astype(BF16)
+
+            out_sum.end(store)
+            pltpu.sync_copy(resid_x, output)
+
+        events = [out_sum.corners, finish_output]
+        for h in range(3, count):
+            events += [functools.partial(down_line.hop, h), functools.partial(up_line.hop, h)]
+        share = -(-len(events) // count)
+
+        @pl.loop(0, count)
+        def _(layer):
+            @pl.when(layer < z)
+            def _():
+                stage(layer, False)
+                pltpu.sync_copy(grad_kv_low, kv_own.at[layer])
+
+                @pl.when(z == count - 1)
+                def _():
+                    kv_move(layer, kv_own).start()
+
+            @pl.when(layer == z)
+            def _():
+                stage(layer, True)
+
+            for k in range(count):
+                batch = events[k * share : (k + 1) * share]
+                if batch:
+
+                    @pl.when(layer == k)
+                    def _():
+                        for event in batch:
+                            event()
+
+        grad_kv_low[:, :local] = grad_query[...].astype(BF16)
+
+        def query_terms(in_ref, grad_ref, kv_ref, kv_out, query_out):
+            kv_out[...] = kv_ref[...].astype(BF16)
+            query_out[...] = contract(in_ref[...], grad_ref[:, :local], ((0,), (0,))).astype(BF16)
+
+        pltpu.emit_pipeline(
+            query_terms,
+            grid=(blocks,),
+            in_specs=[
+                column_spec(group),
+                whole_spec(group, 2 * local),
+                pl.BlockSpec((block, 2 * local), lambda i: (i, 0)),
+            ],
+            out_specs=[
+                pl.BlockSpec((block, 2 * local), lambda i: (i, 0)),
+                pl.BlockSpec((block, local), lambda i: (i, 2)),
+            ],
+        )(in_all.at[0], grad_kv_low, kv_weight, terms.at[2], terms.at[2])
+        attn_line.hop(1)
+
+        def kv_line(layer):
+            @pl.when((layer < z) & (z < count - 1))
+            def _():
+                kv_move(layer, kv_own).wait_recv()
+                add_rows(kv_own.at[layer], kv_landing.at[layer], kv_sums.at[layer])
+                kv_move(layer, kv_sums).start()
+
+        def add_rows(left, right, out):
+            def step(left_ref, right_ref, out_ref):
+                out_ref[...] = (left_ref[...].astype(F32) + right_ref[...].astype(F32)).astype(BF16)
+
+            pltpu.emit_pipeline(
+                step,
+                grid=(tiles,),
+                in_specs=[rows_spec(2 * local)] * 2,
+                out_specs=[rows_spec(2 * local)],
+            )(left, right, out)
+
+        home(0)
+        for h in range(2, count):
+            kv_line(h - 2)
+            attn_line.hop(h)
+            if h == 2:
+                home(1)
+        kv_line(count - 2)
+        first_sum.drain()
+
+        @pl.when(z < count - 1)
+        def _():
+            kv_move(z, kv_own).wait_recv()
+            pltpu.sync_copy(kv_landing.at[z], kv)
+
+        @pl.loop(0, tiles)
+        def _(i):
+            part = pl.ds(pl.multiple_of(i * tile, tile), tile)
+
+            @pl.when(z < count - 1)
+            def _():
+                grad_kv[part, :] += kv[part, :].astype(F32)
+
+            partial[part, :] = (
+                contract(grad_kv[part, :].astype(BF16), qkv_w[:, : 2 * local], ((1,), (1,)))
+                + contract(grad_query[part, :].astype(BF16), qkv_w[:, 2 * local :], ((1,), (1,)))
+            ).astype(BF16)
+
+        last_sum.start()
+        last_sum.twins()
+        attn_line.final(attn_grads.at[z, x])
+        spread.first()
+        last_sum.corners()
+        last_sum.end(store_into(last_gather))
+        last_gather.start()
+        last_gather.middle()
+        spread.hop(1)
+        last_gather.corner()
+        last_gather.end()
+
+        def first_back(x_ref, grad_ref, resid_ref, out_ref):
+            normed, inverse = normed_rows(x_ref[...].astype(F32))
+            grad = grad_ref[...].astype(F32)
+            scaled = grad * gain1[...]
+            centre = jnp.mean(scaled, axis=1, keepdims=True)
+            slope = jnp.mean(scaled * normed, axis=1, keepdims=True)
+            gains[0:1, :] += jnp.sum(grad * normed, axis=0, keepdims=True)
+            wide[...] = inverse * (scaled - centre - normed * slope)
+            out_ref[...] = resid_ref[...] + wide[:, own_column]
+
+        pltpu.emit_pipeline(
+            first_back,
+            grid=(group // thin,),
+            in_specs=[thin_spec, thin_spec, rows_spec(width, thin)],
+            out_specs=[rows_spec(width, thin)],
+        )(x_all.at[0], full3, grad_resid, input_grad)
+
+        def gain_copy(step):
+            to = lax.rem(z + step, count)
+            return pltpu.make_async_remote_copy(
+                src_ref=gains,
+                dst_ref=gains_landing.at[z],
+                send_sem=gain_send.at[step],
+                recv_sem=gain_recv.at[z],
+                device_id={"z": to},
+                device_id_type=MESH,
+            )
+
+        for step in range(1, count):
+            gain_copy(step).start()
+        for h in range(2, count):
+            spread.hop(h)
+        gains_landing[z] = gains[...]
+        for step in range(1, count):
+            source = lax.rem(z + step, count)
+            pltpu.make_async_remote_copy(
+                src_ref=gains,
+                dst_ref=gains_landing.at[source],
+                send_sem=gain_send.at[step],
+                recv_sem=gain_recv.at[source],
+                device_id={"z": source},
+                device_id_type=MESH,
+            ).wait_recv()
+        for step in range(1, count):
+            gain_copy(step).wait_send()
+        gains[...] = jnp.sum(gains_landing[...], axis=0)
+        pltpu.sync_copy(gains, gains_out)
+        spread.end()
+
+        @pl.loop(0, count)
+        def _(layer):
+            @pl.when(layer < z)
+            def _():
+                kv_move(layer, kv_own).wait_send()
+
+    pl.run_scoped(
+        attention,
+        pltpu.VMEM((features, 3 * local), BF16),
+        pltpu.VMEM((features, local), BF16),
+        pltpu.VMEM((group, local), BF16),
+        pltpu.VMEM((group, local), BF16),
+        pltpu.VMEM((group, 2 * local), BF16),
+        pltpu.VMEM((group, local), BF16),
+        pltpu.VMEM((group, local), F32),
+        pltpu.VMEM((group, 2 * local), F32),
+        pltpu.VMEM((group, 2 * local), BF16),
+        pltpu.VMEM((features, 2 * local), F32),
+        pltpu.VMEM((heads, group, HD), F32),
+        pltpu.VMEM((heads, 1, group), F32),
+        pltpu.VMEM((heads, 1, group), F32),
+        pltpu.VMEM((thin, features), F32),
+        pltpu.VMEM((rows, width), BF16),
+        pltpu.VMEM((rows, width), BF16),
+    )
+    for which in (0, 1):
+        home_copy(which, True).wait_recv()
+        home_copy(which).wait_send()
+    for line in (down_line, up_line, attn_line):
+        line.drain()
+    out_sum.drain()
+    last_sum.drain()
+    first_gather.drain()
+    last_gather.drain()
+
+
+def back(count, *args):
+    (x_all, in_all, kv_all, query, *_, w_out, gain1, gain2, start_row, key_place) = args
+    down_all, w_query = args[9], args[11]
+    _, group, features = x_all.shape
+    rows = group // 2
+    local = query.shape[1]
+    heads = local // HD
+    hidden = down_all.shape[1]
+    width = features // 4
+    chunk = features // count
+    hbm, vmem = pl.BlockSpec(memory_space=pl.ANY), pl.BlockSpec(memory_space=pltpu.VMEM)
+
+    def out(*shape, dtype=BF16):
+        return jax.ShapeDtypeStruct(shape, dtype)
+
+    dma = pltpu.SemaphoreType.DMA
+    return pl.pallas_call(
+        functools.partial(back_kernel, count),
+        name="back",
+        out_shape=(
+            out(rows, width),
+            out(group, width, dtype=F32),
+            out(8, features, dtype=F32),
+            out(2, 2, chunk // 2, hidden),
+            out(count, 2, chunk, 4 * local),
+            out(3, features, hidden),
+            out(3, count + 1, chunk, hidden),
+            out(3, count, chunk, hidden),
+            out(2, chunk, hidden),
+            out(group, features),
+            out(group, width, dtype=F32),
+            out(count, group, 2 * local),
+            out(count, group, 2 * local),
+            out(count, group, 2 * local),
+        ),
+        in_specs=[hbm] * 15 + [vmem] * 4,
+        out_specs=[hbm] * 14,
+        scratch_shapes=[
+            pltpu.VMEM((group, features), BF16),
+            pltpu.VMEM((group, features), BF16),
+            pltpu.VMEM((group, features), BF16),
+            pltpu.VMEM((group, features), BF16),
+            *reduce_scratch(rows, width),
+            *reduce_scratch(rows, width),
+            *reduce_scratch(rows, width),
+            pltpu.VMEM((8, features), F32),
+            pltpu.VMEM((count, 8, features), F32),
+            dma((8,)),
+            dma((3, 10)),
+            dma((3, 10)),
+            dma((2, 9)),
+            dma((2, 9)),
+            dma((3, count)),
+            dma((3, count + 1)),
+            dma((2,)),
+            dma((2,)),
+            *[dma((count,))] * 9,
+        ],
+        compiler_params=pltpu.CompilerParams(
+            collective_id=1, has_side_effects=True, vmem_limit_bytes=60 * 1024 * 1024
+        ),
+    )(*args)
 
 
 def body(
@@ -762,168 +1460,45 @@
 ):
     count = lax.axis_size("z")
     z, x = lax.axis_index("z"), lax.axis_index("x")
-    column = lax.axis_index("y") * lax.axis_size("core") + lax.axis_index("core")
-    share_rows, share_width = layer_input.shape
-    rows = 2 * share_rows
+    rows = layer_input.shape[0]
     width = w_query.shape[0]
     local = w_query.shape[1] // 2
-    heads = local // HD
     hidden = w_up.shape[1] // 2
-    scale = HD ** (-0.5)
-    gain1_share = lax.dynamic_slice_in_dim(norm1_gain, column * share_width, share_width)
-    gain2_share = lax.dynamic_slice_in_dim(norm2_gain, column * share_width, share_width)
-
-    def half(weight, which):
-        size = weight.shape[1] // 2
-        return lax.dynamic_slice_in_dim(weight, which * size, size, 1)
-
     clip_ends = jnp.cumsum(clip_lengths)
     position = jnp.arange(key_padding.shape[0], dtype=jnp.int32)
     starts = jnp.max(jnp.where(position[:, None] >= clip_ends, clip_ends, 0), axis=1)
-    key_place = jnp.where(key_padding > 0, position, -1).reshape(count, 1, rows)
-    start_of = lax.dynamic_slice_in_dim(starts, z * rows, rows)[:, None]
-    (x_all, in_all, kv_all, query, attended, log_sum, branch, mlp_in, grad_out, down_full, up_full) = front(
+    key_place = jnp.where(key_padding > 0, position, -1).reshape(count, 1, 2 * rows)
+    own_starts = lax.dynamic_slice_in_dim(starts, z * 2 * rows, 2 * rows)
+    gain1, gain2 = norm1_gain[None], norm2_gain[None]
+    *kept, down_full, up_full = front(
         count, layer_input, out_grad, w_query, w_key, w_value, w_out, w_up, w_down,
-        norm1_gain[None], norm2_gain[None], start_of, key_place,
+        gain1, gain2, own_starts[:, None], key_place,
     )
-    down_full = down_full.reshape(width, hidden)
-    up_full = up_full.reshape(width, hidden)
-    attn_in = in_all[0]
-    below = [kv_all[d] for d in range(1, count)]
-    own_kv = kv_all[0]
-    log_sum = log_sum[:, :, :1]
-    query_w, key_w, value_w, out_w = (half(w, x) for w in (w_query, w_key, w_value, w_out))
-    wide = x_all[0].astype(F32)
-    normed1_all, inverse1 = normed_rows(wide)
-    mean1 = jnp.mean(wide, axis=1, keepdims=True)
-    normed2_all, inverse2_all = normed_rows(wide + branch.astype(F32))
-
-    def split(block):
-        return block.reshape(block.shape[0], heads, HD)
-
-    query_heads = split(query)
-
-    def share_of(array):
-        return lax.dynamic_slice_in_dim(array, x * share_rows, share_rows, 0)
-
-    def block_of(array):
-        return lax.dynamic_slice_in_dim(share_of(array), column * share_width, share_width, 1)
-
-    resid = layer_input.astype(F32) + block_of(branch).astype(F32)
-    normed2, inverse2 = block_of(normed2_all), share_of(inverse2_all)
-
-    grad_act = jnp.dot(grad_out, down_full, preferred_element_type=F32)
-    up_f = jnp.dot(mlp_in, up_full, preferred_element_type=F32)
-    gelu_value, gelu_back = jax.vjp(jax.nn.gelu, up_f)
-    activated = gelu_value.astype(BF16)
-    grad_up = gelu_back(grad_act)[0].astype(BF16)
-    grad_mlp_part = jnp.einsum("tf,df->td", grad_up, up_full, preferred_element_type=F32)
-    grad_mlp = layer_reduce(grad_mlp_part.astype(BF16)).astype(F32)
-    down_part = jnp.einsum("tf,df->td", activated, down_full, preferred_element_type=F32)
-    layer_output = (resid + layer_reduce(down_part.astype(BF16)).astype(F32)).astype(BF16)
-
-    down_term = jnp.einsum("tc,tf->cf", grad_out, activated, preferred_element_type=F32)
-    up_term = jnp.einsum("tc,tf->cf", mlp_in, grad_up, preferred_element_type=F32)
-
-    def weight_home(term):
-        mine = line_reduce(term.astype(BF16), count, z).astype(BF16)
-        size = mine.shape[0] // 2
-        other = swapped(lax.dynamic_slice_in_dim(mine, (1 - x) * size, size, 0), "x")
-        own = lax.dynamic_slice_in_dim(mine, x * size, size, 0)
-        return jnp.where(
-            x == 0, jnp.concatenate([own, other], 1), jnp.concatenate([other, own], 1)
-        ).astype(F32)
-
-    down_grad = weight_home(down_term)
-    up_grad = weight_home(up_term)
-
-    def norm_back(grad, normed, inverse, gain_share):
-        scaled = grad * gain_share
-        sums = lax.psum(
-            jnp.stack([jnp.sum(scaled, axis=1), jnp.sum(scaled * normed, axis=1)], axis=1),
-            ("y", "core"),
+    output, input_grad, gains, mlp_grads, attn_grads, *_ = back(
+        count, *kept, down_full.reshape(width, hidden), up_full.reshape(width, hidden),
+        w_query, w_key, w_value, w_out, gain1, gain2, own_starts[None], key_place,
+    )
+
+    def both_halves(first, size):
+        part = attn_grads[..., first : first + size].astype(F32)
+        return jnp.concatenate(
+            [part[:, 0].reshape(width, size), part[:, 1].reshape(width, size)], axis=1
         )
-        centre, slope = sums[:, :1] / width, sums[:, 1:] / width
-        return inverse * (scaled - centre - normed * slope), jnp.sum(grad * normed, axis=0)
-
-    back2, gain2_part = norm_back(grad_mlp, normed2, inverse2, gain2_share)
-    grad_resid = out_grad.astype(F32) + back2
-    grad_branch = layer_gather(grad_resid.astype(BF16))
-    out_weight_part = jnp.einsum("td,tf->df", grad_branch, attended, preferred_element_type=F32)
-    grad_attended = jnp.dot(grad_branch, out_w, preferred_element_type=F32).astype(BF16)
-    grad_heads = split(grad_attended)
-    delta = jnp.einsum("thd,thd->ht", grad_heads.astype(F32), split(attended).astype(F32))
-
-    def stage(kv, distance):
-        keys, values = split(kv[:, :local]), split(kv[:, local:])
-        places = key_place[jnp.maximum(z - distance, 0)]
-        allowed = (places >= start_of) & (z >= distance)
-        if distance == 0:
-            at = jnp.arange(rows)
-            allowed = (allowed & (at[None, :] <= at[:, None])) | (at[None, :] == at[:, None])
-        scores = jnp.einsum("qhd,khd->hqk", query_heads, keys, preferred_element_type=F32) * (scale * LOG2E)
-        probs = jnp.where(allowed[None], jnp.exp2(scores - log_sum), 0.0)
-        grad_probs = jnp.einsum("qhd,khd->hqk", grad_heads, values, preferred_element_type=F32)
-        grad_scores = (probs * (grad_probs - delta[:, :, None]) * scale).astype(BF16)
-        grad_query = jnp.einsum("hqk,khd->qhd", grad_scores, keys, preferred_element_type=F32)
-        grad_key = jnp.einsum("hqk,qhd->khd", grad_scores, query_heads, preferred_element_type=F32)
-        grad_value = jnp.einsum(
-            "hqk,qhd->khd", probs.astype(BF16), grad_heads, preferred_element_type=F32
-        )
-        return grad_query.reshape(rows, local), jnp.concatenate(
-            [grad_key.reshape(rows, local), grad_value.reshape(rows, local)], axis=1
-        )
-
-    grad_query, moving = jnp.zeros((rows, local), F32), None
-    for hop in range(1, count):
-        more, grad_kv = stage(below[count - hop - 1], count - hop)
-        grad_query = grad_query + more
-        if moving is not None:
-            grad_kv = grad_kv + moving.astype(F32)
-        moving = shifted(grad_kv.astype(BF16), "z", -1, max(count - hop, 1), count - 1)
-    more, grad_kv = stage(own_kv, 0)
-    grad_query = (grad_query + more).astype(BF16)
-    if moving is not None:
-        grad_kv = grad_kv + moving.astype(F32)
-    grad_kv = grad_kv.astype(BF16)
-    grads = jnp.concatenate([grad_query, grad_kv], axis=1)
-
-    qkv_w = jnp.concatenate([query_w, key_w, value_w], axis=1)
-    grad_attn_part = jnp.einsum("tf,df->td", grads, qkv_w, preferred_element_type=F32)
-    grad_attn = layer_reduce(grad_attn_part.astype(BF16)).astype(F32)
-    qkv_part = jnp.einsum("td,tf->df", attn_in, grads, preferred_element_type=F32)
-
-    def weight_everywhere(partial):
-        mine = line_reduce(partial.astype(BF16), count, z).astype(BF16)
-        return line_whole(mine, count, z)
-
-    def both_halves(block):
-        other = swapped(block, "x")
-        return jnp.where(
-            x == 0, jnp.concatenate([block, other], 1), jnp.concatenate([other, block], 1)
-        ).astype(F32)
-
-    out_weight_grad = both_halves(weight_everywhere(out_weight_part))
-    qkv_grad = weight_everywhere(qkv_part)
-    query_grad = both_halves(qkv_grad[:, :local])
-    key_grad = both_halves(qkv_grad[:, local : 2 * local])
-    value_grad = both_halves(qkv_grad[:, 2 * local :])
-
-    mean1_share, inverse1_share = share_of(mean1), share_of(inverse1)
-    normed1 = (layer_input.astype(F32) - mean1_share) * inverse1_share
-    back1, gain1_part = norm_back(grad_attn, normed1, inverse1_share, gain1_share)
-    input_grad = grad_resid + back1
-
-    gains = lax.psum(jnp.stack([gain1_part, gain2_part]), ("z", "x"))
-    gains = lax.all_gather(gains, ("y", "core"), axis=1, tiled=True)
+
+    key_grad, value_grad, query_grad, out_grad_w = (
+        both_halves(i * local, local) for i in range(4)
+    )
+    down_grad, up_grad = (
+        jnp.concatenate([mlp_grads[i, 0], mlp_grads[i, 1]], axis=1).astype(F32) for i in range(2)
+    )
     return (
-        layer_output,
-        input_grad,
+        output,
+        lax.dynamic_slice_in_dim(input_grad, x * rows, rows, 0),
         gains[0],
         query_grad,
         key_grad,
         value_grad,
-        out_weight_grad,
+        out_grad_w,
         gains[1],
         up_grad,
         down_grad,

time: 1050 us -> 710 us (0.68)
  Pallas kernels: 204 us -> 665 us
  waiting for transfers between devices: 355 us -> 0 us
  starting transfers between devices: 156 us -> 0 us
  matrix products: 127 us -> 0 us
  other arithmetic: 96.9 us -> 23.7 us
  local copies, waits for them, and re-layouts: 55.3 us -> 11.6 us
  blocking collectives: 35.2 us -> 0 us
  between operations: 15.9 us -> 1.16 us
    pallas_call x0 -> x1, Pallas kernels: none -> 460 us  [back(): pl.pallas_call(functools.partial(back_kernel, count), name='back', out_sh...]
    ppermute x45 -> x0, waiting for transfers between devices: 234 us -> none  [the longest x39 195 us: shifted(): lax.ppermute(block, axis, [(i, i + step) for i in range(first, last + 1)])]
    ppermute x45 -> x0, starting transfers between devices: 155 us -> none  [the longest x39 149 us: shifted(): lax.ppermute(block, axis, [(i, i + step) for i in range(first, last + 1)])]
    dot_general x30 -> x0, matrix products: 127 us -> none  [the longest x4 19.9 us: stage(): jnp.einsum('qhd,khd->hqk', grad_heads, values, preferred_element_type=F32)]
    reduce_scatter x6 -> x0, waiting for transfers between devices: 85.2 us -> none  [the longest x3 67.1 us: layer_reduce(): tall = lax.psum_scatter(partial, 'x', scatter_dimension=0, tiled=True)]
    convert_element_type x26 -> x2, other arithmetic: 62.7 us -> 11.1 us  [the longest x1 8.55 us: both_halves(): part = attn_grads[..., first:first + size].astype(F32)]
    all_gather x2 -> x0, waiting for transfers between devices: 36 us -> none  [the longest x1 18.7 us: layer_gather(): wide = lax.all_gather(share, ('y', 'core'), axis=1, tiled=True)]
    psum x3 -> x0, blocking collectives: 30 us -> none  [the longest x1 18.6 us: body(): gains = lax.psum(jnp.stack([gain1_part, gain2_part]), ('z', 'x'))]
  transfers between devices with their start and end apart: 53 -> 0, of which waited for: 20 -> 0; matrix products, arithmetic and copies ran while one was open for 19% -> 0% of each run, Pallas kernels for 0% -> 0%
where the time goes in v3:
time: 710 us; the launch traced here: 701 us
  Pallas kernels  665 us (94%)
  other arithmetic  23.7 us (3%)
  local copies, waits for them, and re-layouts  11.6 us (2%)
    pallas_call x1, Pallas kernels, back(): pl.pallas_call(functools.partial(back_kernel, count), name='back', out_sh...  460 us
    pallas_call x1, Pallas kernels, front(): pl.pallas_call(functools.partial(front_kernel, count), name='front', out_...  204 us

profile of v3, /device:TPU:0, one launch (start us, length us, event | category | flops | bytes accessed | tf_op | source)
XLA Modules:
  0.0 701.0 jit_solution(13657620320093169791)
XLA Ops:
  0.6 0.8 reduce-window.8
  1.5 0.1 select_reduce_fusion
  1.6 0.0 copy-start.3
  1.6 1.3 iota_select_fusion
  3.0 1.0 copy.23.start_of
  4.0 204.3 %front.1 = (bf16[4,1024,2048]{2,1,0:T(8,128)(2,1)}, bf16[4,1024,2048]{2,1,0:T(8,128)(2,1)}, bf16[4,1024,512]{2,1,0:T(8,128)(2,1)}, bf16[1024,256]{1,0:T(8,128)(2...) custom-call(bf16[512,512]{1,0:T(8,128)(2,1)} %xs.1, ...), custom_call_target="tpu_custom_call" | custom-call | tf_op jit(solution)/shard_map/front/pallas_call | solution.py:646
  208.3 0.0 copy-done.3
  208.3 460.3 %back.1 = (bf16[512,512]{1,0:T(8,128)(2,1)}, f32[1024,512]{1,0:T(8,128)}, f32[8,2048]{1,0:T(8,128)}, bf16[2,2,256,1024]{3,2,1,0:T(8,128)(2,1)}, bf16[4,2,512,102...) custom-call(bf16[4,1024,2048]{2,1,0:T(8,128)(2,1)} %get-tuple-elemen, ...), custom_call_target="tpu_custom_call" | custom-call | tf_op jit(solution)/shard_map/back/pallas_call | solution.py:1399
  668.6 0.0 copy-start.1
  668.6 1.6 fusion.4
  670.3 2.3 constant_dynamic-slice_fusion
  672.5 0.0 copy-done.1
  672.5 0.2 slice_bitcast_fusion.1
  672.7 2.5 maximum_convert_fusion
  675.3 8.6 %slice_convert_fusion = (f32[4,2,512,256]{3,2,1,0:T(8,128)}, f32[4,2,512,256]{3,2,1,0:T(8,128)}, f32[4,2,512,256]{3,2,1,0:T(8,128)S(1)}, f32[4,2,512,256]{3,2,1,0:T(8,128)}) fusion(bf16[4,2,512,1024]{3,2,1,0:T(8,128)(2,1)} %get-tuple-element.40), kind=kLoop, calls=%fused_computation.4 | loop fusion | flops 4194304 | bytes 25165824 | tf_op jit(solution)/shard_map/convert_element_type | solution.py:1483
  683.8 4.0 fusion
  687.8 2.5 pad_maximum_fusion.3
  690.4 0.0 copy-start
  690.4 2.7 pad_maximum_fusion.2
  693.0 1.0 copy-done
  694.1 0.6 fusion.2
  694.7 2.5 pad_maximum_fusion.1
  697.2 0.0 copy-start.2
  697.2 2.5 pad_maximum_fusion
  699.8 0.0 copy-done.2
  699.8 0.8 copy.25
  (1 shorter events, 0.0 us)
Async XLA Ops:
  1.6 206.6 %copy-start.3 = (s32[1024]{0:T(1024)}, s32[1024]{0:T(1024)S(1)}, u32[]{:S(2)}) copy-start(s32[1024]{0:T(1024)S(1)} %dynamic_slice.6) | copy-start | bytes 12292
  668.6 3.9 copy-start.1
  690.4 3.7 copy-start
  697.2 2.5 copy-start.2

commit v4 on v3

--- a/solution.py
+++ b/solution.py
@@ -1,3 +1,4 @@
+import copy
 import functools
 
 import jax
@@ -29,6 +30,12 @@
     )
 
 
+def pick(which, left, right):
+    if isinstance(which, bool):
+        return left if which else right
+    return jnp.where(which, left, right)
+
+
 def contract(left, right, dims):
     return lax.dot_general(left, right, (dims, ((), ())), preferred_element_type=F32)
 
@@ -39,6 +46,11 @@
         self.z = lax.axis_index("z")
         self.x, self.y, self.c = lax.axis_index("x"), lax.axis_index("y"), lax.axis_index("core")
         self.ox, self.oy, self.oc = 1 - self.x, 1 - self.y, 1 - self.c
+
+    def fixed(self, z):
+        other = copy.copy(self)
+        other.z = z
+        return other
 
     def meet(self, whole_line=False):
         barrier = pltpu.get_barrier_semaphore()
@@ -238,11 +250,10 @@
     def columns(self, which):
         return self.weight.at[:, pl.ds(pl.multiple_of(which * self.half, self.half), self.half)]
 
-    def own(self):
+    def own(self, stage, out):
         at = self.at
-        return pltpu.make_async_copy(
-            self.columns(at.x), self.whole.at[at.z, at.x], self.local.at[self.which]
-        )
+        source, target = (stage, self.whole.at[at.z, at.x]) if out else (self.columns(at.x), stage)
+        return pltpu.make_async_copy(source, target, self.local.at[self.which])
 
     def swap(self, landing=False):
         at = self.at
@@ -261,21 +272,15 @@
             device_id_type=MESH,
         )
 
-    def first(self, mine):
+    def first(self, mine, steps=(1, -1)):
         at = self.at
         part = at.x if mine else at.ox
-        if mine:
-            self.own().wait()
-        else:
-            self.swap(True).wait_recv()
-
-        @pl.when(at.z < at.count - 1)
-        def _():
-            self.move(at.z, part, 1).start()
-
-        @pl.when(at.z > 0)
-        def _():
-            self.move(at.z, part, -1).start()
+        for step, there in ((1, at.z < at.count - 1), (-1, at.z > 0)):
+            if step in steps:
+
+                @pl.when(there)
+                def _():
+                    self.move(at.z, part, step).start()
 
     def hop(self, distance, mine):
         at = self.at
@@ -404,25 +409,41 @@
     down = Weights(at, 0, w_down, down_all, weight_sems)
     up = Weights(at, 1, w_up, up_all, weight_sems)
 
-    own_x = pltpu.make_async_copy(xs, own_block(0), load_sem.at[4])
-    own_og = pltpu.make_async_copy(og, og_gather.block(x, y, c), load_sem.at[5])
-    own_x.start()
-    down.own().start()
-    up.own().start()
-    own_og.start()
-    for load in loads:
-        load.start()
+    w_rows, hidden = w_up.shape[0], w_up.shape[1] // 2
+    places = [
+        partial.at[pl.ds(0, rows), pl.ds(i * width, width)] for i in range(2)
+    ] + [partial.at[pl.ds(rows, w_rows), pl.ds(i * hidden, hidden)] for i in range(2)]
+    into = [
+        pltpu.make_async_copy(xs, places[0], load_sem.at[4]),
+        down.own(places[2], False),
+        up.own(places[3], False),
+        pltpu.make_async_copy(og, places[1], load_sem.at[5]),
+    ]
+    onto = [
+        pltpu.make_async_copy(places[0], own_block(0), load_sem.at[4]),
+        down.own(places[2], True),
+        up.own(places[3], True),
+        pltpu.make_async_copy(places[1], og_gather.block(x, y, c), load_sem.at[5]),
+    ]
+    for copy in into + loads:
+        copy.start()
+    for first, second in zip(into, onto):
+        first.wait()
+        second.start()
     at.meet()
-    own_x.wait()
+    onto[0].wait()
 
     @pl.when(z < count - 1)
     def _():
         line_copy(0).start()
 
     gather_of(0).start()
+    onto[1].wait()
     down.first(True)
+    onto[2].wait()
+    up.first(True, (-1,))
+    onto[3].wait()
     gather_of(0).middle()
-    down.swap().start()
     for load in loads:
         load.wait()
 
@@ -481,20 +502,10 @@
                 total[h, part, :] = jnp.broadcast_to(mass, (tile, HD))
                 sums[part, span] = value
 
-    def piece(d, diagonal):
-        project(d, diagonal)
+    def fetch(d, diagonal):
         pltpu.sync_copy(kv_all.at[d], kv)
         if diagonal:
             pltpu.sync_copy(query_out, query)
-        attend(d, diagonal)
-
-    halves = [(up, True), (down, False), (up, False)]
-
-    def send_half(step):
-        weight, mine = halves[step]
-        weight.first(mine)
-        if step == 0:
-            up.swap().start()
 
     def bring(d):
         @pl.when(z >= d)
@@ -513,53 +524,91 @@
             for name in names:
                 getattr(gather_of(d), name)()
 
-    hops = [
-        (weight, distance, mine)
-        for distance in range(1, count)
-        for weight, mine in ((down, True), (up, True), (down, False), (up, False))
+    def other_rows(weight):
+        weight.swap(True).wait_recv()
+        weight.first(False)
+
+    def hop_of(weight, distance, mine):
+        return functools.partial(weight.hop, distance, mine)
+
+    events = [
+        hop_of(down, 1, True),
+        hop_of(up, 1, True),
+        functools.partial(other_rows, down),
+        hop_of(down, 1, False),
+        functools.partial(other_rows, up),
+        hop_of(up, 1, False),
     ]
-
-    def hop(many=1):
-        for _ in range(min(many, len(hops))):
-            weight, distance, mine = hops.pop(0)
-            weight.hop(distance, mine)
-
+    for distance in range(2, count):
+        for mine in (True, False):
+            events += [hop_of(down, distance, mine), hop_of(up, distance, mine)]
+
+    def advance(many=1):
+        for _ in range(min(many, len(events))):
+            events.pop(0)()
+
+    bring(1)
+    up.first(True, (1,))
     gather_of(0).corner()
     gather_of(0).end()
-    bring(1)
-    send_half(0)
-    piece(0, True)
+    project(0, True)
     within(1, "middle")
+    down.swap().start()
+    fetch(0, True)
+    attend(0, True)
 
     @pl.loop(2, count)
     def _(d):
+        bring(d)
+
+        for k in (2, 3):
+
+            @pl.when(d == k)
+            def _():
+                events[2 * k - 4]()
+
         within(d - 1, "corner", "end")
-        bring(d)
-        for step in (1, 2):
-
-            @pl.when(d == step + 1)
-            def _():
-                send_half(step)
 
         @pl.when(z >= d - 1)
         def _():
-            piece(d - 1, False)
+            project(d - 1, False)
 
         within(d, "middle")
 
-    for step in range(max(count - 1, 1), 3):
-        send_half(step)
-    hop(2)
+        for k in (2, 3):
+
+            @pl.when(d == k)
+            def _():
+                if k == 2:
+                    up.swap().start()
+                events[2 * k - 3]()
+
+        @pl.when(z >= d - 1)
+        def _():
+            fetch(d - 1, False)
+            attend(d - 1, False)
+
+    if count < 3:
+        up.swap().start()
+    del events[: 2 * min(count - 2, 2)]
+    advance()
+    og_gather.start()
     within(count - 1, "corner", "end")
-    own_og.wait()
-    og_gather.start()
 
     @pl.when(z >= count - 1)
     def _():
-        piece(count - 1, False)
-
-    hop()
+        project(count - 1, False)
+
+    advance()
     og_gather.middle()
+
+    @pl.when(z >= count - 1)
+    def _():
+        fetch(count - 1, False)
+        attend(count - 1, False)
+
+    advance(2)
+    og_gather.corner()
 
     @pl.loop(0, tiles)
     def _(i):
@@ -577,17 +626,15 @@
     ]
     for out in outs:
         out.start()
-    hop()
-    og_gather.corner()
     reduce = Reduce(
         at, partial, rows, width, (twin, corner_x, corner_y, from_x, from_y), reduce_send, reduce_recv
     )
     reduce.start()
     og_gather.end()
     reduce.twins()
-    hop()
+    advance()
     reduce.corners()
-    hop()
+    advance()
     own_branch = branch_gather.block(x, y, c)
 
     def store(part, value):
@@ -595,11 +642,10 @@
 
     reduce.end(store)
     branch_gather.start()
-    hop()
+    advance()
     branch_gather.middle()
-    hop()
+    advance()
     branch_gather.corner()
-    hop()
     branch_gather.end()
     pltpu.sync_copy(branch, branch_out)
 
@@ -611,7 +657,7 @@
     pltpu.emit_pipeline(second_norm, grid=(tiles,), in_specs=[spec, spec], out_specs=[spec])(
         x_all.at[0], branch_out, mlp_out
     )
-    hop(len(hops))
+    advance(len(events))
 
     for out in outs:
         out.wait()
@@ -694,19 +740,19 @@
 
 
 class LineSum:
-    def __init__(self, at, which, terms, landing, sums, sends, recvs):
-        self.at, self.which = at, which
+    def __init__(self, at, which, terms, landing, sums, sends, recvs, eager=False):
+        self.at, self.which, self.eager = at, which, eager
         self.terms, self.landing, self.sums = terms, landing, sums
         self.sends, self.recvs = sends, recvs
-        self.rows = sums.shape[2]
+        self.rows = sums.shape[1]
 
     def chunk(self, c):
-        return self.terms.at[self.which, pl.ds(pl.multiple_of(c * self.rows, self.rows), self.rows)]
+        return self.terms.at[pl.ds(pl.multiple_of(c * self.rows, self.rows), self.rows)]
 
     def move(self, source, c, slot, step):
         return pltpu.make_async_remote_copy(
             src_ref=source,
-            dst_ref=self.landing.at[self.which, slot],
+            dst_ref=self.landing.at[slot],
             send_sem=self.sends.at[self.which, c],
             recv_sem=self.recvs.at[self.which, slot],
             device_id={"z": self.at.z + step},
@@ -714,8 +760,7 @@
         )
 
     def landed(self, slot):
-        ref = self.landing.at[self.which, slot]
-        self.move(ref, 0, slot, 0).wait_recv()
+        self.move(self.landing.at[slot], 0, slot, 0).wait_recv()
 
     def total(self, refs, out):
         tile = min(256, self.rows)
@@ -726,34 +771,43 @@
                 value = value + other[...].astype(F32)
             tiles[-1][...] = value.astype(BF16)
 
-        spec = pl.BlockSpec((tile, self.sums.shape[3]), lambda i: (i, 0))
+        spec = pl.BlockSpec((tile, self.sums.shape[2]), lambda i: (i, 0))
         pltpu.emit_pipeline(
             step, grid=(self.rows // tile,), in_specs=[spec] * len(refs), out_specs=[spec]
         )(*refs, out)
 
-    def hop(self, h):
+    def begin(self, h):
+        n, z = self.at.count, self.at.z
+        for step, end, c, slot in ((1, 0, n - h, n - h), (-1, n - 1, h - 1, None)):
+            if slot is None:
+                slot = n if c == n - 2 else c
+
+            @pl.when(z == end)
+            def _():
+                self.move(self.chunk(c), c, slot, step).start()
+
+    def hop(self, h, steps=(1, -1)):
         at, n, z = self.at, self.at.count, self.at.z
-        for step, c, there, slot in (
-            (1, n - h + z, (z <= h - 1) & (z < n - 1), n - h + z),
-            (-1, z - n + h, (z >= n - h) & (z > 0), None),
+        if h == 1:
+            for each in range(1, n if self.eager else 2):
+                self.begin(each)
+        for step, c, there in (
+            (1, n - h + z, (z <= h - 1) & (z < n - 1) & (z > 0)),
+            (-1, z - n + h, (z >= n - h) & (z > 0) & (z < n - 1)),
         ):
-            if slot is None:
-                slot = jnp.where(c == z - 1, n, c)
-            first = z == (0 if step > 0 else n - 1)
-
-            @pl.when(there & first)
-            def _():
-                self.move(self.chunk(c), c, slot, step).start()
-
-            @pl.when(there & jnp.logical_not(first))
+            if step not in steps:
+                continue
+            slot = c if step > 0 else pick(c == z - 1, n, c)
+
+            @pl.when(there)
             def _():
                 self.landed(c)
-                self.total([self.chunk(c), self.landing.at[self.which, c]], self.sums.at[self.which, c])
-                self.move(self.sums.at[self.which, c], c, slot, step).start()
+                self.total([self.chunk(c), self.landing.at[c]], self.sums.at[c])
+                self.move(self.sums.at[c], c, slot, step).start()
 
     def final(self, out):
         n, z = self.at.count, self.at.z
-        below, above = self.landing.at[self.which, z], self.landing.at[self.which, n]
+        below, above = self.landing.at[z], self.landing.at[n]
 
         @pl.when(z > 0)
         def _():
@@ -786,18 +840,18 @@
 
 
 class Spread:
-    def __init__(self, at, whole, ups, downs, lines, sides, sidesr):
-        self.at, self.whole = at, whole
+    def __init__(self, at, which, whole, ups, downs, lines, sides, sidesr):
+        self.at, self.which, self.whole = at, which, whole
         self.ups, self.downs, self.lines, self.sides, self.sidesr = ups, downs, lines, sides, sidesr
 
     def move(self, layer, step):
         ref = self.whole.at[layer, self.at.x]
         sends = self.ups if step > 0 else self.downs
-        return remote(ref, ref, sends, self.lines, (layer,), z=self.at.z + step)
+        return remote(ref, ref, sends, self.lines, (self.which, layer), z=self.at.z + step)
 
     def side(self, layer, part):
         ref = self.whole.at[layer, part]
-        return remote(ref, ref, self.sides, self.sidesr, (layer,), x=self.at.ox)
+        return remote(ref, ref, self.sides, self.sidesr, (self.which, layer), x=self.at.ox)
 
     def first(self):
         at = self.at
@@ -812,28 +866,19 @@
 
         self.side(at.z, at.x).start()
 
-    def hop(self, distance):
+    def hop(self, distance, step):
         at = self.at
-
-        @pl.when(at.z >= distance)
+        layer = at.z - step * distance
+
+        @pl.when((layer >= 0) & (layer < at.count))
         def _():
-            self.move(at.z - distance, 1).wait_recv()
-
-            @pl.when(at.z < at.count - 1)
-            def _():
-                self.move(at.z - distance, 1).start()
-
-            self.side(at.z - distance, at.x).start()
-
-        @pl.when(at.z + distance < at.count)
-        def _():
-            self.move(at.z + distance, -1).wait_recv()
-
-            @pl.when(at.z > 0)
-            def _():
-                self.move(at.z + distance, -1).start()
-
-            self.side(at.z + distance, at.x).start()
+            self.move(layer, step).wait_recv()
+
+            @pl.when((at.z + step >= 0) & (at.z + step < at.count))
+            def _():
+                self.move(layer, step).start()
+
+            self.side(layer, at.x).start()
 
     def end(self):
         at = self.at
@@ -850,6 +895,32 @@
             @pl.when((layer >= at.z) & (at.z > 0))
             def _():
                 self.move(layer, -1).wait_send()
+
+
+ORDERS = {
+    (4, 0): (
+        "b2", "b3", "twins", "corners", "home0", "keep", "home1", "f0", "D01", "D02", "own",
+        "f1", "middle", "D11", "D12", "f2", "D21", "D22", "f3", "D31", "D32", "D03", "D13",
+        "D23", "D33", "rows",
+    ),
+    (4, 1): (
+        "home0", "end", "twins", "u02", "home1", "u03", "corners", "u12", "u13", "d03", "f0",
+        "u22", "keep", "D01", "u23", "s0", "u32", "u33", "own", "d13", "U01", "f1", "middle",
+        "D11", "U11", "d23", "f2", "D21", "d33", "U21", "f3", "D31", "D02", "U31", "D12",
+        "D22", "D32", "rows",
+    ),
+    (4, 2): (
+        "home0", "d02", "home1", "d03", "u03", "f0", "end", "twins", "s0", "u13", "s1", "d12",
+        "U01", "d13", "u23", "f1", "corners", "d22", "u33", "d23", "f2", "d32", "U02", "keep",
+        "d33", "U11", "f3", "U12", "own", "U21", "D01", "D11", "D21", "middle", "U31", "D31",
+        "U22", "U32", "rows",
+    ),
+    (4, 3): (
+        "b2", "b3", "home0", "home1", "end", "twins", "f0", "U01", "f1", "U02", "corners",
+        "f2", "U11", "f3", "U21", "keep", "own", "U03", "U12", "U31", "U13", "middle", "U22",
+        "U32", "U23", "rows", "U33",
+    ),
+}
 
 
 def back_kernel(
@@ -877,35 +948,42 @@
     input_grad,
     gains_out,
     mlp_grads,
-    attn_grads,
-    terms,
-    landing,
-    sums,
+    out_grads,
+    query_grads,
+    key_grads,
+    value_grads,
+    down_terms,
+    up_terms,
+    out_terms,
+    query_terms,
+    key_terms,
+    value_terms,
+    down_landing,
+    up_landing,
+    out_landing,
+    query_landing,
+    key_landing,
+    value_landing,
+    down_sums,
+    up_sums,
+    out_sums,
+    query_sums,
+    key_sums,
+    value_sums,
     mine,
     grad_branch,
     grad_resid,
-    kv_own,
-    kv_landing,
-    kv_sums,
-    partial,
-    partial2,
+    share_own,
+    share_landing,
+    share_sums,
+    partials,
     full1,
     full3,
-    twin_a,
-    corner_xa,
-    corner_ya,
-    from_xa,
-    from_ya,
-    twin_b,
-    corner_xb,
-    corner_yb,
-    from_xb,
-    from_yb,
-    twin_c,
-    corner_xc,
-    corner_yc,
-    from_xc,
-    from_yc,
+    twin,
+    corner_x,
+    corner_y,
+    from_x,
+    from_y,
     gains,
     gains_landing,
     load_sem,
@@ -922,8 +1000,8 @@
     spread_line,
     spread_side,
     spread_side_recv,
-    kv_send,
-    kv_recv,
+    share_send,
+    share_recv,
     gain_send,
     gain_recv,
 ):
@@ -938,6 +1016,7 @@
     tile = min(256, group)
     tiles = group // tile
     thin = min(128, group)
+    chunk = features // count
     block = min(512, features)
     blocks = features // block
     own_column = pl.ds(pl.multiple_of((2 * y + c) * width, width), width)
@@ -954,46 +1033,74 @@
     def whole_spec(*shape):
         return pl.BlockSpec(shape, lambda i: (0,) * len(shape))
 
-    def reduce_of(array, buffers, k):
-        return Reduce(at, array, rows, width, buffers, reduce_send.at[k], reduce_recv.at[k])
+    def round_of(r):
+        p = r % 2 if isinstance(r, int) else lax.rem(r, 2)
+        third = r % 3 if isinstance(r, int) else lax.rem(r, 3)
+        buffers = (twin.at[third],) + tuple(
+            b.at[p] for b in (corner_x, corner_y, from_x, from_y)
+        )
+        return Reduce(
+            at, partials.at[p], rows, width, buffers, reduce_send.at[r], reduce_recv.at[r]
+        )
 
     def gather_of(array, k):
         return Gather(at, array, rows, width, gather_send, gather_recv, (k,))
 
-    first_sum = reduce_of(partial, (twin_a, corner_xa, corner_ya, from_xa, from_ya), 0)
-    out_sum = reduce_of(partial2, (twin_b, corner_xb, corner_yb, from_xb, from_yb), 1)
-    last_sum = reduce_of(partial, (twin_c, corner_xc, corner_yc, from_xc, from_yc), 2)
+    first_sum, out_sum = round_of(0), round_of(1)
     first_gather, last_gather = gather_of(full1, 0), gather_of(full3, 1)
-    down_line, up_line, attn_line = (
-        LineSum(at, k, terms, landing, sums, sum_send, sum_recv) for k in range(3)
-    )
-    spread = Spread(
-        at, attn_grads, spread_up, spread_down, spread_line, spread_side, spread_side_recv
-    )
-
-    def weight_terms(which, left, right, size, column):
+    attn_grads = (out_grads, query_grads, key_grads, value_grads)
+
+    def lines_at(at):
+        arrays = (
+            (down_terms, down_landing, down_sums),
+            (up_terms, up_landing, up_sums),
+            (out_terms, out_landing, out_sums),
+            (query_terms, query_landing, query_sums),
+            (key_terms, key_landing, key_sums),
+            (value_terms, value_landing, value_sums),
+        )
+        return [
+            LineSum(at, k, *three, sum_send, sum_recv, k > 1) for k, three in enumerate(arrays)
+        ]
+
+    def spreads_at(at):
+        sems = (spread_up, spread_down, spread_line, spread_side, spread_side_recv)
+        return [Spread(at, k, whole, *sems) for k, whole in enumerate(attn_grads)]
+
+    down_line, up_line, *attn_lines = lines_at(at)
+    spreads = spreads_at(at)
+
+    def weight_terms(terms, left, right, first, many):
+        size = terms.shape[1]
+
+        def at_chunk(i):
+            return lax.rem(first + i, count)
+
         def step(left_ref, right_ref, out_ref):
             out_ref[...] = contract(left_ref[...], right_ref[...], ((0,), (0,))).astype(BF16)
 
         pltpu.emit_pipeline(
             step,
-            grid=(blocks,),
-            in_specs=[column_spec(group), whole_spec(group, size)],
-            out_specs=[pl.BlockSpec((block, size), lambda i: (i, column))],
-        )(left, right, terms.at[which])
-
-    def home(which):
-        line = (down_line, up_line)[which]
+            grid=(many,),
+            in_specs=[
+                pl.BlockSpec((group, chunk), lambda i: (0, at_chunk(i))),
+                whole_spec(group, size),
+            ],
+            out_specs=[pl.BlockSpec((chunk, size), lambda i: (at_chunk(i), 0))],
+        )(left, right, terms)
+
+    def home(which, line):
         line.final(mine.at[which])
         half = mine.shape[1] // 2
-        own = pltpu.make_async_copy(
-            mine.at[which, pl.ds(pl.multiple_of(x * half, half), half)],
-            mlp_grads.at[which, x],
-            load_sem.at[which],
+        home_copy(which).start()
+
+        def step(in_ref, out_ref):
+            out_ref[...] = in_ref[...]
+
+        spec = pl.BlockSpec((half, hidden), lambda i: (i, 0))
+        pltpu.emit_pipeline(step, grid=(1,), in_specs=[spec], out_specs=[spec])(
+            mine.at[which, pl.ds(pl.multiple_of(x * half, half), half)], mlp_grads.at[which, x]
         )
-        own.start()
-        home_copy(which).start()
-        own.wait()
 
     def home_copy(which, landing_part=False):
         half = mine.shape[1] // 2
@@ -1012,8 +1119,6 @@
 
         return store
 
-    at.meet(whole_line=True)
-
     def feed_forward(active, grad_up, w_down, w_up):
         loads = [
             pltpu.make_async_copy(up_all, w_up, load_sem.at[0]),
@@ -1021,6 +1126,7 @@
         ]
         for load in loads:
             load.start()
+        at.meet(whole_line=True)
         for load in loads:
             load.wait()
 
@@ -1041,22 +1147,36 @@
             in_specs=[rows_spec(features)] * 2,
             out_specs=[rows_spec(hidden)] * 2,
         )(mlp_in, og_all, active, grad_up)
-        weight_terms(0, og_all, active, hidden, 0)
+        first = jnp.where(z == 0, count - 1, 0)
+        weight_terms(down_terms, og_all, active, first, 1)
         down_line.hop(1)
-        weight_terms(1, mlp_in, grad_up, hidden, 0)
+        weight_terms(up_terms, mlp_in, grad_up, first, 1)
         up_line.hop(1)
 
-        @pl.loop(0, tiles)
-        def _(i):
-            part = pl.ds(pl.multiple_of(i * tile, tile), tile)
-            partial[part, :] = contract(grad_up[part, :], w_up[...], ((1,), (1,))).astype(BF16)
-
+        def back_through(target, source, weight):
+            @pl.loop(0, tiles)
+            def _(i):
+                part = pl.ds(pl.multiple_of(i * tile, tile), tile)
+                target[part, :] = contract(source[part, :], weight[...], ((1,), (1,))).astype(BF16)
+
+        back_through(partials.at[0], grad_up, w_up)
         first_sum.start()
-
-        @pl.loop(0, tiles)
-        def _(i):
-            part = pl.ds(pl.multiple_of(i * tile, tile), tile)
-            partial2[part, :] = contract(active[part, :], w_down[...], ((1,), (1,))).astype(BF16)
+        weight_terms(down_terms, og_all, active, first + 1, count - 1)
+        first_sum.twins()
+        weight_terms(up_terms, mlp_in, grad_up, first + 1, count - 1)
+        for h in range(2, count):
+            down_line.begin(h)
+            up_line.begin(h)
+        first_sum.corners()
+        back_through(partials.at[1], active, w_down)
+        first_sum.end(store_into(first_gather))
+        first_gather.start()
+        down_line.hop(2)
+        out_sum.start()
+        first_gather.middle()
+        first_gather.corner()
+        out_sum.twins()
+        first_gather.end()
 
     pl.run_scoped(
         feed_forward,
@@ -1065,19 +1185,10 @@
         pltpu.VMEM((features, hidden), BF16),
         pltpu.VMEM((features, hidden), BF16),
     )
-    first_sum.twins()
-    first_sum.corners()
-    first_sum.end(store_into(first_gather))
-    first_gather.start()
-    down_line.hop(2)
-    first_gather.middle()
-    first_gather.corner()
-    first_gather.end()
-    out_sum.start()
 
     def attention(
         qkv_w, out_w, query, attended, kv, grad_att, grad_query, grad_kv, grad_kv_low, kv_weight,
-        logs, log_row, delta_row, wide, resid_x, resid_branch,
+        logs, log_row, delta_row, wide, resid_x, resid_branch, share,
     ):
         loads = [
             pltpu.make_async_copy(
@@ -1111,6 +1222,7 @@
             resid_ref[...] = wide[:, own_column]
             att_ref[...] = jnp.dot(low, out_w[...], preferred_element_type=F32).astype(BF16)
 
+        up_line.hop(2)
         thin_spec = rows_spec(features, thin)
         pltpu.emit_pipeline(
             second_back,
@@ -1118,9 +1230,8 @@
             in_specs=[thin_spec] * 4,
             out_specs=[thin_spec, rows_spec(width, thin), rows_spec(local, thin)],
         )(x_all.at[0], branch_in, og_all, full1, grad_branch, grad_resid, grad_att)
-        up_line.hop(2)
-        out_sum.twins()
-        weight_terms(2, grad_branch, attended, local, 3)
+        out_sum.corners()
+        weight_terms(out_terms, grad_branch, attended, 0, count)
         for h in range(heads):
             span = slice(h * HD, (h + 1) * HD)
             log_row[h] = jnp.transpose(logs[h])[:1]
@@ -1129,12 +1240,14 @@
         grad_query[...] = jnp.zeros_like(grad_query)
         kv_weight[...] = jnp.zeros_like(kv_weight)
 
-        def stage(layer, diagonal):
-            pltpu.sync_copy(kv_all.at[z - layer], kv)
-            grad_kv[...] = jnp.zeros_like(grad_kv)
+        def attend_back(layer, diagonal, early):
+            if early:
+                pltpu.sync_copy(kv_all.at[z - layer], kv)
+                grad_kv[...] = jnp.zeros_like(grad_kv)
             keys = jnp.transpose(jnp.broadcast_to(key_place[layer], (HD, group)))[:, :1]
-
-            @pl.loop(0, tiles)
+            middle = tiles // 2
+
+            @pl.loop(0 if early else middle, middle if early else tiles)
             def _(i):
                 part = pl.ds(pl.multiple_of(i * tile, tile), tile)
                 allowed = keys >= start_row[:, part]
@@ -1159,8 +1272,10 @@
                     grad_kv[:, span] += jnp.dot(grad_scores, asked, preferred_element_type=F32)
                     grad_query[part, span] += contract(grad_scores, key, ((0,), (0,)))
 
-            grad_kv_low[...] = grad_kv[...].astype(BF16)
-
+            if not early:
+                grad_kv_low[...] = grad_kv[...].astype(BF16)
+
+        def kv_terms(layer):
             def add(in_ref, grad_ref, out_ref):
                 out_ref[...] += contract(in_ref[...], grad_ref[...], ((0,), (0,)))
 
@@ -1171,10 +1286,50 @@
                 out_specs=[pl.BlockSpec((block, 2 * local), lambda i: (i, 0))],
             )(in_all.at[z - layer], grad_kv_low, kv_weight)
 
-        def kv_move(layer, source):
+        def back_to_rows(layer, diagonal):
+            target = partials.at[lax.rem(layer, 2)]
+
+            @pl.loop(0, tiles)
+            def _(i):
+                part = pl.ds(pl.multiple_of(i * tile, tile), tile)
+                value = contract(grad_kv_low[part, :], qkv_w[:, : 2 * local], ((1,), (1,)))
+                if diagonal:
+                    value = value + contract(
+                        grad_query[part, :].astype(BF16), qkv_w[:, 2 * local :], ((1,), (1,))
+                    )
+                target[part, :] = value.astype(BF16)
+
+        def share_copy(layer, source):
             return remote(
-                source.at[layer], kv_landing.at[layer], kv_send, kv_recv, (layer,), z=z - 1
+                source.at[layer], share_landing.at[layer], share_send, share_recv, (layer,), z=z - 1
             )
+
+        def keep_share(layer, z):
+            def store(part, value):
+                share[part, :] = value
+
+            round_of(layer + 2).end(store)
+
+            @pl.when(layer < z)
+            def _():
+                resid_x[...] = share[...].astype(BF16)
+                pltpu.sync_copy(resid_x, share_own.at[layer])
+
+                @pl.when(z == count - 1)
+                def _():
+                    share_copy(layer, share_own).start()
+
+        def share_line(layer, z):
+            @pl.when((layer < z) & (z < count - 1))
+            def _():
+                share_copy(layer, share_own).wait_recv()
+                pltpu.sync_copy(share_own.at[layer], resid_x)
+                pltpu.sync_copy(share_landing.at[layer], resid_branch)
+                resid_x[...] = (resid_x[...].astype(F32) + resid_branch[...].astype(F32)).astype(
+                    BF16
+                )
+                pltpu.sync_copy(resid_x, share_sums.at[layer])
+                share_copy(layer, share_sums).start()
 
         def finish_output():
             own = pl.ds(pl.multiple_of(x * rows, rows), rows)
@@ -1188,112 +1343,79 @@
             out_sum.end(store)
             pltpu.sync_copy(resid_x, output)
 
-        events = [out_sum.corners, finish_output]
+        def hop_of(line, h, steps=(1, -1)):
+            return functools.partial(line.hop, h, steps)
+
+        events = [[] for _ in range(count)]
         for h in range(3, count):
-            events += [functools.partial(down_line.hop, h), functools.partial(up_line.hop, h)]
-        share = -(-len(events) // count)
-
-        @pl.loop(0, count)
+            events[min(h - 3, count - 2)].append(hop_of(down_line, h))
+            events[min(h - 2, count - 2)].append(hop_of(up_line, h))
+        attn_lines[0].hop(1)
+
+        def split_terms(in_ref, grad_ref, kv_ref, query_ref, key_ref, value_ref):
+            key_ref[...] = kv_ref[:, :local].astype(BF16)
+            value_ref[...] = kv_ref[:, local:].astype(BF16)
+            query_ref[...] = contract(in_ref[...], grad_ref[:, :local], ((0,), (0,))).astype(BF16)
+
+        def both(layer, act):
+            @pl.when(layer < z)
+            def _():
+                act(layer, False)
+
+            @pl.when(layer == z)
+            def _():
+                act(layer, True)
+
+        @pl.loop(0, z + 1)
         def _(layer):
-            @pl.when(layer < z)
-            def _():
-                stage(layer, False)
-                pltpu.sync_copy(grad_kv_low, kv_own.at[layer])
-
-                @pl.when(z == count - 1)
-                def _():
-                    kv_move(layer, kv_own).start()
-
-            @pl.when(layer == z)
-            def _():
-                stage(layer, True)
-
+            one, two = layer >= 1, layer >= 2
+            both(layer, functools.partial(attend_back, early=True))
+
+            @pl.when(layer == 0)
+            def _():
+                finish_output()
+
+            @pl.when(two)
+            def _():
+                keep_share(layer - 2, z)
+
+            @pl.when(one)
+            def _():
+                round_of(layer + 1).twins()
+
+            both(layer, functools.partial(attend_back, early=False))
             for k in range(count):
-                batch = events[k * share : (k + 1) * share]
-                if batch:
+                if events[k]:
 
                     @pl.when(layer == k)
                     def _():
-                        for event in batch:
+                        for event in events[k]:
                             event()
 
-        grad_kv_low[:, :local] = grad_query[...].astype(BF16)
-
-        def query_terms(in_ref, grad_ref, kv_ref, kv_out, query_out):
-            kv_out[...] = kv_ref[...].astype(BF16)
-            query_out[...] = contract(in_ref[...], grad_ref[:, :local], ((0,), (0,))).astype(BF16)
-
-        pltpu.emit_pipeline(
-            query_terms,
-            grid=(blocks,),
-            in_specs=[
-                column_spec(group),
-                whole_spec(group, 2 * local),
-                pl.BlockSpec((block, 2 * local), lambda i: (i, 0)),
-            ],
-            out_specs=[
-                pl.BlockSpec((block, 2 * local), lambda i: (i, 0)),
-                pl.BlockSpec((block, local), lambda i: (i, 2)),
-            ],
-        )(in_all.at[0], grad_kv_low, kv_weight, terms.at[2], terms.at[2])
-        attn_line.hop(1)
-
-        def kv_line(layer):
-            @pl.when((layer < z) & (z < count - 1))
-            def _():
-                kv_move(layer, kv_own).wait_recv()
-                add_rows(kv_own.at[layer], kv_landing.at[layer], kv_sums.at[layer])
-                kv_move(layer, kv_sums).start()
-
-        def add_rows(left, right, out):
-            def step(left_ref, right_ref, out_ref):
-                out_ref[...] = (left_ref[...].astype(F32) + right_ref[...].astype(F32)).astype(BF16)
-
-            pltpu.emit_pipeline(
-                step,
-                grid=(tiles,),
-                in_specs=[rows_spec(2 * local)] * 2,
-                out_specs=[rows_spec(2 * local)],
-            )(left, right, out)
-
-        home(0)
-        for h in range(2, count):
-            kv_line(h - 2)
-            attn_line.hop(h)
-            if h == 2:
-                home(1)
-        kv_line(count - 2)
-        first_sum.drain()
-
-        @pl.when(z < count - 1)
-        def _():
-            kv_move(z, kv_own).wait_recv()
-            pltpu.sync_copy(kv_landing.at[z], kv)
-
-        @pl.loop(0, tiles)
-        def _(i):
-            part = pl.ds(pl.multiple_of(i * tile, tile), tile)
-
-            @pl.when(z < count - 1)
-            def _():
-                grad_kv[part, :] += kv[part, :].astype(F32)
-
-            partial[part, :] = (
-                contract(grad_kv[part, :].astype(BF16), qkv_w[:, : 2 * local], ((1,), (1,)))
-                + contract(grad_query[part, :].astype(BF16), qkv_w[:, 2 * local :], ((1,), (1,)))
-            ).astype(BF16)
-
-        last_sum.start()
-        last_sum.twins()
-        attn_line.final(attn_grads.at[z, x])
-        spread.first()
-        last_sum.corners()
-        last_sum.end(store_into(last_gather))
-        last_gather.start()
-        last_gather.middle()
-        spread.hop(1)
-        last_gather.corner()
-        last_gather.end()
+            kv_terms(layer)
+
+            @pl.when(layer == z)
+            def _():
+                kv[:, :local] = grad_query[...].astype(BF16)
+                pltpu.emit_pipeline(
+                    split_terms,
+                    grid=(blocks,),
+                    in_specs=[
+                        column_spec(group),
+                        whole_spec(group, 2 * local),
+                        rows_spec(2 * local, block),
+                    ],
+                    out_specs=[rows_spec(local, block)] * 3,
+                )(in_all.at[0], kv, kv_weight, query_terms, key_terms, value_terms)
+                attn_lines[1].hop(1)
+
+            @pl.when(one)
+            def _():
+                round_of(layer + 1).corners()
+
+            round_of(layer).drain()
+            both(layer, back_to_rows)
+            round_of(layer + 2).start()
 
         def first_back(x_ref, grad_ref, resid_ref, out_ref):
             normed, inverse = normed_rows(x_ref[...].astype(F32))
@@ -1304,13 +1426,6 @@
             gains[0:1, :] += jnp.sum(grad * normed, axis=0, keepdims=True)
             wide[...] = inverse * (scaled - centre - normed * slope)
             out_ref[...] = resid_ref[...] + wide[:, own_column]
-
-        pltpu.emit_pipeline(
-            first_back,
-            grid=(group // thin,),
-            in_specs=[thin_spec, thin_spec, rows_spec(width, thin)],
-            out_specs=[rows_spec(width, thin)],
-        )(x_all.at[0], full3, grad_resid, input_grad)
 
         def gain_copy(step):
             to = lax.rem(z + step, count)
@@ -1323,10 +1438,88 @@
                 device_id_type=MESH,
             )
 
-        for step in range(1, count):
-            gain_copy(step).start()
-        for h in range(2, count):
-            spread.hop(h)
+        def take_rows_back():
+            pltpu.emit_pipeline(
+                first_back,
+                grid=(group // thin,),
+                in_specs=[thin_spec, thin_spec, rows_spec(width, thin)],
+                out_specs=[rows_spec(width, thin)],
+            )(x_all.at[0], full3, grad_resid, input_grad)
+            for step in range(1, count):
+                gain_copy(step).start()
+
+        def tail(z):
+            here = at.fixed(z)
+            down_here, up_here, *lines_here = lines_at(here)
+            spreads_here = spreads_at(here)
+            last = z + 2
+
+            def end_before():
+                @pl.when(z >= 1)
+                def _():
+                    keep_share(z - 1, z)
+
+            def own_share():
+                @pl.when(z < count - 1)
+                def _():
+                    share_copy(z, share_own).wait_recv()
+                    pltpu.sync_copy(share_landing.at[z], resid_branch)
+                    share[...] = share[...] + resid_branch[...].astype(F32)
+
+                last_gather.block(x, y, c)[...] = share[...].astype(BF16)
+                last_gather.start()
+
+            def rows_back():
+                last_gather.corner()
+                last_gather.end()
+                take_rows_back()
+
+            def final(k):
+                lines_here[k].final(attn_grads[k].at[z, x])
+                spreads_here[k].first()
+
+            todo = {
+                "end": end_before,
+                "twins": lambda: round_of(last).twins(),
+                "corners": lambda: round_of(last).corners(),
+                "keep": lambda: keep_share(z, z),
+                "home0": lambda: home(0, down_here),
+                "home1": lambda: home(1, up_here),
+                "own": own_share,
+                "middle": last_gather.middle,
+                "rows": rows_back,
+            }
+            for k in range(4):
+                if k > 1:
+                    todo[f"b{k}"] = hop_of(lines_here[k], 1)
+                for h in range(2, count):
+                    todo[f"u{k}{h}"] = hop_of(lines_here[k], h, (1,))
+                    todo[f"d{k}{h}"] = hop_of(lines_here[k], h, (-1,))
+                todo[f"f{k}"] = functools.partial(final, k)
+                for h in range(1, count):
+                    todo[f"U{k}{h}"] = functools.partial(spreads_here[k].hop, h, 1)
+                    todo[f"D{k}{h}"] = functools.partial(spreads_here[k].hop, h, -1)
+            for layer in range(count - 1):
+                todo[f"s{layer}"] = functools.partial(share_line, layer, z)
+            order = ORDERS.get((count, z)) if isinstance(z, int) else None
+            if order is None:
+                order = ["end", "twins", "corners", "keep", "home0", "b2", "b3", "home1"]
+                for k in range(4):
+                    order += [f"{way}{k}{h}" for h in range(2, count) for way in "ud"] + [f"f{k}"]
+                order += [f"s{layer}" for layer in range(count - 1)] + ["own", "middle", "rows"]
+                for k in range(4):
+                    order += [f"{way}{k}{h}" for h in range(1, count) for way in "UD"]
+            for name in order:
+                todo[name]()
+
+        if count <= 4:
+            for k in range(count):
+
+                @pl.when(z == k)
+                def _():
+                    tail(k)
+        else:
+            tail(z)
         gains_landing[z] = gains[...]
         for step in range(1, count):
             source = lax.rem(z + step, count)
@@ -1342,13 +1535,14 @@
             gain_copy(step).wait_send()
         gains[...] = jnp.sum(gains_landing[...], axis=0)
         pltpu.sync_copy(gains, gains_out)
-        spread.end()
+        for spread in spreads:
+            spread.end()
 
         @pl.loop(0, count)
         def _(layer):
             @pl.when(layer < z)
             def _():
-                kv_move(layer, kv_own).wait_send()
+                share_copy(layer, share_own).wait_send()
 
     pl.run_scoped(
         attention,
@@ -1368,25 +1562,25 @@
         pltpu.VMEM((thin, features), F32),
         pltpu.VMEM((rows, width), BF16),
         pltpu.VMEM((rows, width), BF16),
+        pltpu.VMEM((rows, width), F32),
     )
     for which in (0, 1):
         home_copy(which, True).wait_recv()
         home_copy(which).wait_send()
-    for line in (down_line, up_line, attn_line):
+    for line in (down_line, up_line, *attn_lines):
         line.drain()
-    out_sum.drain()
-    last_sum.drain()
+    round_of(z + 1).drain()
+    round_of(z + 2).drain()
     first_gather.drain()
     last_gather.drain()
 
 
 def back(count, *args):
-    (x_all, in_all, kv_all, query, *_, w_out, gain1, gain2, start_row, key_place) = args
-    down_all, w_query = args[9], args[11]
+    (x_all, _, _, query, *_, gain1, gain2, start_row, key_place) = args
+    down_all = args[9]
     _, group, features = x_all.shape
     rows = group // 2
     local = query.shape[1]
-    heads = local // HD
     hidden = down_all.shape[1]
     width = features // 4
     chunk = features // count
@@ -1396,6 +1590,7 @@
         return jax.ShapeDtypeStruct(shape, dtype)
 
     dma = pltpu.SemaphoreType.DMA
+    sizes = (hidden, hidden) + (local,) * 4
     return pl.pallas_call(
         functools.partial(back_kernel, count),
         name="back",
@@ -1404,44 +1599,81 @@
             out(group, width, dtype=F32),
             out(8, features, dtype=F32),
             out(2, 2, chunk // 2, hidden),
-            out(count, 2, chunk, 4 * local),
-            out(3, features, hidden),
-            out(3, count + 1, chunk, hidden),
-            out(3, count, chunk, hidden),
+            *[out(count, 2, chunk, local)] * 4,
+            *[out(features, size) for size in sizes],
+            *[out(count + 1, chunk, size) for size in sizes],
+            *[out(count, chunk, size) for size in sizes],
             out(2, chunk, hidden),
             out(group, features),
             out(group, width, dtype=F32),
-            out(count, group, 2 * local),
-            out(count, group, 2 * local),
-            out(count, group, 2 * local),
+            out(count, rows, width),
+            out(count, rows, width),
+            out(count, rows, width),
         ),
         in_specs=[hbm] * 15 + [vmem] * 4,
-        out_specs=[hbm] * 14,
+        out_specs=[hbm] * 32,
         scratch_shapes=[
+            pltpu.VMEM((2, group, features), BF16),
             pltpu.VMEM((group, features), BF16),
             pltpu.VMEM((group, features), BF16),
-            pltpu.VMEM((group, features), BF16),
-            pltpu.VMEM((group, features), BF16),
-            *reduce_scratch(rows, width),
-            *reduce_scratch(rows, width),
-            *reduce_scratch(rows, width),
+            pltpu.VMEM((3, 4, rows, width), BF16),
+            pltpu.VMEM((2, rows // 2, width), BF16),
+            pltpu.VMEM((2, rows // 2, width), BF16),
+            pltpu.VMEM((2, rows, width), BF16),
+            pltpu.VMEM((2, rows, width), BF16),
             pltpu.VMEM((8, features), F32),
             pltpu.VMEM((count, 8, features), F32),
             dma((8,)),
-            dma((3, 10)),
-            dma((3, 10)),
+            dma((count + 2, 10)),
+            dma((count + 2, 10)),
             dma((2, 9)),
             dma((2, 9)),
-            dma((3, count)),
-            dma((3, count + 1)),
+            dma((6, count)),
+            dma((6, count + 1)),
             dma((2,)),
             dma((2,)),
-            *[dma((count,))] * 9,
+            *[dma((4, count))] * 5,
+            *[dma((count,))] * 4,
         ],
         compiler_params=pltpu.CompilerParams(
             collective_id=1, has_side_effects=True, vmem_limit_bytes=60 * 1024 * 1024
         ),
     )(*args)
+
+
+def finish(mlp_grads, *attn_grads):
+    count, _, chunk, local = attn_grads[0].shape
+    half, hidden = mlp_grads.shape[2:]
+    steps = max(1, min(count, half // 16))
+    part, layers = half // steps, count // steps
+
+    def step(mlp_ref, *refs):
+        up_ref, down_ref = refs[8:]
+        for side in range(2):
+            span = slice(side * local, (side + 1) * local)
+            for source, target in zip(refs[:4], refs[4:8]):
+                for i in range(layers):
+                    target[i * chunk : (i + 1) * chunk, span] = source[i, side].astype(F32)
+            span = slice(side * hidden, (side + 1) * hidden)
+            down_ref[:, span] = mlp_ref[0, side].astype(F32)
+            up_ref[:, span] = mlp_ref[1, side].astype(F32)
+
+    def rows_of(tall, size):
+        return pl.BlockSpec((tall, size), lambda i: (i, 0))
+
+    return pl.pallas_call(
+        step,
+        name="finish",
+        grid=(steps,),
+        in_specs=[
+            pl.BlockSpec((2, 2, part, hidden), lambda i: (0, 0, i, 0)),
+            *[pl.BlockSpec((layers, 2, chunk, local), lambda i: (i, 0, 0, 0))] * 4,
+        ],
+        out_specs=[rows_of(layers * chunk, 2 * local)] * 4 + [rows_of(part, 2 * hidden)] * 2,
+        out_shape=[jax.ShapeDtypeStruct((count * chunk, 2 * local), F32)] * 4
+        + [jax.ShapeDtypeStruct((half, 2 * hidden), F32)] * 2,
+        compiler_params=pltpu.CompilerParams(vmem_limit_bytes=48 * 1024 * 1024),
+    )(mlp_grads, *attn_grads)
 
 
 def body(
@@ -1474,22 +1706,12 @@
         count, layer_input, out_grad, w_query, w_key, w_value, w_out, w_up, w_down,
         gain1, gain2, own_starts[:, None], key_place,
     )
-    output, input_grad, gains, mlp_grads, attn_grads, *_ = back(
+    output, input_grad, gains, mlp_grads, *rest = back(
         count, *kept, down_full.reshape(width, hidden), up_full.reshape(width, hidden),
         w_query, w_key, w_value, w_out, gain1, gain2, own_starts[None], key_place,
     )
-
-    def both_halves(first, size):
-        part = attn_grads[..., first : first + size].astype(F32)
-        return jnp.concatenate(
-            [part[:, 0].reshape(width, size), part[:, 1].reshape(width, size)], axis=1
-        )
-
-    key_grad, value_grad, query_grad, out_grad_w = (
-        both_halves(i * local, local) for i in range(4)
-    )
-    down_grad, up_grad = (
-        jnp.concatenate([mlp_grads[i, 0], mlp_grads[i, 1]], axis=1).astype(F32) for i in range(2)
+    out_grad_w, query_grad, key_grad, value_grad, up_grad, down_grad = finish(
+        mlp_grads, *rest[:4]
     )
     return (
         output,

time: 710 us -> 548 us (0.77)
  the two profiles are of different devices: /device:TPU:0 before, /device:TPU:25 now
where the time goes in v4:
time: 548 us; the launch traced here: 539 us
  Pallas kernels  528 us (96%)
  local copies, waits for them, and re-layouts  7.33 us (1%)
    pallas_call x1, Pallas kernels, back(): pl.pallas_call(functools.partial(back_kernel, count), name='back', out_sh...  338 us
    pallas_call x1, Pallas kernels, front(): pl.pallas_call(functools.partial(front_kernel, count), name='front', out_...  181 us

profile of v4, /device:TPU:25, one launch (start us, length us, event | category | flops | bytes accessed | tf_op | source)
XLA Modules:
  0.0 538.8 jit_solution(10314934444185470812)
XLA Ops:
  0.6 0.8 reduce-window.8
  1.5 0.1 select_reduce_fusion
  1.6 0.0 copy-start.3
  1.6 1.3 iota_select_fusion
  3.0 1.0 copy.23.start_of
  4.0 181.0 %front.1 = (bf16[4,1024,2048]{2,1,0:T(8,128)(2,1)}, bf16[4,1024,2048]{2,1,0:T(8,128)(2,1)}, bf16[4,1024,512]{2,1,0:T(8,128)(2,1)}, bf16[1024,256]{1,0:T(8,128)(2...) custom-call(bf16[512,512]{1,0:T(8,128)(2,1)} %xs.1, ...), custom_call_target="tpu_custom_call" | custom-call | tf_op jit(solution)/shard_map/front/pallas_call | solution.py:692
  185.0 0.0 copy-done.3
  185.0 337.9 %back.1 = (bf16[512,512]{1,0:T(8,128)(2,1)}, f32[1024,512]{1,0:T(8,128)}, f32[8,2048]{1,0:T(8,128)}, bf16[2,2,256,1024]{3,2,1,0:T(8,128)(2,1)}, bf16[4,2,512,256...) custom-call(bf16[4,1024,2048]{2,1,0:T(8,128)(2,1)} %get-tuple-elemen, ...), custom_call_target="tpu_custom_call" | custom-call | tf_op jit(solution)/shard_map/back/pallas_call | solution.py:1594
  522.9 0.0 copy-start
  522.9 1.6 fusion
  524.6 2.3 constant_dynamic-slice_fusion
  526.8 0.0 copy-done
  526.8 0.0 copy-start.1
  526.8 1.6 copy-done.1
  528.4 0.0 copy-start.2
  528.4 9.3 %finish.1 = (f32[2048,512]{1,0:T(8,128)}, f32[2048,512]{1,0:T(8,128)}, f32[2048,512]{1,0:T(8,128)}, f32[2048,512]{1,0:T(8,128)}, f32[256,2048]{1,0:T(8,128)}, /*index=5*/f32[256,2048]{1,0:T(8,128)}) custom-call(bf16[2,2,256,1024]{3,2,1,0:T(8,128)(2,1)S(1)} %copy-done, bf16[4,2,512,256]{3,2,1,0:T(8,128)(2,1)S(1)} %copy-done.1, ...), custom_call_target="tpu_custom_call" | custom-call | tf_op jit(solution)/shard_map/finish/pallas_call | solution.py:1664
  537.7 0.0 copy-done.2
  537.7 0.8 copy.25
  (1 shorter events, 0.0 us)
Async XLA Ops:
  1.6 183.3 %copy-start.3 = (s32[1024]{0:T(1024)}, s32[1024]{0:T(1024)S(1)}, u32[]{:S(2)}) copy-start(s32[1024]{0:T(1024)S(1)} %dynamic_slice.6) | copy-start | bytes 12292
  522.9 3.9 copy-start
  526.8 1.6 copy-start.1
  528.4 9.3 %copy-start.2 = (bf16[512,512]{1,0:T(8,128)(2,1)S(1)}, bf16[512,512]{1,0:T(8,128)(2,1)}, u32[]{:S(2)}) copy-start(bf16[512,512]{1,0:T(8,128)(2,1)} %get-tuple-element.72) | copy-start | bytes 1572868

commit v5 on v4

--- a/solution.py
+++ b/solution.py
@@ -17,6 +17,20 @@
 
 MESH = pl.DeviceIdType.MESH
 LOG2E = 1.4426950408889634
+
+
+def clip_start(position, clip_lengths):
+    end, start = jnp.int32(0), jnp.zeros_like(position)
+    for clip in range(clip_lengths.shape[0]):
+        end = end + clip_lengths[clip]
+        start = jnp.where(position >= end, end, start)
+    return start
+
+
+def place_keys(key_place, key_padding, count, group):
+    for layer in range(count):
+        position = lax.broadcasted_iota(jnp.int32, (1, group), 1) + layer * group
+        key_place[layer] = jnp.where(key_padding[layer] > 0, position, -1)
 
 
 def remote(src, dst, sends, recvs, slot, **device):
@@ -64,7 +78,10 @@
                     device_id={"z": lax.rem(self.z + step, self.count)},
                     device_id_type=MESH,
                 )
-            pl.semaphore_wait(barrier, 3 + self.count - 1)
+            pl.semaphore_signal(
+                barrier, inc=1, device_id={"y": self.oy, "core": self.oc}, device_id_type=MESH
+            )
+            pl.semaphore_wait(barrier, 4 + self.count - 1)
             return
         above, below = self.z < self.count - 1, self.z > 0
         for there, step in ((above, 1), (below, -1)):
@@ -136,9 +153,9 @@
 
 
 class Reduce:
-    def __init__(self, at, array, rows, width, buffers, sends, recvs):
+    def __init__(self, at, array, rows, width, buffers, sends, recvs, by_y=False):
         self.at, self.array, self.sends, self.recvs = at, array, sends, recvs
-        self.rows, self.width = rows, width
+        self.rows, self.width, self.by_y = rows, width, by_y
         self.twin, self.corner_x, self.corner_y, self.from_x, self.from_y = buffers
 
     def block(self, xi, yi, ci, first=0, size=None):
@@ -154,7 +171,7 @@
             2: ((x, oy, oc), self.twin.at[2], {"core": oc}),
             3: ((x, y, oc), self.twin.at[3], {"core": oc}),
             4: ((ox, oy, c, 0, half), self.corner_y, {"y": oy}),
-            5: ((ox, oy, c, half, half), self.corner_x, {"x": ox}),
+            5: ((ox, oy, c, half, half), self.corner_x, {"y": oy} if self.by_y else {"x": ox}),
             6: ((ox, y, c, half, half), self.from_x.at[high], {"x": ox}),
             7: ((x, oy, c, 0, half), self.from_y.at[low], {"y": oy}),
             8: ((ox, y, c, 0, half), self.from_x.at[low], {"x": ox}),
@@ -187,10 +204,13 @@
         self.copy(5).start()
         self.copy(1).wait_recv()
         self.add(self.block(ox, y, c), self.twin.at[1])
-        self.copy(6).start()
+        if not self.by_y:
+            self.copy(6).start()
         self.copy(2).wait_recv()
         self.add(self.block(x, oy, c), self.twin.at[2])
         self.copy(7).start()
+        if self.by_y:
+            self.copy(9).start()
         self.copy(3).wait_recv()
 
     def corners(self):
@@ -199,8 +219,12 @@
         self.add(self.block(at.ox, at.y, at.c, 0, half), self.corner_y)
         self.copy(8).start()
         self.copy(5).wait_recv()
-        self.add(self.block(at.x, at.oy, at.c, half, half), self.corner_x)
-        self.copy(9).start()
+        if self.by_y:
+            self.add(self.block(at.ox, at.y, at.c, half, half), self.corner_x)
+            self.copy(6).start()
+        else:
+            self.add(self.block(at.x, at.oy, at.c, half, half), self.corner_x)
+            self.copy(9).start()
 
     def end(self, store):
         for k in (6, 7, 8, 9):
@@ -330,8 +354,8 @@
     w_down,
     gain1,
     gain2,
-    start_of,
-    key_place,
+    clip_lengths,
+    key_padding,
     x_all,
     in_all,
     kv_all,
@@ -343,6 +367,8 @@
     og_all,
     down_all,
     up_all,
+    start_of,
+    key_place,
     qkv_w,
     out_w,
     query,
@@ -427,6 +453,9 @@
     ]
     for copy in into + loads:
         copy.start()
+    position = lax.broadcasted_iota(jnp.int32, (group, 1), 0) + z * group
+    start_of[...] = clip_start(position, clip_lengths)
+    place_keys(key_place, key_padding, count, group)
     for first, second in zip(into, onto):
         first.wait()
         second.start()
@@ -676,14 +705,17 @@
             line_copy(d).wait_send()
 
 
-def front(count, xs, og, w_query, w_key, w_value, w_out, w_up, w_down, gain1, gain2, start_of, key_place):
+def front(count, xs, og, *args):
+    w_query, w_up, gain1 = args[0], args[4], args[6]
     rows, width = xs.shape
     group, features = 2 * rows, gain1.shape[1]
     local = w_query.shape[1] // 2
     heads = local // HD
     hidden = w_up.shape[1] // 2
     w_rows = w_up.shape[0]
-    hbm, vmem = pl.BlockSpec(memory_space=pl.ANY), pl.BlockSpec(memory_space=pltpu.VMEM)
+    hbm, vmem, smem = (
+        pl.BlockSpec(memory_space=space) for space in (pl.ANY, pltpu.VMEM, pltpu.SMEM)
+    )
 
     def out(*shape, dtype=BF16):
         return jax.ShapeDtypeStruct(shape, dtype)
@@ -705,9 +737,11 @@
             out(count, 2, w_rows, hidden),
             out(count, 2, w_rows, hidden),
         ),
-        in_specs=[hbm] * 8 + [vmem] * 4,
+        in_specs=[hbm] * 8 + [vmem] * 2 + [smem, vmem],
         out_specs=[hbm] * 11,
         scratch_shapes=[
+            pltpu.VMEM((group, 1), jnp.int32),
+            pltpu.VMEM((count, 1, group), jnp.int32),
             pltpu.VMEM((features, 3 * local), BF16),
             pltpu.VMEM((features, local), BF16),
             pltpu.VMEM((group, local), BF16),
@@ -736,7 +770,7 @@
         compiler_params=pltpu.CompilerParams(
             collective_id=0, has_side_effects=True, vmem_limit_bytes=56 * 1024 * 1024
         ),
-    )(xs, og, w_query, w_key, w_value, w_out, w_up, w_down, gain1, gain2, start_of, key_place)
+    )(xs, og, *args)
 
 
 class LineSum:
@@ -899,26 +933,26 @@
 
 ORDERS = {
     (4, 0): (
-        "b2", "b3", "twins", "corners", "home0", "keep", "home1", "f0", "D01", "D02", "own",
-        "f1", "middle", "D11", "D12", "f2", "D21", "D22", "f3", "D31", "D32", "D03", "D13",
-        "D23", "D33", "rows",
+        "b2", "b3", "twins", "corners", "home0", "keep", "home1", "f0", "D01", "D02", "norm",
+        "own", "rows", "columns", "f1", "D11", "D12", "f2", "D21", "D22", "f3", "D31", "D32",
+        "D03", "D13", "D23", "D33", "gains",
     ),
     (4, 1): (
         "home0", "end", "twins", "u02", "home1", "u03", "corners", "u12", "u13", "d03", "f0",
-        "u22", "keep", "D01", "u23", "s0", "u32", "u33", "own", "d13", "U01", "f1", "middle",
-        "D11", "U11", "d23", "f2", "D21", "d33", "U21", "f3", "D31", "D02", "U31", "D12",
-        "D22", "D32", "rows",
+        "u22", "keep", "D01", "u23", "norm", "s0", "u32", "u33", "own", "rows", "columns",
+        "d13", "U01", "gains", "f1", "D11", "d23", "U11", "f2", "D21", "d33", "U21", "f3",
+        "D31", "D02", "U31", "D12", "D22", "D32",
     ),
     (4, 2): (
-        "home0", "d02", "home1", "d03", "u03", "f0", "end", "twins", "s0", "u13", "s1", "d12",
-        "U01", "d13", "u23", "f1", "corners", "d22", "u33", "d23", "f2", "d32", "U02", "keep",
-        "d33", "U11", "f3", "U12", "own", "U21", "D01", "D11", "D21", "middle", "U31", "D31",
-        "U22", "U32", "rows",
+        "d02", "home1", "d03", "u03", "f0", "s0", "end", "twins", "u13", "s1", "d12", "U01",
+        "d13", "u23", "corners", "f1", "d22", "u33", "d23", "keep", "f2", "d32", "U02", "d33",
+        "U11", "f3", "norm", "D01", "U12", "U21", "own", "rows", "columns", "D11", "gains",
+        "D21", "U31", "D31", "U22", "U32",
     ),
     (4, 3): (
-        "b2", "b3", "home0", "home1", "end", "twins", "f0", "U01", "f1", "U02", "corners",
-        "f2", "U11", "f3", "U21", "keep", "own", "U03", "U12", "U31", "U13", "middle", "U22",
-        "U32", "U23", "rows", "U33",
+        "b2", "b3", "norm", "f0", "U01", "end", "s2", "twins", "f1", "U02", "f2", "U11",
+        "corners", "f3", "U21", "keep", "own", "rows", "U12", "columns", "gains", "U31", "U03",
+        "U22", "U13", "U32", "U23", "U33",
     ),
 }
 
@@ -942,8 +976,8 @@
     w_out,
     gain1,
     gain2,
-    start_row,
-    key_place,
+    clip_lengths,
+    key_padding,
     output,
     input_grad,
     gains_out,
@@ -976,9 +1010,15 @@
     share_own,
     share_landing,
     share_sums,
+    start_row,
+    key_place,
     partials,
     full1,
-    full3,
+    stat_own,
+    stat_in,
+    part_own,
+    part_x,
+    part_in,
     twin,
     corner_x,
     corner_y,
@@ -1004,6 +1044,10 @@
     share_recv,
     gain_send,
     gain_recv,
+    stat_send,
+    stat_recv,
+    part_send,
+    part_recv,
 ):
     at = Place(count)
     z, x, y, c = at.z, at.x, at.y, at.c
@@ -1033,21 +1077,28 @@
     def whole_spec(*shape):
         return pl.BlockSpec(shape, lambda i: (0,) * len(shape))
 
-    def round_of(r):
+    def round_of(r, by_y=False):
         p = r % 2 if isinstance(r, int) else lax.rem(r, 2)
         third = r % 3 if isinstance(r, int) else lax.rem(r, 3)
         buffers = (twin.at[third],) + tuple(
             b.at[p] for b in (corner_x, corner_y, from_x, from_y)
         )
         return Reduce(
-            at, partials.at[p], rows, width, buffers, reduce_send.at[r], reduce_recv.at[r]
+            at,
+            partials.at[p],
+            rows,
+            width,
+            buffers,
+            reduce_send.at[r],
+            reduce_recv.at[r],
+            by_y,
         )
 
     def gather_of(array, k):
         return Gather(at, array, rows, width, gather_send, gather_recv, (k,))
 
-    first_sum, out_sum = round_of(0), round_of(1)
-    first_gather, last_gather = gather_of(full1, 0), gather_of(full3, 1)
+    first_sum, out_sum = round_of(0, False), round_of(1, False)
+    first_gather = gather_of(full1, 0)
     attn_grads = (out_grads, query_grads, key_grads, value_grads)
 
     def lines_at(at):
@@ -1126,6 +1177,9 @@
         ]
         for load in loads:
             load.start()
+        position = lax.broadcasted_iota(jnp.int32, (1, group), 1) + z * group
+        start_row[...] = clip_start(position, clip_lengths)
+        place_keys(key_place, key_padding, count, group)
         at.meet(whole_line=True)
         for load in loads:
             load.wait()
@@ -1147,7 +1201,7 @@
             in_specs=[rows_spec(features)] * 2,
             out_specs=[rows_spec(hidden)] * 2,
         )(mlp_in, og_all, active, grad_up)
-        first = jnp.where(z == 0, count - 1, 0)
+        first = pick(z == 0, count - 1, 0)
         weight_terms(down_terms, og_all, active, first, 1)
         down_line.hop(1)
         weight_terms(up_terms, mlp_in, grad_up, first, 1)
@@ -1188,7 +1242,7 @@
 
     def attention(
         qkv_w, out_w, query, attended, kv, grad_att, grad_query, grad_kv, grad_kv_low, kv_weight,
-        logs, log_row, delta_row, wide, resid_x, resid_branch, share,
+        logs, log_row, delta_row, wide, resid_x, resid_branch, share, resid, normed1, inverse1,
     ):
         loads = [
             pltpu.make_async_copy(
@@ -1315,11 +1369,17 @@
                 resid_x[...] = share[...].astype(BF16)
                 pltpu.sync_copy(resid_x, share_own.at[layer])
 
+                @pl.when((z == count - 1) & (layer < z - 1))
+                def _():
+                    share_copy(layer, share_own).start()
+
+        def share_line(layer, z):
+            if layer == count - 2:
+
                 @pl.when(z == count - 1)
                 def _():
                     share_copy(layer, share_own).start()
 
-        def share_line(layer, z):
             @pl.when((layer < z) & (z < count - 1))
             def _():
                 share_copy(layer, share_own).wait_recv()
@@ -1350,6 +1410,10 @@
         for h in range(3, count):
             events[min(h - 3, count - 2)].append(hop_of(down_line, h))
             events[min(h - 2, count - 2)].append(hop_of(up_line, h))
+        if count > 3:
+            events[count - 2].append(functools.partial(home, 0, down_line))
+        if count == 4:
+            events[count - 1].append(functools.partial(home, 1, up_line))
         attn_lines[0].hop(1)
 
         def split_terms(in_ref, grad_ref, kv_ref, query_ref, key_ref, value_ref):
@@ -1417,15 +1481,79 @@
             both(layer, back_to_rows)
             round_of(layer + 2).start()
 
-        def first_back(x_ref, grad_ref, resid_ref, out_ref):
-            normed, inverse = normed_rows(x_ref[...].astype(F32))
-            grad = grad_ref[...].astype(F32)
-            scaled = grad * gain1[...]
-            centre = jnp.mean(scaled, axis=1, keepdims=True)
-            slope = jnp.mean(scaled * normed, axis=1, keepdims=True)
-            gains[0:1, :] += jnp.sum(grad * normed, axis=0, keepdims=True)
-            wide[...] = inverse * (scaled - centre - normed * slope)
-            out_ref[...] = resid_ref[...] + wide[:, own_column]
+        own_rows = pl.ds(pl.multiple_of(x * rows, rows), rows)
+
+        def first_norm():
+            def step(x_ref, normed_ref, inverse_ref):
+                normed, inverse = normed_rows(x_ref[...].astype(F32))
+                wide[...] = normed
+                normed_ref[...] = wide[:, own_column]
+                inverse_ref[...] = jnp.broadcast_to(inverse, inverse_ref.shape)
+
+            pltpu.emit_pipeline(
+                step,
+                grid=(rows // thin,),
+                in_specs=[rows_spec(features, thin)],
+                out_specs=[rows_spec(width, thin), rows_spec(HD, thin)],
+            )(x_all.at[0, own_rows], normed1, inverse1)
+            pltpu.sync_copy(grad_resid.at[own_rows], resid)
+
+        def beside(k):
+            return ({"core": at.oc}, {"y": at.oy}, {"y": at.oy, "core": at.oc})[k]
+
+        def stat_copy(k):
+            return remote(stat_own, stat_in.at[k], stat_send, stat_recv, (k,), **beside(k))
+
+        def part_copy(k):
+            return remote(part_own, part_in.at[k], part_send, part_recv, (k,), **beside(k))
+
+        def part_across():
+            return remote(part_own, part_x, part_send, part_recv, (3,), x=at.ox)
+
+        def row_stats():
+            grad = share[...]
+            scaled = grad * gain1[:, own_column]
+            lane = lax.broadcasted_iota(jnp.int32, (rows, HD), 1)
+            first = jnp.sum(scaled, axis=1, keepdims=True)
+            second = jnp.sum(scaled * normed1[...], axis=1, keepdims=True)
+            both_sums = jnp.where(lane == 0, first, jnp.where(lane == 1, second, 0.0))
+            stat_own[...] = jnp.transpose(both_sums)[:8]
+            for k in range(3):
+                stat_copy(k).start()
+            part_own[...] = jnp.broadcast_to(
+                jnp.sum(grad * normed1[...], axis=0, keepdims=True), part_own.shape
+            )
+            part_across().start()
+
+        def rows_back():
+            for k in range(3):
+                stat_copy(k).wait_recv()
+            sums = (stat_own[...] + stat_in[0] + stat_in[1] + stat_in[2]) * (1.0 / features)
+            sums = jnp.transpose(jnp.concatenate([sums] * (HD // 8), axis=0))
+            centre, slope = sums[:, :1], sums[:, 1:2]
+            scaled = share[...] * gain1[:, own_column]
+            share[...] = resid[...] + inverse1[:, :1] * (
+                scaled - centre - normed1[...] * slope
+            )
+            pltpu.sync_copy(share, input_grad)
+
+        def gain_columns():
+            part_across().wait_recv()
+            part_across().wait_send()
+            part_own[...] = part_own[...] + part_x[...]
+            for k in range(3):
+                part_copy(k).start()
+
+        def gain_line():
+            def column_of(yi, ci):
+                return pl.ds(pl.multiple_of((2 * yi + ci) * width, width), width)
+
+            gains[0:1, own_column] = part_own[:1]
+            for k, (yi, ci) in enumerate(((y, at.oc), (at.oy, c), (at.oy, at.oc))):
+                part_copy(k).wait_recv()
+                gains[0:1, column_of(yi, ci)] = part_in[k, :1]
+            for step in range(1, count):
+                gain_copy(step).start()
 
         def gain_copy(step):
             to = lax.rem(z + step, count)
@@ -1438,21 +1566,11 @@
                 device_id_type=MESH,
             )
 
-        def take_rows_back():
-            pltpu.emit_pipeline(
-                first_back,
-                grid=(group // thin,),
-                in_specs=[thin_spec, thin_spec, rows_spec(width, thin)],
-                out_specs=[rows_spec(width, thin)],
-            )(x_all.at[0], full3, grad_resid, input_grad)
-            for step in range(1, count):
-                gain_copy(step).start()
-
         def tail(z):
             here = at.fixed(z)
             down_here, up_here, *lines_here = lines_at(here)
             spreads_here = spreads_at(here)
-            last = z + 2
+            last = at.z + 2
 
             def end_before():
                 @pl.when(z >= 1)
@@ -1466,13 +1584,7 @@
                     pltpu.sync_copy(share_landing.at[z], resid_branch)
                     share[...] = share[...] + resid_branch[...].astype(F32)
 
-                last_gather.block(x, y, c)[...] = share[...].astype(BF16)
-                last_gather.start()
-
-            def rows_back():
-                last_gather.corner()
-                last_gather.end()
-                take_rows_back()
+                row_stats()
 
             def final(k):
                 lines_here[k].final(attn_grads[k].at[z, x])
@@ -1483,11 +1595,13 @@
                 "twins": lambda: round_of(last).twins(),
                 "corners": lambda: round_of(last).corners(),
                 "keep": lambda: keep_share(z, z),
-                "home0": lambda: home(0, down_here),
-                "home1": lambda: home(1, up_here),
+                "home0": lambda: pl.when(count < 4 or z < count - 2)(lambda: home(0, down_here)),
+                "home1": lambda: pl.when(count != 4 or z < count - 1)(lambda: home(1, up_here)),
+                "norm": first_norm,
                 "own": own_share,
-                "middle": last_gather.middle,
                 "rows": rows_back,
+                "columns": gain_columns,
+                "gains": gain_line,
             }
             for k in range(4):
                 if k > 1:
@@ -1506,7 +1620,8 @@
                 order = ["end", "twins", "corners", "keep", "home0", "b2", "b3", "home1"]
                 for k in range(4):
                     order += [f"{way}{k}{h}" for h in range(2, count) for way in "ud"] + [f"f{k}"]
-                order += [f"s{layer}" for layer in range(count - 1)] + ["own", "middle", "rows"]
+                order += [f"s{layer}" for layer in range(count - 1)] + ["norm", "own", "rows"]
+                order += ["columns", "gains"]
                 for k in range(4):
                     order += [f"{way}{k}{h}" for h in range(1, count) for way in "UD"]
             for name in order:
@@ -1533,6 +1648,9 @@
             ).wait_recv()
         for step in range(1, count):
             gain_copy(step).wait_send()
+        for k in range(3):
+            stat_copy(k).wait_send()
+            part_copy(k).wait_send()
         gains[...] = jnp.sum(gains_landing[...], axis=0)
         pltpu.sync_copy(gains, gains_out)
         for spread in spreads:
@@ -1563,6 +1681,9 @@
         pltpu.VMEM((rows, width), BF16),
         pltpu.VMEM((rows, width), BF16),
         pltpu.VMEM((rows, width), F32),
+        pltpu.VMEM((rows, width), F32),
+        pltpu.VMEM((rows, width), F32),
+        pltpu.VMEM((rows, HD), F32),
     )
     for which in (0, 1):
         home_copy(which, True).wait_recv()
@@ -1572,19 +1693,19 @@
     round_of(z + 1).drain()
     round_of(z + 2).drain()
     first_gather.drain()
-    last_gather.drain()
 
 
 def back(count, *args):
-    (x_all, _, _, query, *_, gain1, gain2, start_row, key_place) = args
-    down_all = args[9]
+    x_all, query, down_all = args[0], args[3], args[9]
     _, group, features = x_all.shape
     rows = group // 2
     local = query.shape[1]
     hidden = down_all.shape[1]
     width = features // 4
     chunk = features // count
-    hbm, vmem = pl.BlockSpec(memory_space=pl.ANY), pl.BlockSpec(memory_space=pltpu.VMEM)
+    hbm, vmem, smem = (
+        pl.BlockSpec(memory_space=space) for space in (pl.ANY, pltpu.VMEM, pltpu.SMEM)
+    )
 
     def out(*shape, dtype=BF16):
         return jax.ShapeDtypeStruct(shape, dtype)
@@ -1596,7 +1717,7 @@
         name="back",
         out_shape=(
             out(rows, width),
-            out(group, width, dtype=F32),
+            out(rows, width, dtype=F32),
             out(8, features, dtype=F32),
             out(2, 2, chunk // 2, hidden),
             *[out(count, 2, chunk, local)] * 4,
@@ -1610,12 +1731,18 @@
             out(count, rows, width),
             out(count, rows, width),
         ),
-        in_specs=[hbm] * 15 + [vmem] * 4,
+        in_specs=[hbm] * 15 + [vmem] * 2 + [smem, vmem],
         out_specs=[hbm] * 32,
         scratch_shapes=[
+            pltpu.VMEM((1, group), jnp.int32),
+            pltpu.VMEM((count, 1, group), jnp.int32),
             pltpu.VMEM((2, group, features), BF16),
             pltpu.VMEM((group, features), BF16),
-            pltpu.VMEM((group, features), BF16),
+            pltpu.VMEM((8, rows), F32),
+            pltpu.VMEM((3, 8, rows), F32),
+            pltpu.VMEM((8, width), F32),
+            pltpu.VMEM((8, width), F32),
+            pltpu.VMEM((3, 8, width), F32),
             pltpu.VMEM((3, 4, rows, width), BF16),
             pltpu.VMEM((2, rows // 2, width), BF16),
             pltpu.VMEM((2, rows // 2, width), BF16),
@@ -1626,14 +1753,16 @@
             dma((8,)),
             dma((count + 2, 10)),
             dma((count + 2, 10)),
-            dma((2, 9)),
-            dma((2, 9)),
+            dma((1, 9)),
+            dma((1, 9)),
             dma((6, count)),
             dma((6, count + 1)),
             dma((2,)),
             dma((2,)),
             *[dma((4, count))] * 5,
             *[dma((count,))] * 4,
+            *[dma((3,))] * 2,
+            *[dma((4,))] * 2,
         ],
         compiler_params=pltpu.CompilerParams(
             collective_id=1, has_side_effects=True, vmem_limit_bytes=60 * 1024 * 1024
@@ -1641,19 +1770,27 @@
     )(*args)
 
 
-def finish(mlp_grads, *attn_grads):
+def finish(output, input_grad, gains, mlp_grads, *attn_grads):
     count, _, chunk, local = attn_grads[0].shape
     half, hidden = mlp_grads.shape[2:]
-    steps = max(1, min(count, half // 16))
-    part, layers = half // steps, count // steps
-
-    def step(mlp_ref, *refs):
-        up_ref, down_ref = refs[8:]
+    steps = max(1, min(2 * count, half // 16))
+    part, layers = half // steps, max(count // steps, 1)
+    pieces = max(steps // count, 1)
+    tall = chunk // pieces
+    rows, width = output.shape
+
+    def step(output_ref, input_ref, gains_ref, mlp_ref, *refs):
+        sources, targets = refs[:4], refs[4:8]
+        up_ref, down_ref, output_out, input_out, gain1_out, gain2_out = refs[8:]
+        output_out[...] = output_ref[...]
+        input_out[...] = input_ref[...]
+        gain1_out[...] = gains_ref[0:1]
+        gain2_out[...] = gains_ref[1:2]
         for side in range(2):
             span = slice(side * local, (side + 1) * local)
-            for source, target in zip(refs[:4], refs[4:8]):
+            for source, target in zip(sources, targets):
                 for i in range(layers):
-                    target[i * chunk : (i + 1) * chunk, span] = source[i, side].astype(F32)
+                    target[i * tall : (i + 1) * tall, span] = source[i, side].astype(F32)
             span = slice(side * hidden, (side + 1) * hidden)
             down_ref[:, span] = mlp_ref[0, side].astype(F32)
             up_ref[:, span] = mlp_ref[1, side].astype(F32)
@@ -1661,19 +1798,40 @@
     def rows_of(tall, size):
         return pl.BlockSpec((tall, size), lambda i: (i, 0))
 
+    def whole(*shape):
+        return pl.BlockSpec(shape, lambda i: (0, 0))
+
+    share = rows_of(rows // steps, width)
+    gain = jax.ShapeDtypeStruct((1, gains.shape[1]), F32)
     return pl.pallas_call(
         step,
         name="finish",
         grid=(steps,),
         in_specs=[
+            share,
+            share,
+            whole(*gains.shape),
             pl.BlockSpec((2, 2, part, hidden), lambda i: (0, 0, i, 0)),
-            *[pl.BlockSpec((layers, 2, chunk, local), lambda i: (i, 0, 0, 0))] * 4,
+            *[
+                pl.BlockSpec(
+                    (layers, 2, tall, local), lambda i: (i // pieces, 0, i % pieces, 0)
+                )
+            ]
+            * 4,
         ],
-        out_specs=[rows_of(layers * chunk, 2 * local)] * 4 + [rows_of(part, 2 * hidden)] * 2,
+        out_specs=[rows_of(layers * tall, 2 * local)] * 4
+        + [rows_of(part, 2 * hidden)] * 2
+        + [share, share, whole(*gain.shape), whole(*gain.shape)],
         out_shape=[jax.ShapeDtypeStruct((count * chunk, 2 * local), F32)] * 4
-        + [jax.ShapeDtypeStruct((half, 2 * hidden), F32)] * 2,
-        compiler_params=pltpu.CompilerParams(vmem_limit_bytes=48 * 1024 * 1024),
-    )(mlp_grads, *attn_grads)
+        + [jax.ShapeDtypeStruct((half, 2 * hidden), F32)] * 2
+        + [
+            jax.ShapeDtypeStruct(output.shape, output.dtype),
+            jax.ShapeDtypeStruct(input_grad.shape, input_grad.dtype),
+            gain,
+            gain,
+        ],
+        compiler_params=pltpu.CompilerParams(vmem_limit_bytes=62 * 1024 * 1024),
+    )(output, input_grad, gains, mlp_grads, *attn_grads)
 
 
 def body(
@@ -1691,37 +1849,31 @@
     out_grad,
 ):
     count = lax.axis_size("z")
-    z, x = lax.axis_index("z"), lax.axis_index("x")
     rows = layer_input.shape[0]
     width = w_query.shape[0]
-    local = w_query.shape[1] // 2
     hidden = w_up.shape[1] // 2
-    clip_ends = jnp.cumsum(clip_lengths)
-    position = jnp.arange(key_padding.shape[0], dtype=jnp.int32)
-    starts = jnp.max(jnp.where(position[:, None] >= clip_ends, clip_ends, 0), axis=1)
-    key_place = jnp.where(key_padding > 0, position, -1).reshape(count, 1, 2 * rows)
-    own_starts = lax.dynamic_slice_in_dim(starts, z * 2 * rows, 2 * rows)
     gain1, gain2 = norm1_gain[None], norm2_gain[None]
+    key_padding = key_padding.reshape(count, 1, 2 * rows)
     *kept, down_full, up_full = front(
         count, layer_input, out_grad, w_query, w_key, w_value, w_out, w_up, w_down,
-        gain1, gain2, own_starts[:, None], key_place,
+        gain1, gain2, clip_lengths, key_padding,
     )
-    output, input_grad, gains, mlp_grads, *rest = back(
+    results = back(
         count, *kept, down_full.reshape(width, hidden), up_full.reshape(width, hidden),
-        w_query, w_key, w_value, w_out, gain1, gain2, own_starts[None], key_place,
+        w_query, w_key, w_value, w_out, gain1, gain2, clip_lengths, key_padding,
     )
-    out_grad_w, query_grad, key_grad, value_grad, up_grad, down_grad = finish(
-        mlp_grads, *rest[:4]
-    )
+    grads = finish(*results[:8])
+    out_grad_w, query_grad, key_grad, value_grad, up_grad, down_grad = grads[:6]
+    output, input_grad, gain1_grad, gain2_grad = grads[6:]
     return (
         output,
-        lax.dynamic_slice_in_dim(input_grad, x * rows, rows, 0),
-        gains[0],
+        input_grad,
+        gain1_grad[0],
         query_grad,
         key_grad,
         value_grad,
         out_grad_w,
-        gains[1],
+        gain2_grad[0],
         up_grad,
         down_grad,
     )

time: 548 us -> 537 us (0.980)
  the two profiles are of different devices: /device:TPU:25 before, /device:TPU:0 now
where the time goes in v5:
time: 537 us; the launch traced here: 528 us
  Pallas kernels  527 us (98%)
    pallas_call x1, Pallas kernels, back(): pl.pallas_call(functools.partial(back_kernel, count), name='back', out_sh...  332 us
    pallas_call x1, Pallas kernels, front(): pl.pallas_call(functools.partial(front_kernel, count), name='front', out_...  182 us
    pallas_call x1, Pallas kernels, finish(): pl.pallas_call(step, name='finish', grid=(steps,), in_specs=[share, share...  13.1 us

profile of v5, /device:TPU:0, one launch (start us, length us, event | category | flops | bytes accessed | tf_op | source)
XLA Modules:
  0.0 527.6 jit_solution(3037126990189682175)
XLA Ops:
  0.6 181.8 %front.1 = (bf16[4,1024,2048]{2,1,0:T(8,128)(2,1)}, bf16[4,1024,2048]{2,1,0:T(8,128)(2,1)}, bf16[4,1024,512]{2,1,0:T(8,128)(2,1)}, bf16[1024,256]{1,0:T(8,128)(2...) custom-call(bf16[512,512]{1,0:T(8,128)(2,1)} %xs.1, ...), custom_call_target="tpu_custom_call" | custom-call | tf_op jit(solution)/shard_map/front/pallas_call | solution.py:724
  182.5 331.6 %back.1 = (bf16[512,512]{1,0:T(8,128)(2,1)}, f32[512,512]{1,0:T(8,128)}, f32[8,2048]{1,0:T(8,128)}, bf16[2,2,256,1024]{3,2,1,0:T(8,128)(2,1)}, bf16[4,2,512,256]...) custom-call(bf16[4,1024,2048]{2,1,0:T(8,128)(2,1)} %get-tuple-elemen, ...), custom_call_target="tpu_custom_call" | custom-call | tf_op jit(solution)/shard_map/back/pallas_call | solution.py:1715
  514.1 13.1 %finish.1 = (f32[2048,512]{1,0:T(8,128)}, f32[2048,512]{1,0:T(8,128)}, f32[2048,512]{1,0:T(8,128)}, f32[2048,512]{1,0:T(8,128)}, f32[256,2048]{1,0:T(8,128)}, /*...) custom-call(bf16[512,512]{1,0:T(8,128)(2,1)} %get-tuple-element.50.o, ...), custom_call_target="tpu_custom_call" | custom-call | tf_op jit(solution)/shard_map/finish/pallas_call | solution.py:1806

commit v6 on v5

--- a/solution.py
+++ b/solution.py
@@ -1773,7 +1773,7 @@
 def finish(output, input_grad, gains, mlp_grads, *attn_grads):
     count, _, chunk, local = attn_grads[0].shape
     half, hidden = mlp_grads.shape[2:]
-    steps = max(1, min(2 * count, half // 16))
+    steps = max(1, min(count, half // 16))
     part, layers = half // steps, max(count // steps, 1)
     pieces = max(steps // count, 1)
     tall = chunk // pieces

time: 537 us -> 535 us (level)
  no operation moved by 1% of the time
where the time goes in v6:
time: 535 us; the launch traced here: 527 us
  Pallas kernels  525 us (98%)
    pallas_call x1, Pallas kernels, back(): pl.pallas_call(functools.partial(back_kernel, count), name='back', out_sh...  332 us
    pallas_call x1, Pallas kernels, front(): pl.pallas_call(functools.partial(front_kernel, count), name='front', out_...  182 us
    pallas_call x1, Pallas kernels, finish(): pl.pallas_call(step, name='finish', grid=(steps,), in_specs=[share, share...  12 us

profile of v6, /device:TPU:0, one launch (start us, length us, event | category | flops | bytes accessed | tf_op | source)
XLA Modules:
  0.0 526.6 jit_solution(1069189842095627954)
XLA Ops:
  0.6 181.8 %front.1 = (bf16[4,1024,2048]{2,1,0:T(8,128)(2,1)}, bf16[4,1024,2048]{2,1,0:T(8,128)(2,1)}, bf16[4,1024,512]{2,1,0:T(8,128)(2,1)}, bf16[1024,256]{1,0:T(8,128)(2...) custom-call(bf16[512,512]{1,0:T(8,128)(2,1)} %xs.1, ...), custom_call_target="tpu_custom_call" | custom-call | tf_op jit(solution)/shard_map/front/pallas_call | solution.py:724
  182.5 331.6 %back.1 = (bf16[512,512]{1,0:T(8,128)(2,1)}, f32[512,512]{1,0:T(8,128)}, f32[8,2048]{1,0:T(8,128)}, bf16[2,2,256,1024]{3,2,1,0:T(8,128)(2,1)}, bf16[4,2,512,256]...) custom-call(bf16[4,1024,2048]{2,1,0:T(8,128)(2,1)} %get-tuple-elemen, ...), custom_call_target="tpu_custom_call" | custom-call | tf_op jit(solution)/shard_map/back/pallas_call | solution.py:1715
  514.1 12.0 %finish.1 = (f32[2048,512]{1,0:T(8,128)}, f32[2048,512]{1,0:T(8,128)}, f32[2048,512]{1,0:T(8,128)}, f32[2048,512]{1,0:T(8,128)}, f32[256,2048]{1,0:T(8,128)}, /*...) custom-call(bf16[512,512]{1,0:T(8,128)(2,1)} %get-tuple-element.50.o, ...), custom_call_target="tpu_custom_call" | custom-call | tf_op jit(solution)/shard_map/finish/pallas_call | solution.py:1806
